TPU v7x, 32 devices: a whole 2x2x4 slice. The times are simulated.
32 devices in a mesh: fsdp: 16 (over z, y, core), tp: 2 (over x).
Axes of the slice: x: 2, y: 2, z: 4, core: 2. Of those that a mesh axis runs over, the one named last changes fastest.
Arguments:
- tokens: bfloat16 [16384, 1024], P(('fsdp', 'tp')), may hold values from -6 to 6
- seq_lens: int32 [16, 4], P('fsdp'), may hold values from 1 to 512, 1024 in all within a row
- routes: int32 [16384, 8], P('fsdp'), may hold values from 0 to 15, all different within a row; in each aligned block of 1024 rows (0 to 1023, 1024 to 2047, ...) at most 768 rows name the same one
- route_gates: float32 [16384, 8], P('fsdp'), may hold values from 0.06 to 0.19
- query_weight: bfloat16 [1024, 1024], P('fsdp', 'tp'), may hold values from -0.25 to 0.25
- key_matrix: bfloat16 [1024, 512], P('fsdp', 'tp'), may hold values from -0.25 to 0.25
- value_matrix: bfloat16 [1024, 512], P('fsdp', 'tp'), may hold values from -0.1875 to 0.1875
- out_weight: bfloat16 [1024, 1024], P('fsdp', 'tp'), may hold values from -6 to 6
- norm_gains: bfloat16 [2, 1024], P(None, 'fsdp'), may hold values from 0.5 to 1.5
- gate_weight: bfloat16 [16, 1024, 512], P(None, 'fsdp', 'tp'), may hold values from -0.1875 to 0.1875
- up_weight: bfloat16 [16, 1024, 512], P(None, 'fsdp', 'tp'), may hold values from -0.1875 to 0.1875
- down_weight: bfloat16 [16, 1024, 512], P(None, 'fsdp', 'tp'), may hold values from -6 to 6
- cotangent: bfloat16 [16384, 1024], P(('fsdp', 'tp')), may hold values from -6 to 6
Outputs:
- layer_out: bfloat16 [16384, 1024], P(('fsdp', 'tp'))
- grad_tokens: bfloat16 [16384, 1024], P(('fsdp', 'tp'))
- grad_query: float32 [1024, 1024], P('fsdp', 'tp')
- grad_key: float32 [1024, 512], P('fsdp', 'tp')
- grad_value: float32 [1024, 512], P('fsdp', 'tp')
- grad_out_weight: float32 [1024, 1024], P('fsdp', 'tp')
- grad_gains: float32 [2, 1024], P(None, 'fsdp')
- grad_gate: float32 [16, 1024, 512], P(None, 'fsdp', 'tp')
- grad_up: float32 [16, 1024, 512], P(None, 'fsdp', 'tp')
- grad_down: float32 [16, 1024, 512], P(None, 'fsdp', 'tp')
Inputs may be any that keep to these rules, and one draw needn't show every extreme that they name: Within the 1024 routes rows of one group (aligned blocks) no expert is named by more than 768 rows, a bound that some block reaches. `seq_lens`: each row sums to 1024; its largest length is 512.
All inputs are finite; a program needn't handle non-finite values.
Results may differ from a plain program's by a relative error of at most 0.018.
Values may be sent and summed in bfloat16 or wider, within the bound.
No kernel may reach another device: no remote copies, remote signals or barrier semaphores. Data moves between devices by JAX's collectives and lax.ppermute only.
A program may use at most 384 MiB of HBM per device.

v0:
```python
import jax
import jax.numpy as jnp
from jax import lax
from jax.sharding import PartitionSpec as P

HEAD_DIM = 64
EXPERTS = 16
CAP = 768


EPSILON = 1e-06
BRANCH_SCALE = 0.22
ROPE_BASE = 10000.0


def seq_layout(lengths, row_total):
    places = jnp.arange(row_total, dtype=jnp.int32)
    ends = jnp.cumsum(lengths)
    starts = ends - lengths
    segment = jnp.sum((places[:, None] >= ends[None, :]).astype(jnp.int32), axis=1)
    chosen = segment[:, None] == jnp.arange(lengths.shape[0], dtype=jnp.int32)[None, :]
    opening = jnp.sum(jnp.where(chosen, starts[None, :], 0), axis=1)
    return (segment, places - opening)


def rotary_tables(position, head_size):
    halfway = head_size // 2
    ladder = jnp.arange(halfway, dtype=jnp.float32)
    inverse = jnp.exp(ladder * (-2.0 * jnp.log(ROPE_BASE) / head_size))
    angles = position.astype(jnp.float32)[:, None] * inverse[None, :]
    return (jnp.cos(angles), jnp.sin(angles))


def rotate(head_rows, cos_table, sine_table):
    halfway = head_rows.shape[-1] // 2
    first_half = head_rows[..., :halfway]
    second_half = head_rows[..., halfway:]
    cos_rows = cos_table[:, None, :]
    sine_rows = sine_table[:, None, :]
    return jnp.concatenate(
        [
            first_half * cos_rows - second_half * sine_rows,
            second_half * cos_rows + first_half * sine_rows,
        ],
        axis=-1,
    )


def rotate_back(grad_rows, cos_table, sine_table):
    halfway = grad_rows.shape[-1] // 2
    first_half = grad_rows[..., :halfway]
    second_half = grad_rows[..., halfway:]
    cos_rows = cos_table[:, None, :]
    sine_rows = sine_table[:, None, :]
    return jnp.concatenate(
        [
            first_half * cos_rows + second_half * sine_rows,
            second_half * cos_rows - first_half * sine_rows,
        ],
        axis=-1,
    )


def route_slots(routes, experts, capacity):
    row_total, chosen = routes.shape
    flat_ids = routes.reshape(-1)
    onehot = (flat_ids[:, None] == jnp.arange(experts, dtype=jnp.int32)[None, :]).astype(jnp.int32)
    earlier = jnp.cumsum(onehot, axis=0) - onehot
    slot_place = jnp.sum(earlier * onehot, axis=1)
    slot_index = flat_ids * capacity + slot_place
    source = jnp.full((experts * capacity,), row_total * chosen, jnp.int32)
    source = source.at[slot_index].set(jnp.arange(row_total * chosen, dtype=jnp.int32))
    return (slot_index.reshape(row_total, chosen), source)


def block_scores(query_blk, key_rows, seg_blk, place_blk, segment, places, score_scale):
    scores = (
        jnp.einsum("qjgd,kjd->jgqk", query_blk, key_rows, preferred_element_type=jnp.float32)
        * score_scale
    )
    allowed = (seg_blk[:, None] == segment[None, :]) & (place_blk[:, None] >= places[None, :])
    return jnp.where(allowed[None, None], scores, -1e30)


def attend_forward(query_rows, key_rows, value_rows, segment, score_scale):
    row_total = query_rows.shape[0]
    block_rows = min(512, row_total)
    blocks = row_total // block_rows
    places = jnp.arange(row_total, dtype=jnp.int32)

    def one_block(block_item):
        query_blk, seg_blk, place_blk = block_item
        scores = block_scores(query_blk, key_rows, seg_blk, place_blk, segment, places, score_scale)
        row_peak = jnp.max(scores, axis=-1, keepdims=True)
        weights = jnp.exp(scores - row_peak)
        totals = jnp.sum(weights, axis=-1, keepdims=True)
        prob_rows = (weights / totals).astype(jnp.bfloat16)
        output_result = jnp.einsum(
            "jgqk,kjd->qjgd", prob_rows, value_rows, preferred_element_type=jnp.float32
        )
        return (output_result, (row_peak + jnp.log(totals))[..., 0])

    outputs, logsum = lax.map(
        one_block,
        (
            query_rows.reshape((blocks, block_rows) + query_rows.shape[1:]),
            segment.reshape(blocks, block_rows),
            places.reshape(blocks, block_rows),
        ),
    )
    return (outputs.reshape(query_rows.shape), logsum)


def attend_backward(query_rows, key_rows, value_rows, grad_out, logsum, segment, score_scale):
    row_total = query_rows.shape[0]
    block_rows = min(512, row_total)
    blocks = row_total // block_rows
    places = jnp.arange(row_total, dtype=jnp.int32)

    def one_block(running, block_item):
        key_acc, value_acc = running
        query_blk, grad_blk, lse_blk, seg_blk, place_blk = block_item
        scores = block_scores(query_blk, key_rows, seg_blk, place_blk, segment, places, score_scale)
        prob_rows = jnp.exp(scores - lse_blk[..., None])
        grad_probs = jnp.einsum(
            "qjgd,kjd->jgqk", grad_blk, value_rows, preferred_element_type=jnp.float32
        )
        inner = jnp.sum(prob_rows * grad_probs, axis=-1, keepdims=True)
        grad_scores = (prob_rows * (grad_probs - inner)).astype(jnp.bfloat16)
        grad_query = (
            jnp.einsum("jgqk,kjd->qjgd", grad_scores, key_rows, preferred_element_type=jnp.float32)
            * score_scale
        )
        key_acc = (
            key_acc
            + jnp.einsum(
                "jgqk,qjgd->kjd", grad_scores, query_blk, preferred_element_type=jnp.float32
            )
            * score_scale
        )
        value_acc = value_acc + jnp.einsum(
            "jgqk,qjgd->kjd",
            prob_rows.astype(jnp.bfloat16),
            grad_blk,
            preferred_element_type=jnp.float32,
        )
        return ((key_acc, value_acc), grad_query)

    empty = jnp.zeros(key_rows.shape, jnp.float32)
    (grad_keys, grad_values), grad_queries = lax.scan(
        one_block,
        (empty, empty),
        (
            query_rows.reshape((blocks, block_rows) + query_rows.shape[1:]),
            grad_out.reshape((blocks, block_rows) + grad_out.shape[1:]),
            logsum,
            segment.reshape(blocks, block_rows),
            places.reshape(blocks, block_rows),
        ),
    )
    return (grad_queries.reshape(query_rows.shape), grad_keys, grad_values)


def norm_backward(values, row_scale, gain_row, grad_rows):
    unit_rows = values * row_scale
    scaled = grad_rows * gain_row
    gain_grad = jnp.sum(grad_rows * unit_rows, axis=0)
    grad_values = row_scale * (
        scaled - unit_rows * jnp.mean(scaled * unit_rows, axis=1, keepdims=True)
    )
    return (grad_values, gain_grad)


def contract_last(left, right):
    return lax.dot_general(
        left, right, (((1,), (1,)), ((), ())), preferred_element_type=jnp.float32
    )


def contract_rows(left, right):
    return lax.dot_general(
        left, right, (((0,), (0,)), ((), ())), preferred_element_type=jnp.float32
    )


def per_device(
    tokens,
    seq_lens,
    routes,
    route_gates,
    query_weight,
    key_matrix,
    value_matrix,
    out_weight,
    norm_gains,
    gate_weight,
    up_weight,
    down_weight,
    cotangent,
):
    local_rows = tokens.shape[0]
    model_width = tokens.shape[1]
    query_w, key_w, value_w, out_w, gains_all = (
        lax.all_gather(query_weight, "fsdp", axis=0, tiled=True),
        lax.all_gather(key_matrix, "fsdp", axis=0, tiled=True),
        lax.all_gather(value_matrix, "fsdp", axis=0, tiled=True),
        lax.all_gather(out_weight, "fsdp", axis=0, tiled=True),
        lax.all_gather(norm_gains, "fsdp", axis=1, tiled=True),
    )
    gate_w, up_w, down_w = (
        lax.all_gather(gate_weight, "fsdp", axis=1, tiled=True),
        lax.all_gather(up_weight, "fsdp", axis=1, tiled=True),
        lax.all_gather(down_weight, "fsdp", axis=1, tiled=True),
    )
    gain_rows = gains_all.astype(jnp.float32)
    inputs = tokens.astype(jnp.float32)
    scale_one = lax.rsqrt(jnp.mean(inputs * inputs, axis=1, keepdims=True) + EPSILON)
    normed_one = (inputs * scale_one * gain_rows[0]).astype(jnp.bfloat16)
    normed_full = lax.all_gather(normed_one, "tp", axis=0, tiled=True)
    row_total = normed_full.shape[0]
    segment, position = seq_layout(seq_lens[0], row_total)
    cos_table, sine_table = rotary_tables(position, HEAD_DIM)
    kv_heads = key_w.shape[1] // HEAD_DIM
    group_size = query_w.shape[1] // key_w.shape[1]
    score_scale = HEAD_DIM ** (-0.5)
    query_raw = jnp.dot(normed_full, query_w, preferred_element_type=jnp.float32).reshape(
        row_total, kv_heads * group_size, HEAD_DIM
    )
    query_rows = (
        rotate(query_raw, cos_table, sine_table)
        .astype(jnp.bfloat16)
        .reshape(row_total, kv_heads, group_size, HEAD_DIM)
    )
    key_raw = jnp.dot(normed_full, key_w, preferred_element_type=jnp.float32).reshape(
        row_total, kv_heads, HEAD_DIM
    )
    key_rows = rotate(key_raw, cos_table, sine_table).astype(jnp.bfloat16)
    value_rows = (
        jnp.dot(normed_full, value_w, preferred_element_type=jnp.float32)
        .astype(jnp.bfloat16)
        .reshape(row_total, kv_heads, HEAD_DIM)
    )
    attended, logsum = attend_forward(query_rows, key_rows, value_rows, segment, score_scale)
    attended_b = attended.reshape(row_total, query_w.shape[1]).astype(jnp.bfloat16)
    piece = attended_b
    attn_out = lax.psum_scatter(contract_last(piece, out_w), "tp", scatter_dimension=0, tiled=True)
    middle = inputs + BRANCH_SCALE * attn_out
    scale_two = lax.rsqrt(jnp.mean(middle * middle, axis=1, keepdims=True) + EPSILON)
    normed_two = (middle * scale_two * gain_rows[1]).astype(jnp.bfloat16)
    ffn_full, grad_full = (
        lax.all_gather(normed_two, "tp", axis=0, tiled=True),
        lax.all_gather(cotangent, "tp", axis=0, tiled=True),
    )
    chosen = routes.shape[1]
    slot_index, source = route_slots(routes, EXPERTS, CAP)
    slot_token = source // chosen
    padded = jnp.concatenate([ffn_full, jnp.zeros((1, model_width), jnp.bfloat16)], axis=0)
    expert_rows = padded[slot_token].reshape(EXPERTS, CAP, model_width)
    gate_pre = jnp.einsum("ecd,edf->ecf", expert_rows, gate_w, preferred_element_type=jnp.float32)
    up_pre = jnp.einsum("ecd,edf->ecf", expert_rows, up_w, preferred_element_type=jnp.float32)
    sigmoid_gate = jax.nn.sigmoid(gate_pre)
    silu_gate = gate_pre * sigmoid_gate
    hidden = (silu_gate * up_pre).astype(jnp.bfloat16)
    expert_out = jnp.einsum(
        "ecf,edf->ecd", hidden, down_w, preferred_element_type=jnp.float32
    ).reshape(EXPERTS * CAP, model_width)
    picked = slot_index
    moe_out = lax.psum_scatter(
        jnp.sum(route_gates[:, :, None] * expert_out[picked], axis=1).astype(jnp.bfloat16),
        "tp",
        scatter_dimension=0,
        tiled=True,
    ).astype(jnp.float32)
    layer_out = (middle + BRANCH_SCALE * moe_out).astype(jnp.bfloat16)
    query_w, key_w, value_w, out_w, gains_all, gate_w, up_w, down_w = (
        lax.all_gather(query_weight, "fsdp", axis=0, tiled=True),
        lax.all_gather(key_matrix, "fsdp", axis=0, tiled=True),
        lax.all_gather(value_matrix, "fsdp", axis=0, tiled=True),
        lax.all_gather(out_weight, "fsdp", axis=0, tiled=True),
        lax.all_gather(norm_gains, "fsdp", axis=1, tiled=True),
        lax.all_gather(gate_weight, "fsdp", axis=1, tiled=True),
        lax.all_gather(up_weight, "fsdp", axis=1, tiled=True),
        lax.all_gather(down_weight, "fsdp", axis=1, tiled=True),
    )
    gain_rows = gains_all.astype(jnp.float32)
    grad_local = cotangent.astype(jnp.float32)
    grad_moe = BRANCH_SCALE * grad_full.astype(jnp.float32)
    grad_padded = jnp.concatenate([grad_moe, jnp.zeros((1, model_width), jnp.float32)], axis=0)
    gate_padded = jnp.concatenate([route_gates.reshape(-1), jnp.zeros((1,), jnp.float32)], axis=0)
    grad_expert = (
        (gate_padded[source][:, None] * grad_padded[slot_token])
        .astype(jnp.bfloat16)
        .reshape(EXPERTS, CAP, model_width)
    )
    grad_down_w = jnp.einsum(
        "ecd,ecf->edf", grad_expert, hidden, preferred_element_type=jnp.float32
    )
    grad_hidden = jnp.einsum(
        "ecd,edf->ecf", grad_expert, down_w, preferred_element_type=jnp.float32
    )
    grad_gate_pre = (
        grad_hidden * up_pre * sigmoid_gate * (1.0 + gate_pre * (1.0 - sigmoid_gate))
    ).astype(jnp.bfloat16)
    grad_up_pre = (grad_hidden * silu_gate).astype(jnp.bfloat16)
    grad_gate_w = jnp.einsum(
        "ecd,ecf->edf", expert_rows, grad_gate_pre, preferred_element_type=jnp.float32
    )
    grad_up_w = jnp.einsum(
        "ecd,ecf->edf", expert_rows, grad_up_pre, preferred_element_type=jnp.float32
    )
    expert_grads = (
        lax.psum_scatter(grad_gate_w, "fsdp", scatter_dimension=1, tiled=True),
        lax.psum_scatter(grad_up_w, "fsdp", scatter_dimension=1, tiled=True),
        lax.psum_scatter(grad_down_w, "fsdp", scatter_dimension=1, tiled=True),
    )
    row_grads = (
        jnp.einsum("ecf,edf->ecd", grad_gate_pre, gate_w, preferred_element_type=jnp.float32)
        + jnp.einsum("ecf,edf->ecd", grad_up_pre, up_w, preferred_element_type=jnp.float32)
    ).reshape(EXPERTS * CAP, model_width)
    picked = slot_index
    grad_normed_two = lax.psum_scatter(
        jnp.sum(row_grads[picked], axis=1), "tp", scatter_dimension=0, tiled=True
    )
    grad_middle_norm, gain_grad_two = norm_backward(
        middle, scale_two, gain_rows[1], grad_normed_two
    )
    grad_middle = grad_local + grad_middle_norm
    grad_attn = (BRANCH_SCALE * grad_middle).astype(jnp.bfloat16)
    grad_attn_full = lax.all_gather(grad_attn, "tp", axis=0, tiled=True)
    grad_out_w = contract_rows(grad_attn_full, attended_b)
    grad_attended = (
        jnp.dot(grad_attn_full, out_w, preferred_element_type=jnp.float32)
        .astype(jnp.bfloat16)
        .reshape(row_total, kv_heads, group_size, HEAD_DIM)
    )
    grad_query_rot, grad_key_rot, value_gradient_total = attend_backward(
        query_rows, key_rows, value_rows, grad_attended, logsum, segment, score_scale
    )
    grad_query_b = (
        rotate_back(
            grad_query_rot.reshape(row_total, kv_heads * group_size, HEAD_DIM),
            cos_table,
            sine_table,
        )
        .astype(jnp.bfloat16)
        .reshape(row_total, query_w.shape[1])
    )
    grad_key_b = (
        rotate_back(grad_key_rot, cos_table, sine_table)
        .astype(jnp.bfloat16)
        .reshape(row_total, key_w.shape[1])
    )
    grad_value_b = value_gradient_total.astype(jnp.bfloat16).reshape(row_total, value_w.shape[1])
    grad_query_w = contract_rows(normed_full, grad_query_b)
    grad_key_w = contract_rows(normed_full, grad_key_b)
    grad_value_w = contract_rows(normed_full, grad_value_b)
    summed = jnp.zeros((local_rows * lax.axis_size("tp"), model_width), jnp.float32)
    for grad_rows, weight_rows in (
        (grad_query_b, query_w),
        (grad_key_b, key_w),
        (grad_value_b, value_w),
    ):
        piece = grad_rows
        summed = summed + contract_last(piece, weight_rows)
    grad_normed_one = lax.psum_scatter(
        summed.astype(jnp.bfloat16), "tp", scatter_dimension=0, tiled=True
    ).astype(jnp.float32)
    grad_input_norm, gain_grad_one = norm_backward(inputs, scale_one, gain_rows[0], grad_normed_one)
    grad_tokens = (grad_middle + grad_input_norm).astype(jnp.bfloat16)
    gain_grads = lax.psum(jnp.stack([gain_grad_one, gain_grad_two], axis=0), "tp")
    attn_grads = (
        lax.psum_scatter(grad_query_w, "fsdp", scatter_dimension=0, tiled=True),
        lax.psum_scatter(grad_key_w, "fsdp", scatter_dimension=0, tiled=True),
        lax.psum_scatter(grad_value_w, "fsdp", scatter_dimension=0, tiled=True),
        lax.psum_scatter(grad_out_w, "fsdp", scatter_dimension=0, tiled=True),
        lax.psum_scatter(gain_grads, "fsdp", scatter_dimension=1, tiled=True),
    )
    return (
        layer_out,
        grad_tokens,
        attn_grads[0],
        attn_grads[1],
        attn_grads[2],
        attn_grads[3],
        attn_grads[4],
        expert_grads[0],
        expert_grads[1],
        expert_grads[2],
    )


def solution(mesh):
    in_specs = (
        P(("fsdp", "tp"), None),
        P("fsdp", None),
        P("fsdp", None),
        P("fsdp", None),
        P("fsdp", "tp"),
        P("fsdp", "tp"),
        P("fsdp", "tp"),
        P("fsdp", "tp"),
        P(None, "fsdp"),
        P(None, "fsdp", "tp"),
        P(None, "fsdp", "tp"),
        P(None, "fsdp", "tp"),
        P(("fsdp", "tp"), None),
    )
    out_specs = (
        P(("fsdp", "tp"), None),
        P(("fsdp", "tp"), None),
        P("fsdp", "tp"),
        P("fsdp", "tp"),
        P("fsdp", "tp"),
        P("fsdp", "tp"),
        P(None, "fsdp"),
        P(None, "fsdp", "tp"),
        P(None, "fsdp", "tp"),
        P(None, "fsdp", "tp"),
    )
    return jax.shard_map(
        per_device, mesh=mesh, in_specs=in_specs, out_specs=out_specs, check_vma=False
    )
```

profile of v0, /device:TPU:0, one launch (start us, length us, event | category | flops | bytes accessed | tf_op | source)
XLA Modules:
  0.0 1947.4 jit_solution(4508841819208230397)
XLA Ops:
  8.7 23.2 %all-gather = bf16[16,64,2]{1,2,0:T(2,128)(2,1)S(1)} all-gather(bf16[1,64,2]{1,2,0:T(2,128)(2,1)} %bitcast.312), channel_id=1, replica_groups=mesh['fsdp'=16,'tp'=2] {'fsdp'}, dimensions={0}, use_global_device_ids=true | all-gather | bytes 4352 | tf_op jit(solution)/shard_map/all_gather | solution.py:208
  39.0 19.1 all_gather.47
  58.1 20.6 %all_gather.48 = bf16[1024,256]{1,0:T(8,128)(2,1)S(1)} all-gather(bf16[64,256]{1,0:T(8,128)(2,1)} %param.23), channel_id=1, replica_groups=mesh['fsdp'=16,'tp'=2] {'fsdp'}, dimensions={0}, use_global_device_ids=true | all-gather | bytes 557056 | tf_op jit(solution)/shard_map/all_gather | solution.py:206
  82.5 23.9 %all-gather.13.cloned.1.call-done = bf16[1024,512]{1,0:T(8,128)(2,1)} async-done(((bf16[64,512]{1,0:T(8,128)(2,1)}), bf16[1024,512]{1,0:T(8,128)(2,1)}) %all-gather.13.cloned.1.call-update) | async-done | bytes 1048592 | tf_op jit(solution)/shard_map/all_gather | solution.py:204
  116.4 27.4 %while.28 = (s32[]{:T(128)}, bf16[2,512,4,2,64]{1,4,3,2,0:T(8,128)(2,1)S(1)}, f32[2,4,2,512]{3,2,1,0:T(2,128)S(1)}, s32[2,512]{1,0:T(2,128)S(1)}, s32[1024]{0:T(...) while((s32[]{:T(128)}, ...), condition=%wide.region_7.8_spmd.clone, body=%wide.region_4.7_spmd.clone.sunk | while | flops 1125642240 | bytes 55197820 | solution.py:103
  151.9 52.7 %reduce-scatter.15.cloned.1.call-done = f32[512,1024]{1,0:T(8,128)} async-done(((f32[1024,1024]{1,0:T(8,128)}), f32[512,1024]{1,0:T(8,128)}) %reduce-scatter.15.cloned.1.call-update) | async-done | bytes 2097168 | tf_op jit(solution)/shard_map/reduce_scatter | solution.py:246
  220.3 30.5 %scatter_custom_fusion = s32[12288]{0:T(1024)S(1)} fusion(s32[8192]{0:T(1024)S(1)} %bitcast.307, s32[8192]{0:T(1024)S(1)} %iota.49, s32[]{:T(128)} %constant.96.clone.1), kind=kCustom, calls=%fused_computation.145 | custom fusion | bytes 49156 | tf_op jit(solution)/shard_map/scatter | solution.py:72
  250.9 68.0 %gather_fusion.2 = f32[12288]{0:T(1024)S(1)} fusion(f32[8193]{0:T(1024)S(1)} %pad_maximum_fusion.4, s32[12288]{0:T(1024)S(1)} %get-tuple-element.365), kind=kCustom, calls=%fused_computation.2 | custom fusion | bytes 147456 | tf_op jit(solution)/shard_map/gather | solution.py:291
  324.6 67.2 %gather_fusion.3 = f32[12288,1024]{1,0:T(8,128)} fusion(f32[1025,1024]{1,0:T(8,128)} %concatenate.36, s32[12288]{0:T(1024)S(1)} %get-tuple-element.366), kind=kCustom, calls=%fused_computation.3 | custom fusion | bytes 100712448 | tf_op jit(solution)/shard_map/gather | solution.py:291
  391.9 49.1 %copy.85 = f32[16,768,1024]{1,2,0:T(8,128)} copy(f32[16,768,1024]{2,1,0:T(8,128)} %bitcast.280) | data formatting | bytes 100663296 | tf_op jit(solution)/shard_map/gather | solution.py:291
  442.7 52.7 %gather_fusion = bf16[12288,1024]{1,0:T(8,128)(2,1)} fusion(bf16[1025,1024]{1,0:T(8,128)(2,1)S(1)} %concatenate.34, s32[12288]{0:T(1024)S(1)} %get-tuple-element.366), kind=kCustom, calls=%fused_computation | custom fusion | bytes 50380800 | tf_op jit(solution)/shard_map/gather | solution.py:258
  529.0 34.2 %multiply_convert_fusion.1 = (bf16[16,768,256]{2,1,0:T(8,128)(2,1)}, bf16[16,768,256]{2,1,0:T(8,128)(2,1)}, bf16[16,768,256]{2,1,0:T(8,128)(2,1)}) fusion(f32[16,768,256]{2,1,0:T(8,128)} %fusion.82, f32[16,768,256]{2,1,0:T(8,128)} %fusion.83, bf16[16,1024,256]{2,1,0:T(8,128)(2,1)} %all-gather.23.cloned.1.call-done, f32[16,768,1024]{1,2,0:T(8,128)} %copy.85, ...), kind=kOutput, calls=%fused_computation.73 | convolution fusion | flops 6514802688 | bytes 102809600 | tf_op jit(solution)/shard_map/ecd,edf->ecf/dot_general | solution.py:298
  563.2 23.6 %fusion.85 = f32[16,768,1024]{2,1,0:T(8,128)} fusion(bf16[16,768,256]{2,1,0:T(8,128)(2,1)} %get-tuple-element.351, bf16[16,1024,256]{2,1,0:T(8,128)(2,1)} %all-gather.19.cloned.1.call-done), kind=kOutput, calls=%fused_computation.170 | convolution fusion | flops 6442450944 | bytes 65011712 | tf_op jit(solution)/shard_map/ecf,edf->ecd/dot_general | solution.py:317
  586.8 39.5 %convolution_add_fusion = f32[16,768,1024]{2,1,0:T(8,128)} fusion(f32[16,768,1024]{2,1,0:T(8,128)} %fusion.85, bf16[16,768,256]{2,1,0:T(8,128)(2,1)} %get-tuple-element.350, bf16[16,1024,256]{2,1,0:T(8,128)(2,1)} %all-gather.21.cloned.1.call-done), kind=kOutput, calls=%fused_computation.72 | convolution fusion | flops 6455033856 | bytes 115343360 | tf_op jit(solution)/shard_map/ecf,edf->ecd/dot_general | solution.py:318
  626.3 59.1 %gather_fusion.4 = f32[8192,1024]{1,0:T(8,128)} fusion(f32[12288,1024]{1,0:T(8,128)} %bitcast.274, s32[8192]{0:T(1024)S(1)} %copy-done.10), kind=kCustom, calls=%fused_computation.4 | custom fusion | bytes 67141632 | tf_op jit(solution)/shard_map/gather | solution.py:322
  702.6 54.4 %reduce-scatter.19.cloned.1.call-done = f32[512,1024]{1,0:T(8,128)} async-done(((f32[1024,1024]{1,0:T(8,128)}), f32[512,1024]{1,0:T(8,128)}) %reduce-scatter.19.cloned.1.call-update) | async-done | bytes 2097168 | tf_op jit(solution)/shard_map/reduce_scatter | solution.py:321
  763.7 33.2 %all-gather.27.cloned.1.call-done = bf16[1024,1024]{1,0:T(8,128)(2,1)} async-done(((bf16[512,1024]{1,0:T(8,128)(2,1)}), bf16[1024,1024]{1,0:T(8,128)(2,1)}) %all-gather.27.cloned.1.call-update) | async-done | bytes 2097168 | tf_op jit(solution)/shard_map/all_gather | solution.py:329
  809.7 127.1 %while.29 = (s32[]{:T(128)}, f32[1024,4,64]{0,2,1:T(8,128)}, f32[1024,4,64]{0,2,1:T(8,128)}, f32[2,512,4,2,64]{1,0,4,3,2:T(2,128)}, bf16[2,512,4,2,64]{1,4,3,2,0...) while((s32[]{:T(128)}, f32[1024,4,64]{0,2,1:T(8,128)}, ...), condition=%wide.region_21.22_spmd.clone, body=%wide.region_19.21_spmd.clone.sunk | while | flops 2725244928 | bytes 177832160 | solution.py:150
  852.6 19.6 %dynamic_update_slice.21 = f32[2,512,4,2,64]{1,0,4,3,2:T(2,128)} dynamic-update-slice(f32[2,512,4,2,64]{1,0,4,3,2:T(2,128)} %get-tuple-element.562, f32[1,512,4,2,64]{1,0,4,3,2:T(1,128)S(1)} %copy.122, s32[]{:T(128)S(6)} %copy.139, s32[]{:T(128)} %constant.56.clone.1..sunk, s32[]{:T(128)} %constant.56.clone.1..sunk, s32[]{:T(128)} %constant.56.clone.1..sunk, s32[]{:T(128)} %constant.56.clone.1..sunk) | dynamic-update-slice | bytes 2097156 | tf_op jit(solution)/shard_map/while/body/jit(dynamic_update_index_in_dim)/dynamic_update_slice | solution.py:103
  917.2 19.6 %dynamic_update_slice.21 = f32[2,512,4,2,64]{1,0,4,3,2:T(2,128)} dynamic-update-slice(f32[2,512,4,2,64]{1,0,4,3,2:T(2,128)} %get-tuple-element.562, f32[1,512,4,2,64]{1,0,4,3,2:T(1,128)S(1)} %copy.122, s32[]{:T(128)S(6)} %copy.139, s32[]{:T(128)} %constant.56.clone.1..sunk, s32[]{:T(128)} %constant.56.clone.1..sunk, s32[]{:T(128)} %constant.56.clone.1..sunk, s32[]{:T(128)} %constant.56.clone.1..sunk) | dynamic-update-slice | bytes 2097156 | tf_op jit(solution)/shard_map/while/body/jit(dynamic_update_index_in_dim)/dynamic_update_slice | solution.py:103
  949.2 23.6 %fusion.84 = f32[16,768,1024]{2,1,0:T(8,128)} fusion(bf16[16,768,256]{2,1,0:T(8,128)(2,1)} %get-tuple-element.352, bf16[16,1024,256]{2,1,0:T(8,128)(2,1)} %all-gather.23.cloned.1.call-done), kind=kOutput, calls=%fused_computation.169 | convolution fusion | flops 6442450944 | bytes 65011712 | tf_op jit(solution)/shard_map/ecf,edf->ecd/dot_general | solution.py:264
  972.9 59.2 %gather_fusion.1 = f32[8192,1024]{1,0:T(8,128)} fusion(f32[12288,1024]{1,0:T(8,128)} %bitcast.275, s32[8192]{0:T(1024)S(1)} %copy-done.11), kind=kCustom, calls=%fused_computation.1 | custom fusion | bytes 67141632 | tf_op jit(solution)/shard_map/gather | solution.py:269
  1067.1 26.4 %fusion.53 = f32[16,1024,256]{2,1,0:T(8,128)} fusion(bf16[16,768,256]{2,1,0:T(8,128)(2,1)} %get-tuple-element.352, f32[16,768,1024]{1,2,0:T(8,128)} %copy.85, f32[16,768]{1,0:T(8,128)S(1)} %copy-done.33), kind=kOutput, calls=%fused_computation.78 | convolution fusion | flops 6467616768 | bytes 73449472 | tf_op jit(solution)/shard_map/ecd,ecf->edf/dot_general | solution.py:295
  1093.7 20.5 %fusion.92 = f32[16,1024,256]{2,1,0:T(8,128)} fusion(bf16[16,768,1024]{2,1,0:T(8,128)(2,1)} %bitcast.278, bf16[16,768,256]{2,1,0:T(8,128)(2,1)} %get-tuple-element.351), kind=kOutput, calls=%fused_computation.177 | convolution fusion | flops 6442450944 | bytes 48234496 | tf_op jit(solution)/shard_map/ecd,ecf->edf/dot_general | solution.py:305
  1114.2 20.4 %fusion.93 = f32[16,1024,256]{2,1,0:T(8,128)} fusion(bf16[16,768,1024]{2,1,0:T(8,128)(2,1)} %bitcast.279, bf16[16,768,256]{2,1,0:T(8,128)(2,1)} %get-tuple-element.350), kind=kOutput, calls=%fused_computation.178 | convolution fusion | flops 6442450944 | bytes 48234496 | tf_op jit(solution)/shard_map/ecd,ecf->edf/dot_general | solution.py:308
  1146.9 54.6 %reduce-scatter.27.cloned.1.call-done = f32[64,256]{1,0:T(8,128)} async-done(((f32[1024,256]{1,0:T(8,128)}), f32[64,256]{1,0:T(8,128)}) %reduce-scatter.27.cloned.1.call-update) | async-done | bytes 65552 | tf_op jit(solution)/shard_map/reduce_scatter | solution.py:374
  1201.5 60.6 %reduce-scatter.25.cloned.1.call-done = f32[64,256]{1,0:T(8,128)} async-done(((f32[1024,256]{1,0:T(8,128)}), f32[64,256]{1,0:T(8,128)}) %reduce-scatter.25.cloned.1.call-update) | async-done | bytes 65552 | tf_op jit(solution)/shard_map/reduce_scatter | solution.py:373
  1262.1 65.2 %reduce-scatter.29.cloned.1.call-done = f32[64,512]{1,0:T(8,128)} async-done(((f32[1024,512]{1,0:T(8,128)}), f32[64,512]{1,0:T(8,128)}) %reduce-scatter.29.cloned.1.call-update) | async-done | bytes 131088 | tf_op jit(solution)/shard_map/reduce_scatter | solution.py:375
  1327.3 64.8 %reduce-scatter.23.cloned.1.call-done = f32[64,512]{1,0:T(8,128)} async-done(((f32[1024,512]{1,0:T(8,128)}), f32[64,512]{1,0:T(8,128)}) %reduce-scatter.23.cloned.1.call-update) | async-done | bytes 131088 | tf_op jit(solution)/shard_map/reduce_scatter | solution.py:372
  1392.1 182.8 %reduce-scatter.35.cloned.1.call-done = f32[16,64,256]{2,1,0:T(8,128)} async-done(((f32[16,1024,256]{2,1,0:T(8,128)}), f32[16,64,256]{2,1,0:T(8,128)}) %reduce-scatter.35.cloned.1.call-update) | async-done | bytes 1048592 | tf_op jit(solution)/shard_map/reduce_scatter | solution.py:314
  1574.9 182.6 %reduce-scatter.31.cloned.1.call-done = f32[16,64,256]{2,1,0:T(8,128)} async-done(((f32[16,1024,256]{2,1,0:T(8,128)}), f32[16,64,256]{2,1,0:T(8,128)}) %reduce-scatter.31.cloned.1.call-update) | async-done | bytes 1048592 | tf_op jit(solution)/shard_map/reduce_scatter | solution.py:312
  1757.5 182.8 %reduce-scatter.33.cloned.1.call-done = f32[16,64,256]{2,1,0:T(8,128)} async-done(((f32[16,1024,256]{2,1,0:T(8,128)}), f32[16,64,256]{2,1,0:T(8,128)}) %reduce-scatter.33.cloned.1.call-update) | async-done | bytes 1048592 | tf_op jit(solution)/shard_map/reduce_scatter | solution.py:313
  (284 shorter events, 297.8 us)
Async XLA Ops:
  7.2 72.1 %all-gather.11.cloned.1.call-start = ((), (), s32[]{:S(2)}) async-start(), calls=%async_computation.12 | async-start | bytes 3145728 | tf_op jit(solution)/shard_map/all_gather | solution.py:219
  35.7 70.7 %all-gather.13.cloned.1.call-start = ((), (), s32[]{:S(2)}) async-start(), calls=%async_computation.13 | async-start | bytes 1114112 | tf_op jit(solution)/shard_map/all_gather | solution.py:204
  36.5 109.7 %all-gather.15.cloned.1.call-start = ((), (), s32[]{:S(2)}) async-start(), calls=%async_computation.14 | async-start | bytes 1114112 | tf_op jit(solution)/shard_map/all_gather | solution.py:207
  37.2 167.3 %reduce-scatter.15.cloned.1.call-start = ((), (), s32[]{:S(2)}) async-start(), calls=%async_computation.15 | async-start | bytes 6291456 | tf_op jit(solution)/shard_map/reduce_scatter | solution.py:246
  58.1 51.5 %copy-start.18 = (bf16[1024,256]{1,0:T(8,128)(2,1)}, bf16[1024,256]{1,0:T(8,128)(2,1)S(1)}, u32[]{:S(2)}) copy-start(bf16[1024,256]{1,0:T(8,128)(2,1)S(1)} %all_gather.47) | copy-start | bytes 1572868
  146.2 58.4 %copy-start.13 = (bf16[512,1024]{1,0:T(8,128)(2,1)S(1)}, bf16[512,1024]{1,0:T(8,128)(2,1)}, u32[]{:S(2)}) copy-start(bf16[512,1024]{1,0:T(8,128)(2,1)} %param.17) | copy-start | bytes 3145732
  151.2 56.8 %copy-start.38 = (f32[1,1024]{1,0:T(1,128)S(1)}, f32[1,1024]{1,0:T(1,128)}, u32[]{:S(2)}) copy-start(f32[1,1024]{1,0:T(1,128)} %get-tuple-element.367) | copy-start | bytes 12292
  151.2 60.2 %copy-start.46 = (s32[1024,8]{0,1:T(8,128)S(1)}, s32[1024,8]{0,1:T(8,128)}, u32[]{:S(2)}) copy-start(s32[1024,8]{0,1:T(8,128)} %param.19) | copy-start | bytes 98308
  151.2 169.0 %all-gather.25.cloned.1.call-start = ((), (), s32[]{:S(2)}) async-start(), calls=%async_computation.21 | async-start | bytes 3145728 | tf_op jit(solution)/shard_map/all_gather | solution.py:252
  151.8 66.4 %copy-start.47 = (f32[1024,8]{0,1:T(8,128)S(1)}, f32[1024,8]{0,1:T(8,128)}, u32[]{:S(2)}) copy-start(f32[1024,8]{0,1:T(8,128)} %param.20) | copy-start | bytes 98308
  151.8 289.1 %all-gather.17.cloned.1.call-start = ((), (), s32[]{:S(2)}) async-start(), calls=%async_computation.16 | async-start | bytes 3145728 | tf_op jit(solution)/shard_map/all_gather | solution.py:251
  209.2 286.3 %all-gather.21.cloned.1.call-start = ((), (), s32[]{:S(2)}) async-start(), calls=%async_computation.18 | async-start | bytes 8912896 | tf_op jit(solution)/shard_map/all_gather | solution.py:212
  209.9 302.5 %all-gather.19.cloned.1.call-start = ((), (), s32[]{:S(2)}) async-start(), calls=%async_computation.17 | async-start | bytes 8912896 | tf_op jit(solution)/shard_map/all_gather | solution.py:211
  210.7 318.3 %all-gather.23.cloned.1.call-start = ((), (), s32[]{:S(2)}) async-start(), calls=%async_computation.19 | async-start | bytes 8912896 | tf_op jit(solution)/shard_map/all_gather | solution.py:213
  211.4 545.6 %reduce-scatter.19.cloned.1.call-start = ((), (), s32[]{:S(2)}) async-start(), calls=%async_computation.22 | async-start | bytes 6291456 | tf_op jit(solution)/shard_map/reduce_scatter | solution.py:321
  218.4 100.5 %copy-start.16 = (f32[1024,8]{1,0:T(8,128)}, f32[1024,8]{1,0:T(8,128)S(1)}, u32[]{:S(2)}) copy-start(f32[1024,8]{1,0:T(8,128)S(1)} %copy.80) | copy-start | bytes 98308
  685.4 71.6 %copy-start.4 = (f32[512,1024]{1,0:T(8,128)S(1)}, f32[512,1024]{1,0:T(8,128)}, u32[]{:S(2)}) copy-start(f32[512,1024]{1,0:T(8,128)} %copy-done.3) | copy-start | bytes 6291460
  685.4 71.6 %copy-start.39 = (f32[1,1024]{1,0:T(1,128)S(1)}, f32[1,1024]{1,0:T(1,128)}, u32[]{:S(2)}) copy-start(f32[1,1024]{1,0:T(1,128)} %get-tuple-element.367) | copy-start | bytes 12292
  685.4 71.6 %copy-start.44 = (f32[512]{0:T(512)S(1)}, f32[512]{0:T(512)}, u32[]{:S(2)}) copy-start(f32[512]{0:T(512)} %copy-done.43) | copy-start | bytes 6148
  702.5 57.8 %copy-start.15 = (bf16[512,1024]{1,0:T(8,128)(2,1)S(1)}, bf16[512,1024]{1,0:T(8,128)(2,1)}, u32[]{:S(2)}) copy-start(bf16[512,1024]{1,0:T(8,128)(2,1)} %param.29) | copy-start | bytes 3145732
  702.6 94.3 %all-gather.27.cloned.1.call-start = ((), (), s32[]{:S(2)}) async-start(), calls=%async_computation.23 | async-start | bytes 3145728 | tf_op jit(solution)/shard_map/all_gather | solution.py:329
  763.5 285.9 %reduce-scatter.21.cloned.1.call-start = ((), (), s32[]{:S(2)}) async-start(), calls=%async_computation.24 | async-start | bytes 3145728 | tf_op jit(solution)/shard_map/reduce_scatter | solution.py:365
  763.6 46.0 %copy-start.2 = (bf16[1024,4,64]{0,2,1:T(8,128)(2,1)S(1)}, bf16[1024,4,64]{0,2,1:T(8,128)(2,1)}, u32[]{:S(2)}) copy-start(bf16[1024,4,64]{0,2,1:T(8,128)(2,1)} %copy-done.1) | copy-start | bytes 1572868
  949.2 185.6 %reduce-scatter.17.cloned.1.call-start = ((), (), s32[]{:S(2)}) async-start(), calls=%async_computation.20 | async-start | bytes 3145728 | tf_op jit(solution)/shard_map/reduce_scatter | solution.py:268
  1049.4 91.2 %reduce-scatter.37.cloned.1.call-start = ((), (), s32[]{:S(2)}) async-start(), calls=%async_computation.32 | async-start | bytes 557056
  1052.6 148.9 %reduce-scatter.27.cloned.1.call-start = ((), (), s32[]{:S(2)}) async-start(), calls=%async_computation.27 | async-start | bytes 1114112 | tf_op jit(solution)/shard_map/reduce_scatter | solution.py:374
  1055.4 206.6 %reduce-scatter.25.cloned.1.call-start = ((), (), s32[]{:S(2)}) async-start(), calls=%async_computation.26 | async-start | bytes 1114112 | tf_op jit(solution)/shard_map/reduce_scatter | solution.py:373
  1058.4 268.9 %reduce-scatter.29.cloned.1.call-start = ((), (), s32[]{:S(2)}) async-start(), calls=%async_computation.28 | async-start | bytes 2228224 | tf_op jit(solution)/shard_map/reduce_scatter | solution.py:375
  1063.1 328.9 %reduce-scatter.23.cloned.1.call-start = ((), (), s32[]{:S(2)}) async-start(), calls=%async_computation.25 | async-start | bytes 2228224 | tf_op jit(solution)/shard_map/reduce_scatter | solution.py:372
  1067.1 507.8 %reduce-scatter.35.cloned.1.call-start = ((), (), s32[]{:S(2)}) async-start(), calls=%async_computation.31 | async-start | bytes 17825792 | tf_op jit(solution)/shard_map/reduce_scatter | solution.py:314
  1093.6 663.9 %reduce-scatter.31.cloned.1.call-start = ((), (), s32[]{:S(2)}) async-start(), calls=%async_computation.29 | async-start | bytes 17825792 | tf_op jit(solution)/shard_map/reduce_scatter | solution.py:312
  1114.2 826.2 %reduce-scatter.33.cloned.1.call-start = ((), (), s32[]{:S(2)}) async-start(), calls=%async_computation.30 | async-start | bytes 17825792 | tf_op jit(solution)/shard_map/reduce_scatter | solution.py:313
  (44 other events, 557.4 us)
Sparse Core Ops, SparseCore 0:
  35.8 30.3 all-gather.10
  68.4 37.9 all-gather.12
  108.6 36.8 all-gather.14
  151.3 53.1 reduce-scatter.14
  206.0 33.0 all-gather.24
  241.2 33.1 all-gather.16
  276.8 74.8 all-gather.20
  354.1 73.1 all-gather.18
  429.8 73.1 all-gather.22
  702.7 54.2 reduce-scatter.18
  763.7 33.1 all-gather.26
  949.3 31.8 reduce-scatter.20
  1049.5 31.8 reduce-scatter.16
  1084.8 55.7 reduce-scatter.36
  1145.1 56.3 reduce-scatter.26
  1205.6 56.4 reduce-scatter.24
  1266.7 60.5 reduce-scatter.28
  1331.5 60.5 reduce-scatter.22
  1397.3 177.5 reduce-scatter.34
  1579.9 177.5 reduce-scatter.30
  1762.8 177.5 reduce-scatter.32
where the time goes:
time: 1960 us; the launch traced here: 1950 us
  waiting for transfers between devices  962 us (49%)
  local copies, waits for them, and re-layouts  461 us (24%)
  matrix products  342 us (17%)
  other arithmetic  96.7 us (5%)
  blocking collectives  68.3 us (3%)
    reduce_scatter x1, waiting for transfers between devices, per_device(): lax.psum_scatter(grad_up_w, 'fsdp', scatter_dimension=1, tiled=True)  183 us
    reduce_scatter x1, waiting for transfers between devices, per_device(): lax.psum_scatter(grad_down_w, 'fsdp', scatter_dimension=1, tiled=True)  183 us
    reduce_scatter x1, waiting for transfers between devices, per_device(): lax.psum_scatter(grad_gate_w, 'fsdp', scatter_dimension=1, tiled=True)  183 us
    gather x2, local copies, waits for them, and re-layouts, per_device(): grad_padded[slot_token]  116 us
    gather x1, local copies, waits for them, and re-layouts, per_device(): gate_padded[source][:, None] * grad_padded[slot_token]  68 us
    reduce_scatter x1, waiting for transfers between devices, per_device(): lax.psum_scatter(grad_out_w, 'fsdp', scatter_dimension=0, tiled=True)  65.2 us
    reduce_scatter x1, waiting for transfers between devices, per_device(): lax.psum_scatter(grad_query_w, 'fsdp', scatter_dimension=0, tiled=True)  64.8 us
    reduce_scatter x1, waiting for transfers between devices, per_device(): lax.psum_scatter(grad_key_w, 'fsdp', scatter_dimension=0, tiled=True)  60.6 us
  transfers between devices with their start and end apart: 21, of which 12 were waited for; matrix products, arithmetic and copies ran while one was open for 28% of the time, Pallas kernels for 0%

commit v1 on v0

v1 whole, which is shorter than its diff:
```python
import functools

import jax
import jax.numpy as jnp
from jax import lax
from jax.experimental import pallas as pl
from jax.experimental.pallas import tpu as pltpu
from jax.sharding import PartitionSpec as P

HEAD_DIM = 64
EXPERTS = 16
MAXLEN = 512
EPSILON = 1e-06
BRANCH_SCALE = 0.22
ROPE_BASE = 10000.0
ROWS = 256
LANES = 128
CHUNKS = 2
MIB = 1 << 20
BF16 = jnp.bfloat16
F32 = jnp.float32


def dot_nn(left, right):
    return lax.dot_general(left, right, (((1,), (0,)), ((), ())), preferred_element_type=F32)


def dot_nt(left, right):
    return lax.dot_general(left, right, (((1,), (1,)), ((), ())), preferred_element_type=F32)


def dot_tn(left, right):
    return lax.dot_general(left, right, (((0,), (0,)), ((), ())), preferred_element_type=F32)


def seq_layout(lengths, row_total):
    places = jnp.arange(row_total, dtype=jnp.int32)
    ends = jnp.cumsum(lengths)
    starts = ends - lengths
    segment = jnp.sum((places[:, None] >= ends[None, :]).astype(jnp.int32), axis=1)
    chosen = segment[:, None] == jnp.arange(lengths.shape[0], dtype=jnp.int32)[None, :]
    opening = jnp.sum(jnp.where(chosen, starts[None, :], 0), axis=1)
    return (opening, places - opening)


def rotary_tables(position, head_size):
    halfway = head_size // 2
    ladder = jnp.arange(halfway, dtype=F32)
    inverse = jnp.exp(ladder * (-2.0 * jnp.log(ROPE_BASE) / head_size))
    angles = position.astype(F32)[:, None] * inverse[None, :]
    cos_half, sine_half = (jnp.cos(angles), jnp.sin(angles))
    copies = LANES // head_size
    return (
        jnp.concatenate([cos_half, cos_half] * copies, axis=1),
        jnp.concatenate([-sine_half, sine_half] * copies, axis=1),
    )


def rotate_lanes(values, cos_rows, sine_rows):
    lane = lax.broadcasted_iota(jnp.int32, cos_rows.shape, 1)
    first = lane % HEAD_DIM < HEAD_DIM // 2
    parts = []
    for at in range(0, values.shape[1], LANES):
        part = values[:, at : at + LANES]
        partner = jnp.where(
            first,
            pltpu.roll(part, LANES - HEAD_DIM // 2, 1),
            pltpu.roll(part, HEAD_DIM // 2, 1),
        )
        parts.append(part * cos_rows + partner * sine_rows)
    return jnp.concatenate(parts, axis=1)


def key_window(block):
    low = max(0, block * ROWS - ((MAXLEN - 1 + ROWS - 1) // ROWS) * ROWS)
    return (low, (block + 1) * ROWS)


def allowed_pairs(opening_rows, block, low, high):
    shape = (ROWS, high - low)
    query_at = block * ROWS + lax.broadcasted_iota(jnp.int32, shape, 0)
    key_at = low + lax.broadcasted_iota(jnp.int32, shape, 1)
    return (key_at <= query_at) & (key_at >= opening_rows)


def attend_kernel(
    q_width,
    x_ref,
    gain_ref,
    w_ref,
    cos_ref,
    sine_ref,
    opening_ref,
    a_ref,
    q_ref,
    k_ref,
    v_ref,
    o_ref,
    lse_ref,
    lse_cols,
):
    rows_all = x_ref.shape[0]
    kv_width = k_ref.shape[1]
    kv_heads = kv_width // HEAD_DIM
    group = q_width // kv_width
    scale = HEAD_DIM ** (-0.5)
    for block in range(rows_all // ROWS):
        at = pl.ds(block * ROWS, ROWS)
        x = x_ref[at, :].astype(F32)
        r1 = lax.rsqrt(jnp.mean(x * x, axis=1, keepdims=True) + EPSILON)
        a = (x * r1 * gain_ref[...]).astype(BF16)
        a_ref[at, :] = a
        qkv = dot_nn(a, w_ref[...])
        turned = rotate_lanes(
            qkv[:, : q_width + kv_width], cos_ref[at, :], sine_ref[at, :]
        ).astype(BF16)
        q_ref[at, :] = turned[:, :q_width]
        k_ref[at, :] = turned[:, q_width:]
        v_ref[at, :] = qkv[:, q_width + kv_width :].astype(BF16)
    lane = lax.broadcasted_iota(jnp.int32, (ROWS, LANES), 1)
    for block in range(rows_all // ROWS):
        at = pl.ds(block * ROWS, ROWS)
        low, high = key_window(block)
        keep = allowed_pairs(opening_ref[at, :], block, low, high)
        lse = jnp.zeros((ROWS, LANES), F32)
        outs = []
        for j in range(kv_heads):
            head = slice(j * HEAD_DIM, (j + 1) * HEAD_DIM)
            keys = k_ref[low:high, head]
            vals = v_ref[low:high, head]
            for g in range(group):
                h = j * group + g
                s = dot_nt(q_ref[at, h * HEAD_DIM : (h + 1) * HEAD_DIM], keys) * scale
                s = jnp.where(keep, s, -1e30)
                peak = jnp.max(s, axis=1, keepdims=True)
                p = jnp.exp(s - peak)
                total = jnp.sum(p, axis=1, keepdims=True)
                outs.append((dot_nn(p.astype(BF16), vals) / total).astype(BF16))
                lse = jnp.where(lane == h, peak + jnp.log(total), lse)
        o_ref[at, :] = jnp.concatenate(outs, axis=1)
        lse_cols[at, :] = lse
    lse_ref[...] = lse_cols[...].T[: lse_ref.shape[0], :]


def attend_back_kernel(
    q_ref,
    k_ref,
    v_ref,
    go_ref,
    lse_ref,
    cos_ref,
    sine_ref,
    opening_ref,
    x_ref,
    w_ref,
    d_ref,
    da_ref,
    gain_ref,
    dk_acc,
    dv_acc,
    dq_acc,
):
    rows_all, q_width = q_ref.shape
    kv_width = k_ref.shape[1]
    kv_heads = kv_width // HEAD_DIM
    group = q_width // kv_width
    scale = HEAD_DIM ** (-0.5)
    blocks = rows_all // ROWS
    dk_acc[...] = jnp.zeros_like(dk_acc)
    dv_acc[...] = jnp.zeros_like(dv_acc)
    for block in range(blocks):
        at = pl.ds(block * ROWS, ROWS)
        low, high = key_window(block)
        shape = (high - low, ROWS)
        query_at = block * ROWS + lax.broadcasted_iota(jnp.int32, shape, 1)
        key_at = low + lax.broadcasted_iota(jnp.int32, shape, 0)
        keep = (key_at <= query_at) & (key_at >= opening_ref[:, at])
        for j in range(kv_heads):
            head = slice(j * HEAD_DIM, (j + 1) * HEAD_DIM)
            keys = k_ref[low:high, head]
            vals = v_ref[low:high, head]
            dk = jnp.zeros((high - low, HEAD_DIM), F32)
            dv = jnp.zeros((high - low, HEAD_DIM), F32)
            for g in range(group):
                h = j * group + g
                mine = slice(h * HEAD_DIM, (h + 1) * HEAD_DIM)
                q = q_ref[at, mine]
                go = go_ref[at, mine]
                s = dot_nt(keys, q) * scale
                p = jnp.where(keep, jnp.exp(jnp.minimum(s - lse_ref[h : h + 1, at], 1.0)), 0.0)
                dp = dot_nt(vals, go)
                inner = jnp.sum(p * dp, axis=0, keepdims=True)
                ds = (p * (dp - inner)).astype(BF16)
                dq_acc[at, mine] = dot_tn(ds, keys) * scale
                dk = dk + dot_nn(ds, q)
                dv = dv + dot_nn(p.astype(BF16), go)
            dk_acc[low:high, head] += dk * scale
            dv_acc[low:high, head] += dv
    gain = jnp.zeros((1, x_ref.shape[1]), F32)
    for block in range(blocks):
        at = pl.ds(block * ROWS, ROWS)
        turned = jnp.concatenate([dq_acc[at, :], dk_acc[at, :]], axis=1)
        back = rotate_lanes(turned, cos_ref[at, :], -sine_ref[at, :])
        d = jnp.concatenate([back, dv_acc[at, :]], axis=1).astype(BF16)
        d_ref[at, :] = d
        da = dot_nt(d, w_ref[...])
        da_ref[at, :] = da.astype(BF16)
        x = x_ref[at, :].astype(F32)
        r1 = lax.rsqrt(jnp.mean(x * x, axis=1, keepdims=True) + EPSILON)
        gain = gain + jnp.sum(da * (x * r1), axis=0, keepdims=True)
    gain_ref[...] = gain


def middle_kernel(x_ref, own_ref, other_ref, w_own_ref, w_other_ref, gain_ref, x1_ref, b_ref):
    attn = dot_nt(own_ref[...], w_own_ref[...]) + dot_nt(other_ref[...], w_other_ref[...])
    x1 = x_ref[...].astype(F32) + BRANCH_SCALE * attn
    x1_ref[...] = x1
    r2 = lax.rsqrt(jnp.mean(x1 * x1, axis=1, keepdims=True) + EPSILON)
    b_ref[...] = (x1 * r2 * gain_ref[...]).astype(BF16)


def experts_kernel(
    first, started, b_ref, bt_ref, dy_ref, dyt_ref, gates_ref, w_ref, moe_in, db_in, g_ref, moe_ref, db_ref
):
    step = pl.program_id(0)
    rows_all, width = b_ref.shape

    @pl.when(step == 0)
    def _():
        if started:
            moe_ref[...] = moe_in[...]
            db_ref[...] = db_in[...]
        else:
            moe_ref[...] = jnp.zeros_like(moe_ref)
            db_ref[...] = jnp.zeros_like(db_ref)

    hidden = w_ref.shape[-1]
    gate_w = w_ref[:, 0, 0].reshape(width, hidden)
    up_w = w_ref[:, 0, 1].reshape(width, hidden)
    down_w = w_ref[:, 0, 2].reshape(width, hidden)
    lane = lax.broadcasted_iota(jnp.int32, (ROWS, gates_ref.shape[1]), 1)
    weighted, gate_grads, up_grads = [], [], []
    for block in range(rows_all // ROWS):
        at = pl.ds(block * ROWS, ROWS)
        b = b_ref[at, :]
        route = jnp.sum(
            jnp.where(lane == first + step, gates_ref[at, :], 0.0), axis=1, keepdims=True
        )
        gate = dot_nn(b, gate_w)
        up = dot_nn(b, up_w)
        back = dot_nn(dy_ref[at, :], down_w) * (route * BRANCH_SCALE)
        sig = jax.nn.sigmoid(gate)
        silu = gate * sig
        h = (silu * up * route).astype(BF16)
        dg = (back * up * sig * (1.0 + gate * (1.0 - sig))).astype(BF16)
        du = (back * silu).astype(BF16)
        moe_ref[at, :] += dot_nt(h, down_w)
        db_ref[at, :] += dot_nt(dg, gate_w) + dot_nt(du, up_w)
        weighted.append(h)
        gate_grads.append(dg)
        up_grads.append(du)
    shards, _, _, per_shard, _ = g_ref.shape
    shape = (shards, per_shard, hidden)
    g_ref[:, 0, 0] = dot_nn(bt_ref[...], jnp.concatenate(gate_grads, axis=0)).astype(BF16).reshape(shape)
    g_ref[:, 0, 1] = dot_nn(bt_ref[...], jnp.concatenate(up_grads, axis=0)).astype(BF16).reshape(shape)
    down_grad = dot_nn(dyt_ref[...], jnp.concatenate(weighted, axis=0)) * BRANCH_SCALE
    g_ref[:, 0, 2] = down_grad.astype(BF16).reshape(shape)


def whole(shape):
    return pl.BlockSpec(shape, lambda *_: (0,) * len(shape), pipeline_mode=pl.Buffered(1))


def run_experts(first, b, bt, dy, dyt, gates, weights, carried):
    rows_all, width = b.shape
    shards, count, kinds, per_shard, hidden = weights.shape
    block = (shards, 1, kinds, per_shard, hidden)
    started = carried is not None
    full = jax.ShapeDtypeStruct((rows_all, width), F32)
    moved = lambda e: (0, e, 0, 0, 0)
    if not started:
        carried = (jnp.zeros((8, LANES), F32),) * 2
    flops = 9 * 2 * rows_all * width * hidden * count
    return pl.pallas_call(
        functools.partial(experts_kernel, first, started),
        grid=(count,),
        in_specs=[whole(t.shape) for t in (b, bt, dy, dyt, gates)]
        + [pl.BlockSpec(block, moved)]
        + [whole(t.shape) for t in carried],
        out_specs=[
            pl.BlockSpec(block, moved),
            whole((rows_all, width)),
            whole((rows_all, width)),
        ],
        out_shape=[jax.ShapeDtypeStruct(weights.shape, BF16), full, full],
        compiler_params=pltpu.CompilerParams(vmem_limit_bytes=56 * MIB),
        cost_estimate=pl.CostEstimate(
            flops=flops, bytes_accessed=4 * weights.size + 24 * MIB, transcendentals=0
        ),
        name="experts",
    )(b, bt, dy, dyt, gates, weights, *carried)


def per_device(
    tokens,
    seq_lens,
    routes,
    route_gates,
    query_weight,
    key_matrix,
    value_matrix,
    out_weight,
    norm_gains,
    gate_weight,
    up_weight,
    down_weight,
    cotangent,
):
    local_rows, width = tokens.shape
    rows_all = local_rows * 2
    shards = lax.axis_size("fsdp")
    per_shard = width // shards
    q_width = query_weight.shape[1]
    kv_width = key_matrix.shape[1]
    qkv_width = q_width + 2 * kv_width
    place = lax.axis_index("tp")
    mine_at = place * local_rows
    other_at = (1 - place) * local_rows

    def swap(values):
        return lax.ppermute(values, "tp", [(0, 1), (1, 0)])

    def both(own, other):
        return jnp.where(
            place == 0,
            jnp.concatenate([own, other], axis=0),
            jnp.concatenate([other, own], axis=0),
        )

    attn_local = jnp.concatenate(
        [
            query_weight,
            key_matrix,
            value_matrix,
            out_weight,
            swap(out_weight),
            jnp.pad(norm_gains.T, ((0, 0), (0, LANES - 2))),
        ],
        axis=1,
    )
    attn_w = lax.all_gather(attn_local, "fsdp", axis=0, tiled=True)
    gain_rows = attn_w[:, qkv_width + 2 * q_width :][:, :2].T.astype(F32)
    expert_local = jnp.stack([gate_weight, up_weight, down_weight], axis=1)
    per_chunk = EXPERTS // CHUNKS
    small_shards = per_shard % 16 != 0
    expert_w = []
    for chunk in range(CHUNKS):
        part = lax.all_gather(
            expert_local[chunk * per_chunk : (chunk + 1) * per_chunk], "fsdp", axis=0, tiled=False
        )
        if small_shards:
            part = part.transpose(1, 2, 0, 3, 4).reshape((1,) + part.shape[1:3] + (width, -1))
        expert_w.append(part)

    x_full = both(tokens, swap(tokens))
    dy_full = both(cotangent, swap(cotangent))
    dy_t = dy_full.T
    opening, position = seq_layout(seq_lens[0], rows_all)
    cos_table, sine_table = rotary_tables(position, HEAD_DIM)
    gates = jnp.sum(
        jnp.where(
            routes[:, :, None] == jnp.arange(LANES, dtype=jnp.int32)[None, None, :],
            route_gates[:, :, None],
            0.0,
        ),
        axis=1,
    )

    heads = q_width // HEAD_DIM
    rows_of = lambda n, t: jax.ShapeDtypeStruct((rows_all, n), t)
    normed_one, q_rows, k_rows, v_rows, o_own, lse = pl.pallas_call(
        functools.partial(attend_kernel, q_width),
        grid=(1,),
        in_specs=[
            whole((rows_all, width)),
            whole((1, width)),
            whole((width, qkv_width)),
            whole((rows_all, LANES)),
            whole((rows_all, LANES)),
            whole((rows_all, 1)),
        ],
        out_specs=[
            whole((rows_all, width)),
            whole((rows_all, q_width)),
            whole((rows_all, kv_width)),
            whole((rows_all, kv_width)),
            whole((rows_all, q_width)),
            whole((heads, rows_all)),
        ],
        out_shape=[
            rows_of(width, BF16),
            rows_of(q_width, BF16),
            rows_of(kv_width, BF16),
            rows_of(kv_width, BF16),
            rows_of(q_width, BF16),
            jax.ShapeDtypeStruct((heads, rows_all), F32),
        ],
        scratch_shapes=[pltpu.VMEM((rows_all, LANES), F32)],
        compiler_params=pltpu.CompilerParams(vmem_limit_bytes=48 * MIB),
        cost_estimate=pl.CostEstimate(
            flops=8 * rows_all * width * qkv_width, bytes_accessed=12 * MIB, transcendentals=0
        ),
        name="attend",
    )(x_full, gain_rows[:1], attn_w, cos_table, sine_table, opening[:, None])

    o_other = swap(o_own)
    steps = rows_all // ROWS
    by_rows = lambda n: pl.BlockSpec((ROWS, n), lambda i: (i, 0))
    first_out = qkv_width // q_width
    middle, normed_two = pl.pallas_call(
        middle_kernel,
        grid=(steps,),
        in_specs=[
            by_rows(width),
            by_rows(q_width),
            by_rows(q_width),
            pl.BlockSpec((width, q_width), lambda i: (0, first_out)),
            pl.BlockSpec((width, q_width), lambda i: (0, first_out + 1)),
            pl.BlockSpec((1, width), lambda i: (0, 0)),
        ],
        out_specs=[by_rows(width), by_rows(width)],
        out_shape=[rows_of(width, F32), rows_of(width, BF16)],
        compiler_params=pltpu.CompilerParams(vmem_limit_bytes=32 * MIB),
        cost_estimate=pl.CostEstimate(
            flops=4 * rows_all * width * q_width, bytes_accessed=14 * MIB, transcendentals=0
        ),
        name="middle",
    )(x_full, o_own, o_other, attn_w, attn_w, gain_rows[1:])

    normed_two_t = normed_two.T
    carried = None
    expert_parts = []
    for chunk in range(CHUNKS):
        grads, moe, grad_two = run_experts(
            chunk * per_chunk,
            normed_two,
            normed_two_t,
            dy_full,
            dy_t,
            gates,
            expert_w[chunk],
            carried,
        )
        carried = (moe, grad_two)
        if small_shards:
            grads = grads.reshape(per_chunk, 3, shards, per_shard, -1).transpose(2, 0, 1, 3, 4)
        expert_parts.append(
            lax.psum_scatter(grads, "fsdp", scatter_dimension=0, tiled=False)
        )
    expert_grads = jnp.concatenate(expert_parts, axis=0).astype(F32)

    def own_rows(values):
        return lax.dynamic_slice_in_dim(values, mine_at, local_rows, axis=0)

    def other_rows(values):
        return lax.dynamic_slice_in_dim(values, other_at, local_rows, axis=0)

    grad_two_own = own_rows(grad_two) + swap(other_rows(grad_two).astype(BF16)).astype(F32)
    middle_own = own_rows(middle)
    scale_two = lax.rsqrt(jnp.mean(middle_own * middle_own, axis=1, keepdims=True) + EPSILON)
    unit_two = middle_own * scale_two
    scaled_two = grad_two_own * gain_rows[1]
    grad_middle = cotangent.astype(F32) + scale_two * (
        scaled_two - unit_two * jnp.mean(scaled_two * unit_two, axis=1, keepdims=True)
    )
    gain_two = jnp.sum(grad_two_own * unit_two, axis=0, keepdims=True)
    grad_attn = (BRANCH_SCALE * grad_middle).astype(BF16)
    out_own = attn_w[:, qkv_width : qkv_width + q_width]
    out_other = attn_w[:, qkv_width + q_width : qkv_width + 2 * q_width]
    go_send = jnp.dot(grad_attn, out_other, preferred_element_type=F32).astype(BF16)
    go_other = swap(go_send)
    go_own = jnp.dot(grad_attn, out_own, preferred_element_type=F32).astype(BF16)
    go_full = both(go_own, go_other)
    grad_attn_full = both(grad_attn, swap(grad_attn))
    moe_own = own_rows(moe) + swap(other_rows(moe).astype(BF16)).astype(F32)
    layer_out = (middle_own + BRANCH_SCALE * moe_own).astype(BF16)

    d_qkv, grad_one, gain_one = pl.pallas_call(
        attend_back_kernel,
        grid=(1,),
        in_specs=[
            whole((rows_all, q_width)),
            whole((rows_all, kv_width)),
            whole((rows_all, kv_width)),
            whole((rows_all, q_width)),
            whole((heads, rows_all)),
            whole((rows_all, LANES)),
            whole((rows_all, LANES)),
            whole((1, rows_all)),
            whole((rows_all, width)),
            whole((width, qkv_width)),
        ],
        out_specs=[whole((rows_all, qkv_width)), whole((rows_all, width)), whole((1, width))],
        out_shape=[
            rows_of(qkv_width, BF16),
            rows_of(width, BF16),
            jax.ShapeDtypeStruct((1, width), F32),
        ],
        scratch_shapes=[
            pltpu.VMEM((rows_all, kv_width), F32),
            pltpu.VMEM((rows_all, kv_width), F32),
            pltpu.VMEM((rows_all, q_width), F32),
        ],
        compiler_params=pltpu.CompilerParams(vmem_limit_bytes=48 * MIB),
        cost_estimate=pl.CostEstimate(
            flops=16 * rows_all * width * qkv_width, bytes_accessed=12 * MIB, transcendentals=0
        ),
        name="attend_back",
    )(
        q_rows,
        k_rows,
        v_rows,
        go_full,
        lse,
        cos_table,
        sine_table,
        opening[None, :],
        x_full,
        attn_w,
    )

    grad_one_own = own_rows(grad_one).astype(F32) + swap(other_rows(grad_one)).astype(F32)
    gain_part = jnp.concatenate([gain_one, gain_two], axis=0)
    gain_sum = gain_part + swap(gain_part)
    grad_qkv_w = dot_tn(normed_one, d_qkv)
    grad_out_w = dot_tn(grad_attn_full, o_own)
    attn_parts = jnp.concatenate(
        [grad_qkv_w, grad_out_w, jnp.pad(gain_sum.T, ((0, 0), (0, LANES - 2)))], axis=1
    ).astype(BF16)
    attn_grads = lax.psum_scatter(attn_parts, "fsdp", scatter_dimension=0, tiled=True).astype(F32)

    inputs = tokens.astype(F32)
    scale_one = lax.rsqrt(jnp.mean(inputs * inputs, axis=1, keepdims=True) + EPSILON)
    unit_one = inputs * scale_one
    scaled_one = grad_one_own * gain_rows[0]
    grad_tokens = (
        grad_middle
        + scale_one
        * (scaled_one - unit_one * jnp.mean(scaled_one * unit_one, axis=1, keepdims=True))
    ).astype(BF16)
    return (
        layer_out,
        grad_tokens,
        attn_grads[:, :q_width],
        attn_grads[:, q_width : q_width + kv_width],
        attn_grads[:, q_width + kv_width : qkv_width],
        attn_grads[:, qkv_width : qkv_width + q_width],
        attn_grads[:, qkv_width + q_width :][:, :2].T,
        expert_grads[:, 0],
        expert_grads[:, 1],
        expert_grads[:, 2],
    )


def solution(mesh):
    in_specs = (
        P(("fsdp", "tp"), None),
        P("fsdp", None),
        P("fsdp", None),
        P("fsdp", None),
        P("fsdp", "tp"),
        P("fsdp", "tp"),
        P("fsdp", "tp"),
        P("fsdp", "tp"),
        P(None, "fsdp"),
        P(None, "fsdp", "tp"),
        P(None, "fsdp", "tp"),
        P(None, "fsdp", "tp"),
        P(("fsdp", "tp"), None),
    )
    out_specs = (
        P(("fsdp", "tp"), None),
        P(("fsdp", "tp"), None),
        P("fsdp", "tp"),
        P("fsdp", "tp"),
        P("fsdp", "tp"),
        P("fsdp", "tp"),
        P(None, "fsdp"),
        P(None, "fsdp", "tp"),
        P(None, "fsdp", "tp"),
        P(None, "fsdp", "tp"),
    )
    return jax.shard_map(
        per_device, mesh=mesh, in_specs=in_specs, out_specs=out_specs, check_vma=False
    )
```

time: 1960 us -> 812 us (0.41)
  waiting for transfers between devices: 962 us -> 503 us
  local copies, waits for them, and re-layouts: 461 us -> 65.1 us
  matrix products: 342 us -> 9.28 us
  Pallas kernels: 0 us -> 160 us
  blocking collectives: 68.3 us -> 0 us
  other arithmetic: 96.7 us -> 36.1 us
    reduce_scatter x11 -> x2, waiting for transfers between devices: 900 us -> 271 us  [per_device(): lax.psum_scatter(grads, 'fsdp', scatter_dimension=0, tiled=False)]
    gather x6 -> x0, local copies, waits for them, and re-layouts: 355 us -> none  [the longest x2 116 us: per_device(): grad_padded[slot_token]]
    dot_general x35 -> x4, matrix products: 342 us -> 9.28 us  [the longest x2 5.4 us: dot_tn(): lax.dot_general(left, right, (((0,), (0,)), ((), ())), preferred_element_...]
    pallas_call x0 -> x5, Pallas kernels: none -> 160 us  [the longest x2 108 us: run_experts(): pl.pallas_call(functools.partial(experts_kernel, first, started), grid=(c...]
    ppermute x0 -> x10, waiting for transfers between devices: none -> 98.2 us  [swap(): return lax.ppermute(values, 'tp', [(0, 1), (1, 0)])]
    all_gather x3 -> x0, blocking collectives: 62.8 us -> none  [the longest x1 23.2 us: per_device(): lax.all_gather(norm_gains, 'fsdp', axis=1, tiled=True)]
    dynamic_update_slice x4 -> x0, local copies, waits for them, and re-layouts: 41.4 us -> none  [attend_forward(): lax.map(one_block, (query_rows.reshape((blocks, block_rows) + query_rows....]
    reduce_sum x8 -> x4, other arithmetic: 50.2 us -> 11.6 us  [the longest x1 6.01 us: per_device(): jnp.sum(jnp.where(routes[:, :, None] == jnp.arange(LANES, dtype=jnp.int32...]
  transfers between devices with their start and end apart: 21 -> 16, of which waited for: 12 -> 12; matrix products, arithmetic and copies ran while one was open for 28% -> 9% of each run, Pallas kernels for 0% -> 13%
where the time goes in v1:
time: 812 us; the launch traced here: 802 us
  waiting for transfers between devices  503 us (62%)
  Pallas kernels  160 us (20%)
  local copies, waits for them, and re-layouts  65.1 us (8%)
  other arithmetic  36.1 us (4%)
  between operations  14.8 us (2%)
  starting transfers between devices  13.1 us (2%)
  matrix products  9.28 us (1%)
    reduce_scatter x2, waiting for transfers between devices, per_device(): lax.psum_scatter(grads, 'fsdp', scatter_dimension=0, tiled=False)  271 us
    pallas_call x2, Pallas kernels, run_experts(): pl.pallas_call(functools.partial(experts_kernel, first, started), grid=(c...  108 us
    ppermute x10, waiting for transfers between devices, swap(): return lax.ppermute(values, 'tp', [(0, 1), (1, 0)])  98.2 us
    all_gather x2, waiting for transfers between devices, per_device(): lax.all_gather(expert_local[chunk * per_chunk:(chunk + 1) * per_chunk], '...  76.1 us
    unnamed x7, waiting for transfers between devices  39.9 us
    pallas_call x1, Pallas kernels, per_device(): pl.pallas_call(attend_back_kernel, grid=(1,), in_specs=[whole((rows_all,...  29 us
    unnamed x64, local copies, waits for them, and re-layouts  22.3 us
    all_gather x2, local copies, waits for them, and re-layouts, per_device(): lax.all_gather(expert_local[chunk * per_chunk:(chunk + 1) * per_chunk], '...  21.8 us
  transfers between devices with their start and end apart: 16, of which 12 were waited for; matrix products, arithmetic and copies ran while one was open for 9% of the time, Pallas kernels for 13%

profile of v1, /device:TPU:0, one launch (start us, length us, event | category | flops | bytes accessed | tf_op | source)
XLA Modules:
  0.0 802.0 jit_solution(13827160556198341169)
XLA Ops:
  7.2 3.0 collective-permute-start.1
  24.2 20.7 %collective-permute-done = bf16[512,1024]{1,0:T(8,128)(2,1)} collective-permute-done((bf16[512,1024]{1,0:T(8,128)(2,1)S(1)}, bf16[512,1024]{1,0:T(8,128)(2,1)}, u32[]{:S(2)}, u32[]{:S(2)}) %collective-permute-start) | collective-permute-done | bytes 1048608 | tf_op jit(solution)/shard_map/ppermute | solution.py:331
  44.9 4.0 maximum_select_fusion.x_ref
  48.9 18.5 %all-gather.6.cloned.1.call-done.w_ref.w_own_ref.w_other_ref = bf16[1024,2176]{1,0:T(8,128)(2,1)} async-done(((bf16[64,2176]{1,0:T(8,128)(2,1)}), bf16[1024,2176]{1,0:T(8,128)(2,1)}) %all-gather.6.cloned.1.call-update) | async-done | bytes 4456464 | tf_op jit(solution)/shard_map/all_gather | solution.py:351
  70.2 18.4 %attend.1 = (bf16[1024,1024]{1,0:T(8,128)(2,1)}, bf16[1024,512]{1,0:T(8,128)(2,1)S(1)}, bf16[1024,256]{1,0:T(8,128)(2,1)S(1)}, bf16[1024,256]{1,0:T(8,128)(2,1)S...) custom-call(bf16[1024,1024]{1,0:T(8,128)(2,1)} %maximum_select_fusion.x_ref, f32[1,1024]{1,0:T(1,128)S(1)} %copy.84.gain_ref, ...), custom_call_target="tpu_custom_call" | custom-call | flops 8589934592 | bytes 12582912 | tf_op jit(solution)/shard_map/attend/pallas_call | solution.py:381
  93.0 6.0 select_reduce_fusion.gates_ref
  99.0 4.8 maximum_select_fusion.1.dy_ref
  103.8 4.1 copy.93.dyt_ref
  109.1 7.4 collective-permute-done.2.other_ref
  116.6 2.3 copy-done
  118.9 4.6 middle.1
  126.8 4.0 copy.87
  130.8 38.7 %all-gather.10.cloned.1.call-done = bf16[128,3,64,256]{3,2,0,1:T(8,128)(2,1)} async-done(((bf16[8,3,64,256]{3,2,0,1:T(8,128)(2,1)}), bf16[128,3,64,256]{3,2,0,1:T(8,128)(2,1)}) %all-gather.10.cloned.1.call-update) | async-done | bytes 12582928 | tf_op jit(solution)/shard_map/all_gather | solution.py:358
  169.5 10.9 %copy.91 = bf16[128,3,64,256]{3,2,1,0:T(8,128)(2,1)} copy(bf16[128,3,64,256]{3,2,0,1:T(8,128)(2,1)} %all-gather.10.cloned.1.call-done) | data formatting | bytes 25165824 | tf_op jit(solution)/shard_map/all_gather | solution.py:358
  181.0 52.9 %experts.2 = (bf16[16,8,3,64,256]{4,3,2,1,0:T(8,128)(2,1)}, f32[1024,1024]{1,0:T(8,128)}, f32[1024,1024]{1,0:T(8,128)}) custom-call(bf16[1024,1024]{1,0:T(8,128)(2,1)} %copy-done.4, bf16[1024,1024]{1,0:T(8,128)(2,1)} %bitcast.44, bf16[1024,1024]{1,0:T(8,128)(2,1)} %maximum_select_fusion.1.dy_ref, bf16[1024,1024]{1,0:T(8,128)(2,1)} %copy.93.dyt_ref, ...), custom_call_target="tpu_custom_call" | custom-call | flops 38654705664 | bytes 50331648 | tf_op jit(solution)/shard_map/experts/pallas_call | solution.py:284
  233.9 37.4 %all-gather.8.cloned.1.call-done = bf16[128,3,64,256]{3,2,0,1:T(8,128)(2,1)} async-done(((bf16[8,3,64,256]{3,2,0,1:T(8,128)(2,1)}), bf16[128,3,64,256]{3,2,0,1:T(8,128)(2,1)}) %all-gather.8.cloned.1.call-update) | async-done | bytes 12582928 | tf_op jit(solution)/shard_map/all_gather | solution.py:358
  271.3 10.9 %copy.90 = bf16[128,3,64,256]{3,2,1,0:T(8,128)(2,1)} copy(bf16[128,3,64,256]{3,2,0,1:T(8,128)(2,1)} %all-gather.8.cloned.1.call-done) | data formatting | bytes 25165824 | tf_op jit(solution)/shard_map/all_gather | solution.py:358
  282.2 55.6 %experts.3 = (bf16[16,8,3,64,256]{4,3,2,1,0:T(8,128)(2,1)}, f32[1024,1024]{1,0:T(8,128)}, f32[1024,1024]{1,0:T(8,128)}) custom-call(bf16[1024,1024]{1,0:T(8,128)(2,1)} %copy-done.4, bf16[1024,1024]{1,0:T(8,128)(2,1)} %bitcast.45, bf16[1024,1024]{1,0:T(8,128)(2,1)} %maximum_select_fusion.1.dy_ref, bf16[1024,1024]{1,0:T(8,128)(2,1)} %copy.93.dyt_ref, ...), custom_call_target="tpu_custom_call" | custom-call | flops 38654705664 | bytes 50331648 | tf_op jit(solution)/shard_map/experts/pallas_call | solution.py:284
  337.7 2.7 dynamic-slice_convert_fusion
  341.9 2.7 dynamic-slice_convert_fusion.1
  347.0 19.6 %collective-permute-done.5 = bf16[512,1024]{1,0:T(8,128)(2,1)S(1)} collective-permute-done((bf16[512,1024]{1,0:T(8,128)(2,1)}, bf16[512,1024]{1,0:T(8,128)(2,1)S(1)}, u32[]{:S(2)}, u32[]{:S(2)}) %collective-permute-start.5) | collective-permute-done | bytes 1048608 | tf_op jit(solution)/shard_map/ppermute | solution.py:331
  366.7 3.1 multiply_reduce_fusion
  369.8 18.7 %collective-permute-done.4 = bf16[512,1024]{1,0:T(8,128)(2,1)S(1)} collective-permute-done((bf16[512,1024]{1,0:T(8,128)(2,1)}, bf16[512,1024]{1,0:T(8,128)(2,1)S(1)}, u32[]{:S(2)}, u32[]{:S(2)}) %collective-permute-start.4) | collective-permute-done | bytes 1048608 | tf_op jit(solution)/shard_map/ppermute | solution.py:331
  388.5 5.4 multiply_convert_fusion
  399.9 10.9 %collective-permute-done.6 = bf16[512,512]{1,0:T(8,128)(2,1)S(1)} collective-permute-done((bf16[512,512]{1,0:T(8,128)(2,1)S(1)}, bf16[512,512]{1,0:T(8,128)(2,1)S(1)}, u32[]{:S(2)}, u32[]{:S(2)}) %collective-permute-start.6) | collective-permute-done | bytes 524320 | tf_op jit(solution)/shard_map/ppermute | solution.py:331
  411.3 29.0 %attend_back.1 = (bf16[1024,1024]{1,0:T(8,128)(2,1)}, bf16[1024,1024]{1,0:T(8,128)(2,1)}, f32[1,1024]{1,0:T(1,128)S(1)}) custom-call(bf16[1024,512]{1,0:T(8,128)(2,1)S(1)} %copy-done.10, bf16[1024,256]{1,0:T(8,128)(2,1)S(1)} %copy-done.12, bf16[1024,256]{1,0:T(8,128)(2,1)S(1)} %copy-done.14, bf16[1024,512]{1,0:T(8,128)(2,1)S(1)} %maximum_select_fusion.6.go_ref, ...), custom_call_target="tpu_custom_call" | custom-call | flops 17179869184 | bytes 12582912 | tf_op jit(solution)/shard_map/attend_back/pallas_call | solution.py:488
  441.9 4.0 convolution_convert_fusion
  447.8 3.7 copy.98
  454.8 20.9 %collective-permute-done.7 = bf16[512,1024]{1,0:T(8,128)(2,1)S(1)} collective-permute-done((bf16[512,1024]{1,0:T(8,128)(2,1)S(1)}, bf16[512,1024]{1,0:T(8,128)(2,1)S(1)}, u32[]{:S(2)}, u32[]{:S(2)}) %collective-permute-start.7) | collective-permute-done | bytes 1048608 | tf_op jit(solution)/shard_map/ppermute | solution.py:331
  478.1 38.1 %reduce-scatter.10.cloned.1.call-done = bf16[64,1664]{1,0:T(8,128)(2,1)} async-done(((bf16[1024,1664]{1,0:T(8,128)(2,1)}), bf16[64,1664]{1,0:T(8,128)(2,1)}) %reduce-scatter.10.cloned.1.call-update) | async-done | bytes 213008
  521.1 132.7 %reduce-scatter.8.cloned.1.call-done = bf16[1,8,3,64,256]{4,3,2,1,0:T(8,128)(2,1)} async-done(((bf16[16,8,3,64,256]{4,3,2,1,0:T(8,128)(2,1)}), bf16[1,8,3,64,256]{4,3,2,1,0:T(8,128)(2,1)}) %reduce-scatter.8.cloned.1.call-update) | async-done | bytes 786448 | tf_op jit(solution)/shard_map/reduce_scatter | solution.py:458
  653.8 137.9 %reduce-scatter.6.cloned.1.call-done = bf16[1,8,3,64,256]{4,3,2,1,0:T(8,128)(2,1)} async-done(((bf16[16,8,3,64,256]{4,3,2,1,0:T(8,128)(2,1)}), bf16[1,8,3,64,256]{4,3,2,1,0:T(8,128)(2,1)}) %reduce-scatter.6.cloned.1.call-update) | async-done | bytes 786448 | tf_op jit(solution)/shard_map/reduce_scatter | solution.py:458
  (126 shorter events, 53.6 us)
Async XLA Ops:
  7.2 60.2 %all-gather.6.cloned.1.call-start = ((), (), s32[]{:S(2)}) async-start(), calls=%async_computation.3 | async-start | bytes 4734976 | tf_op jit(solution)/shard_map/all_gather | solution.py:351
  7.2 7.0 collective-permute-start.1
  15.0 154.6 %all-gather.10.cloned.1.call-start = ((), (), s32[]{:S(2)}) async-start(), calls=%async_computation.7 | async-start | bytes 13369344 | tf_op jit(solution)/shard_map/all_gather | solution.py:358
  16.6 4.2 copy-start.23
  17.8 253.4 %all-gather.8.cloned.1.call-start = ((), (), s32[]{:S(2)}) async-start(), calls=%async_computation.6 | async-start | bytes 13369344 | tf_op jit(solution)/shard_map/all_gather | solution.py:358
  18.6 497.6 %reduce-scatter.10.cloned.1.call-start = ((), (), s32[]{:S(2)}) async-start(), calls=%async_computation.8 | async-start | bytes 3620864
  18.6 26.3 %collective-permute-start = (bf16[512,1024]{1,0:T(8,128)(2,1)S(1)}, bf16[512,1024]{1,0:T(8,128)(2,1)}, u32[]{:S(2)}, u32[]{:S(2)}) collective-permute-start(bf16[512,1024]{1,0:T(8,128)(2,1)S(1)} %copy-done.15), channel_id=1, source_target_pairs={{0,1},{1,0},{2,3},{3,2},{4,5},{5,4},{6,7},{7,6},{8,9},{9,8},{10,11... | collective-permute-start | bytes 3145736 | tf_op jit(solution)/shard_map/ppermute | solution.py:331
  19.2 79.8 %collective-permute-start.3 = (bf16[512,1024]{1,0:T(8,128)(2,1)}, bf16[512,1024]{1,0:T(8,128)(2,1)}, u32[]{:S(2)}, u32[]{:S(2)}) collective-permute-start(bf16[512,1024]{1,0:T(8,128)(2,1)} %param.25), channel_id=1, source_target_pairs={{0,1},{1,0},{2,3},{3,2},{4,5},{5,4},{6,7},{7,6},{8,9},{9,8},{10,11... | collective-permute-start | bytes 3145736 | tf_op jit(solution)/shard_map/ppermute | solution.py:331
  24.1 46.0 %copy-start.5 = (f32[1024,128]{1,0:T(8,128)}, f32[1024,128]{1,0:T(8,128)S(1)}, u32[]{:S(2)}) copy-start(f32[1024,128]{1,0:T(8,128)S(1)} %get-tuple-element.115.cos_ref) | copy-start | bytes 1572868
  24.1 46.0 %copy-start.7 = (f32[1024,128]{1,0:T(8,128)}, f32[1024,128]{1,0:T(8,128)S(1)}, u32[]{:S(2)}) copy-start(f32[1024,128]{1,0:T(8,128)S(1)} %get-tuple-element.116.sine_ref) | copy-start | bytes 1572868
  70.2 22.4 %copy-start.21 = (s32[1024,8]{0,1:T(8,128)S(1)}, s32[1024,8]{0,1:T(8,128)}, u32[]{:S(2)}) copy-start(s32[1024,8]{0,1:T(8,128)} %param.15) | copy-start | bytes 98308
  70.2 22.6 %copy-start.22 = (f32[1024,8]{0,1:T(8,128)S(1)}, f32[1024,8]{0,1:T(8,128)}, u32[]{:S(2)}) copy-start(f32[1024,8]{0,1:T(8,128)} %param.16) | copy-start | bytes 98308
  91.1 25.4 %collective-permute-start.2 = (bf16[1024,512]{1,0:T(8,128)(2,1)S(1)}, bf16[1024,512]{1,0:T(8,128)(2,1)}, u32[]{:S(2)}, u32[]{:S(2)}) collective-permute-start(bf16[1024,512]{1,0:T(8,128)(2,1)S(1)} %get-tuple-element.27.own_ref), channel_id=1, source_target_pairs={{0,1},{1,0},{2,3},{3,2},{4,5},{5,4},{6,7},{7,6},{8,9},{9,8},{10,11... | collective-permute-start | bytes 3145736 | tf_op jit(solution)/shard_map/ppermute | solution.py:331
  103.8 12.7 %copy-start.3 = (bf16[1024,1024]{1,0:T(8,128)(2,1)S(1)}, bf16[1024,1024]{1,0:T(8,128)(2,1)}, u32[]{:S(2)}) copy-start(bf16[1024,1024]{1,0:T(8,128)(2,1)} %maximum_select_fusion.x_ref) | copy-start | bytes 6291460
  116.6 2.3 copy-start
  340.5 26.2 %collective-permute-start.5 = (bf16[512,1024]{1,0:T(8,128)(2,1)}, bf16[512,1024]{1,0:T(8,128)(2,1)S(1)}, u32[]{:S(2)}, u32[]{:S(2)}) collective-permute-start(bf16[512,1024]{1,0:T(8,128)(2,1)} %dynamic-slice_convert_fusion), channel_id=1, source_target_pairs={{0,1},{1,0},{2,3},{3,2},{4,5},{5,4},{6,7},{7,6},{8,9},{9,8},{10,11... | collective-permute-start | bytes 3145736 | tf_op jit(solution)/shard_map/ppermute | solution.py:331
  344.7 43.8 %collective-permute-start.4 = (bf16[512,1024]{1,0:T(8,128)(2,1)}, bf16[512,1024]{1,0:T(8,128)(2,1)S(1)}, u32[]{:S(2)}, u32[]{:S(2)}) collective-permute-start(bf16[512,1024]{1,0:T(8,128)(2,1)} %dynamic-slice_convert_fusion.1), channel_id=1, source_target_pairs={{0,1},{1,0},{2,3},{3,2},{4,5},{5,4},{6,7},{7,6},{8,9},{9,8},{10,11... | collective-permute-start | bytes 3145736 | tf_op jit(solution)/shard_map/ppermute | solution.py:331
  366.7 21.8 %copy-start.2 = (f32[1024,1024]{1,0:T(8,128)S(1)}, f32[1024,1024]{1,0:T(8,128)}, u32[]{:S(2)}) copy-start(f32[1024,1024]{1,0:T(8,128)} %copy-done.1) | copy-start | bytes 12582916
  395.8 15.5 %copy-start.6 = (f32[1024,128]{1,0:T(8,128)S(1)}, f32[1024,128]{1,0:T(8,128)}, u32[]{:S(2)}) copy-start(f32[1024,128]{1,0:T(8,128)} %copy-done.5) | copy-start | bytes 1572868
  395.8 15.5 %copy-start.8 = (f32[1024,128]{1,0:T(8,128)S(1)}, f32[1024,128]{1,0:T(8,128)}, u32[]{:S(2)}) copy-start(f32[1024,128]{1,0:T(8,128)} %copy-done.7) | copy-start | bytes 1572868
  395.9 15.5 %copy-start.10 = (bf16[1024,512]{1,0:T(8,128)(2,1)S(1)}, bf16[1024,512]{1,0:T(8,128)(2,1)}, u32[]{:S(2)}) copy-start(bf16[1024,512]{1,0:T(8,128)(2,1)} %copy-done.9) | copy-start | bytes 3145732
  395.9 15.4 %copy-start.12 = (bf16[1024,256]{1,0:T(8,128)(2,1)S(1)}, bf16[1024,256]{1,0:T(8,128)(2,1)}, u32[]{:S(2)}) copy-start(bf16[1024,256]{1,0:T(8,128)(2,1)} %copy-done.11) | copy-start | bytes 1572868
  395.9 15.4 %copy-start.14 = (bf16[1024,256]{1,0:T(8,128)(2,1)S(1)}, bf16[1024,256]{1,0:T(8,128)(2,1)}, u32[]{:S(2)}) copy-start(bf16[1024,256]{1,0:T(8,128)(2,1)} %copy-done.13) | copy-start | bytes 1572868
  395.9 14.9 %collective-permute-start.6 = (bf16[512,512]{1,0:T(8,128)(2,1)S(1)}, bf16[512,512]{1,0:T(8,128)(2,1)S(1)}, u32[]{:S(2)}, u32[]{:S(2)}) collective-permute-start(bf16[512,512]{1,0:T(8,128)(2,1)S(1)} %convolution_convert_fusion.1), channel_id=1, source_target_pairs={{0,1},{1,0},{2,3},{3,2},{4,5},{5,4},{6,7},{7,6},{8,9},{9,8},{10,11... | collective-permute-start | bytes 1572872 | tf_op jit(solution)/shard_map/ppermute | solution.py:331
  397.4 48.6 %collective-permute-start.8 = (bf16[512,1024]{1,0:T(8,128)(2,1)S(1)}, bf16[512,1024]{1,0:T(8,128)(2,1)S(1)}, u32[]{:S(2)}, u32[]{:S(2)}) collective-permute-start(bf16[512,1024]{1,0:T(8,128)(2,1)S(1)} %get-tuple-element.98), channel_id=1, source_target_pairs={{0,1},{1,0},{2,3},{3,2},{4,5},{5,4},{6,7},{7,6},{8,9},{9,8},{10,11... | collective-permute-start | bytes 3145736 | tf_op jit(solution)/shard_map/ppermute | solution.py:331
  411.3 30.6 %copy-start.24 = (bf16[1024,1024]{1,0:T(8,128)(2,1)S(1)}, bf16[1024,1024]{1,0:T(8,128)(2,1)}, u32[]{:S(2)}) copy-start(bf16[1024,1024]{1,0:T(8,128)(2,1)} %get-tuple-element.39) | copy-start | bytes 6291460
  440.4 5.6 collective-permute-start.9
  451.5 202.2 %reduce-scatter.8.cloned.1.call-start = ((), (), s32[]{:S(2)}) async-start(), calls=%async_computation.5 | async-start | bytes 13369344 | tf_op jit(solution)/shard_map/reduce_scatter | solution.py:458
  452.1 339.5 %reduce-scatter.6.cloned.1.call-start = ((), (), s32[]{:S(2)}) async-start(), calls=%async_computation.4 | async-start | bytes 13369344 | tf_op jit(solution)/shard_map/reduce_scatter | solution.py:458
  452.7 22.9 %copy-start.20 = (f32[1024]{0:T(1024)S(1)}, f32[1024]{0:T(1024)}, u32[]{:S(2)}) copy-start(f32[1024]{0:T(1024)} %get-tuple-element.96) | copy-start | bytes 12292
  453.8 22.5 %copy-start.17 = (f32[512,1024]{1,0:T(8,128)S(1)}, f32[512,1024]{1,0:T(8,128)}, u32[]{:S(2)}) copy-start(f32[512,1024]{1,0:T(8,128)} %get-tuple-element.99) | copy-start | bytes 6291460
  453.8 21.8 %collective-permute-start.7 = (bf16[512,1024]{1,0:T(8,128)(2,1)S(1)}, bf16[512,1024]{1,0:T(8,128)(2,1)S(1)}, u32[]{:S(2)}, u32[]{:S(2)}) collective-permute-start(bf16[512,1024]{1,0:T(8,128)(2,1)S(1)} %constant_dynamic-slice_fusion), channel_id=1, source_target_pairs={{0,1},{1,0},{2,3},{3,2},{4,5},{5,4},{6,7},{7,6},{8,9},{9,8},{10,11... | collective-permute-start | bytes 3145736 | tf_op jit(solution)/shard_map/ppermute | solution.py:331
  (9 other events, 12.0 us)
Sparse Core Ops, SparseCore 0:
  15.1 52.2 all-gather.5
  70.2 99.3 all-gather.9
  172.3 98.9 all-gather.7
  451.6 64.4 reduce-scatter.9
  520.1 133.6 reduce-scatter.7
  657.7 133.9 reduce-scatter.5

commit v2 on v1

--- a/solution.py
+++ b/solution.py
@@ -15,7 +15,10 @@
 ROPE_BASE = 10000.0
 ROWS = 256
 LANES = 128
-CHUNKS = 2
+GATHERED = (12, 4)
+SPLIT = (4, 4, 4, 4)
+PERMUTED = (True, True, True, True)
+DIRECT_MAX = 16
 MIB = 1 << 20
 BF16 = jnp.bfloat16
 F32 = jnp.float32
@@ -91,15 +94,17 @@
     cos_ref,
     sine_ref,
     opening_ref,
-    a_ref,
+    at_ref,
     q_ref,
     k_ref,
     v_ref,
     o_ref,
     lse_ref,
+    gain_rows_ref,
     lse_cols,
 ):
     rows_all = x_ref.shape[0]
+    gain_rows_ref[...] = gain_ref[...].astype(F32).T[: gain_rows_ref.shape[0], :]
     kv_width = k_ref.shape[1]
     kv_heads = kv_width // HEAD_DIM
     group = q_width // kv_width
@@ -108,8 +113,8 @@
         at = pl.ds(block * ROWS, ROWS)
         x = x_ref[at, :].astype(F32)
         r1 = lax.rsqrt(jnp.mean(x * x, axis=1, keepdims=True) + EPSILON)
-        a = (x * r1 * gain_ref[...]).astype(BF16)
-        a_ref[at, :] = a
+        a = (x * r1 * gain_rows_ref[0:1, :]).astype(BF16)
+        at_ref[:, at] = a.T
         qkv = dot_nn(a, w_ref[...])
         turned = rotate_lanes(
             qkv[:, : q_width + kv_width], cos_ref[at, :], sine_ref[at, :]
@@ -143,10 +148,12 @@
 
 
 def attend_back_kernel(
+    here_ref,
     q_ref,
     k_ref,
     v_ref,
-    go_ref,
+    go_own_ref,
+    go_other_ref,
     lse_ref,
     cos_ref,
     sine_ref,
@@ -154,12 +161,20 @@
     x_ref,
     w_ref,
     d_ref,
-    da_ref,
+    da_own_ref,
+    da_send_ref,
     gain_ref,
     dk_acc,
     dv_acc,
     dq_acc,
+    go_ref,
 ):
+    here = here_ref[0]
+    local_rows = go_own_ref.shape[0]
+    go_ref[pl.ds(pl.multiple_of(here * local_rows, local_rows), local_rows), :] = go_own_ref[...]
+    go_ref[pl.ds(pl.multiple_of((1 - here) * local_rows, local_rows), local_rows), :] = (
+        go_other_ref[...]
+    )
     rows_all, q_width = q_ref.shape
     kv_width = k_ref.shape[1]
     kv_heads = kv_width // HEAD_DIM
@@ -187,7 +202,7 @@
                 q = q_ref[at, mine]
                 go = go_ref[at, mine]
                 s = dot_nt(keys, q) * scale
-                p = jnp.where(keep, jnp.exp(jnp.minimum(s - lse_ref[h : h + 1, at], 1.0)), 0.0)
+                p = jnp.where(keep, jnp.exp(s - lse_ref[h : h + 1, at]), 0.0)
                 dp = dot_nt(vals, go)
                 inner = jnp.sum(p * dp, axis=0, keepdims=True)
                 ds = (p * (dp - inner)).astype(BF16)
@@ -204,47 +219,121 @@
         d = jnp.concatenate([back, dv_acc[at, :]], axis=1).astype(BF16)
         d_ref[at, :] = d
         da = dot_nt(d, w_ref[...])
-        da_ref[at, :] = da.astype(BF16)
+        half, inside = divmod(block * ROWS, local_rows)
+        da_rows = da.astype(BF16)
+
+        @pl.when(here == half)
+        def _():
+            da_own_ref[inside : inside + ROWS, :] = da_rows
+
+        @pl.when(here != half)
+        def _():
+            da_send_ref[inside : inside + ROWS, :] = da_rows
+
         x = x_ref[at, :].astype(F32)
         r1 = lax.rsqrt(jnp.mean(x * x, axis=1, keepdims=True) + EPSILON)
         gain = gain + jnp.sum(da * (x * r1), axis=0, keepdims=True)
     gain_ref[...] = gain
 
 
-def middle_kernel(x_ref, own_ref, other_ref, w_own_ref, w_other_ref, gain_ref, x1_ref, b_ref):
+def attn_grads_kernel(here_ref, at_ref, d_ref, own_ref, other_ref, o_ref, gain_ref, parts_ref):
+    local_rows = own_ref.shape[0]
+    mine = pl.ds(pl.multiple_of(here_ref[0] * local_rows, local_rows), local_rows)
+    others = pl.ds(pl.multiple_of((1 - here_ref[0]) * local_rows, local_rows), local_rows)
+    qkv_width, q_width = d_ref.shape[1], o_ref.shape[1]
+    parts_ref[:, :qkv_width] = dot_nn(at_ref[...], d_ref[...]).astype(BF16)
+    out_grad = dot_tn(own_ref[...], o_ref[mine, :]) + dot_tn(other_ref[...], o_ref[others, :])
+    parts_ref[:, qkv_width : qkv_width + q_width] = out_grad.astype(BF16)
+    parts_ref[:, qkv_width + q_width :] = gain_ref[...].astype(BF16)
+
+
+def middle_back_kernel(
+    here_ref,
+    db_ref,
+    got_ref,
+    x1_ref,
+    dy_ref,
+    gain_ref,
+    w_own_ref,
+    w_other_ref,
+    dx1_ref,
+    attn_ref,
+    send_ref,
+    own_ref,
+    gain_grad_ref,
+):
+    db = db_ref[...] + got_ref[...].astype(F32)
+    x1 = x1_ref[...]
+    r2 = lax.rsqrt(jnp.mean(x1 * x1, axis=1, keepdims=True) + EPSILON)
+    u2 = x1 * r2
+    e2 = db * gain_ref[1:2, :]
+    dx1 = dy_ref[...].astype(F32) + r2 * (e2 - u2 * jnp.mean(e2 * u2, axis=1, keepdims=True))
+    dx1_ref[...] = dx1
+    attn = (BRANCH_SCALE * dx1).astype(BF16)
+    attn_ref[...] = attn
+    send_ref[...] = dot_nn(attn, w_other_ref[...]).astype(BF16)
+    own_ref[...] = dot_nn(attn, w_own_ref[...]).astype(BF16)
+    gain_grad = jnp.sum(db * u2, axis=0, keepdims=True)
+
+    @pl.when(pl.program_id(0) == 0)
+    def _():
+        gain_grad_ref[...] = gain_grad
+
+    @pl.when(pl.program_id(0) > 0)
+    def _():
+        gain_grad_ref[...] += gain_grad
+
+
+def middle_kernel(x_ref, own_ref, other_ref, w_own_ref, w_other_ref, gain_ref, x1_ref, b_ref, bt_ref):
     attn = dot_nt(own_ref[...], w_own_ref[...]) + dot_nt(other_ref[...], w_other_ref[...])
     x1 = x_ref[...].astype(F32) + BRANCH_SCALE * attn
     x1_ref[...] = x1
     r2 = lax.rsqrt(jnp.mean(x1 * x1, axis=1, keepdims=True) + EPSILON)
-    b_ref[...] = (x1 * r2 * gain_ref[...]).astype(BF16)
+    b = (x1 * r2 * gain_ref[1:2, :]).astype(BF16)
+    b_ref[...] = b
+    bt_ref[...] = b.T
+
+
+def piece_of(d):
+    if d == 0:
+        return 0, 0
+    n = (d & -d).bit_length()
+    return n, d >> n
 
 
 def experts_kernel(
-    first, started, b_ref, bt_ref, dy_ref, dyt_ref, gates_ref, w_ref, moe_in, db_in, g_ref, moe_ref, db_ref
+    started,
+    last,
+    stages,
+    place_ref,
+    b_ref,
+    bt_ref,
+    dy_ref,
+    dyt_ref,
+    gates_ref,
+    w_ref,
+    db_in,
+    *refs,
 ):
+    g_refs, refs = refs[: stages + 1], refs[stages + 1 :]
+    h_ref, db_ref, refs = refs[0], refs[1], refs[2:]
+    g_scr = refs[-1]
     step = pl.program_id(0)
     rows_all, width = b_ref.shape
 
     @pl.when(step == 0)
     def _():
-        if started:
-            moe_ref[...] = moe_in[...]
-            db_ref[...] = db_in[...]
-        else:
-            moe_ref[...] = jnp.zeros_like(moe_ref)
-            db_ref[...] = jnp.zeros_like(db_ref)
+        db_ref[...] = db_in[...] if started else jnp.zeros_like(db_ref)
 
     hidden = w_ref.shape[-1]
-    gate_w = w_ref[:, 0, 0].reshape(width, hidden)
-    up_w = w_ref[:, 0, 1].reshape(width, hidden)
-    down_w = w_ref[:, 0, 2].reshape(width, hidden)
+    gate_w, up_w, down_w = [w_ref[:, kind, 0].reshape(width, hidden) for kind in range(3)]
     lane = lax.broadcasted_iota(jnp.int32, (ROWS, gates_ref.shape[1]), 1)
     weighted, gate_grads, up_grads = [], [], []
     for block in range(rows_all // ROWS):
         at = pl.ds(block * ROWS, ROWS)
         b = b_ref[at, :]
         route = jnp.sum(
-            jnp.where(lane == first + step, gates_ref[at, :], 0.0), axis=1, keepdims=True
+            jnp.where(lane == place_ref[1] + step, gates_ref[at, :], 0.0), axis=1, keepdims=True
         )
         gate = dot_nn(b, gate_w)
         up = dot_nn(b, up_w)
@@ -254,51 +343,182 @@
         h = (silu * up * route).astype(BF16)
         dg = (back * up * sig * (1.0 + gate * (1.0 - sig))).astype(BF16)
         du = (back * silu).astype(BF16)
-        moe_ref[at, :] += dot_nt(h, down_w)
+        h_ref[at, :] = h
         db_ref[at, :] += dot_nt(dg, gate_w) + dot_nt(du, up_w)
         weighted.append(h)
         gate_grads.append(dg)
         up_grads.append(du)
-    shards, _, _, per_shard, _ = g_ref.shape
-    shape = (shards, per_shard, hidden)
-    g_ref[:, 0, 0] = dot_nn(bt_ref[...], jnp.concatenate(gate_grads, axis=0)).astype(BF16).reshape(shape)
-    g_ref[:, 0, 1] = dot_nn(bt_ref[...], jnp.concatenate(up_grads, axis=0)).astype(BF16).reshape(shape)
-    down_grad = dot_nn(dyt_ref[...], jnp.concatenate(weighted, axis=0)) * BRANCH_SCALE
-    g_ref[:, 0, 2] = down_grad.astype(BF16).reshape(shape)
+    for kind, left_ref, right, scale in (
+        (0, bt_ref, gate_grads, None),
+        (1, bt_ref, up_grads, None),
+        (2, dyt_ref, weighted, BRANCH_SCALE),
+    ):
+        grad = dot_nn(left_ref[...], jnp.concatenate(right, axis=0))
+        if scale is not None:
+            grad = grad * scale
+        g_scr[kind] = grad.astype(BF16).reshape(g_scr.shape[1:])
+    for d in range(g_scr.shape[1]):
+        n, at = piece_of(d) if stages else (0, d)
+        source = d ^ place_ref[0] if stages else d
+        for kind in range(3):
+            g_refs[n][at, kind, 0] = g_scr[kind, source]
+
+    if last:
+
+        @pl.when(step == pl.num_programs(0) - 1)
+        def _():
+            send_ref = refs[0]
+            rows = send_ref.shape[0]
+            start = pl.multiple_of(place_ref[2], rows)
+            send_ref[...] = db_ref[pl.ds(start, rows), :].astype(BF16)
+
+
+def output_kernel(counts, *refs):
+    chunks = len(counts)
+    h_refs, w_refs, (moe_ref, acc) = refs[:chunks], refs[chunks : 2 * chunks], refs[2 * chunks :]
+    step = pl.program_id(0)
+    width, hidden = acc.shape[1], w_refs[0].shape[-1]
+
+    @pl.when(step == 0)
+    def _():
+        acc[...] = jnp.zeros_like(acc)
+
+    def add(held):
+        acc[...] += sum(
+            dot_nt(h_refs[n][...], w_refs[n][:, 0, 0].reshape(width, hidden)) for n in held
+        )
+
+    limits = sorted(set(counts))
+    for low, high in zip([0] + limits, limits):
+        held = [n for n in range(chunks) if counts[n] >= high]
+        pl.when((step >= low) & (step < high))(functools.partial(add, held))
+
+    @pl.when(step == pl.num_programs(0) - 1)
+    def _():
+        moe_ref[...] = acc[...].astype(BF16)
 
 
 def whole(shape):
     return pl.BlockSpec(shape, lambda *_: (0,) * len(shape), pipeline_mode=pl.Buffered(1))
 
 
-def run_experts(first, b, bt, dy, dyt, gates, weights, carried):
+def run_experts(
+    place, b, bt, dy, dyt, gates, weights, first, count, parts, stages, carried, last
+):
     rows_all, width = b.shape
-    shards, count, kinds, per_shard, hidden = weights.shape
-    block = (shards, 1, kinds, per_shard, hidden)
+    shards, kinds, _, per_shard, hidden = weights.shape
+    out_rows = width // parts
+    sizes = [1] + [1 << (stages - n) for n in range(1, stages + 1)] if stages else [parts]
+    local_rows = rows_all // 2
     started = carried is not None
-    full = jax.ShapeDtypeStruct((rows_all, width), F32)
-    moved = lambda e: (0, e, 0, 0, 0)
     if not started:
-        carried = (jnp.zeros((8, LANES), F32),) * 2
-    flops = 9 * 2 * rows_all * width * hidden * count
-    return pl.pallas_call(
-        functools.partial(experts_kernel, first, started),
-        grid=(count,),
-        in_specs=[whole(t.shape) for t in (b, bt, dy, dyt, gates)]
-        + [pl.BlockSpec(block, moved)]
-        + [whole(t.shape) for t in carried],
-        out_specs=[
-            pl.BlockSpec(block, moved),
-            whole((rows_all, width)),
-            whole((rows_all, width)),
-        ],
-        out_shape=[jax.ShapeDtypeStruct(weights.shape, BF16), full, full],
-        compiler_params=pltpu.CompilerParams(vmem_limit_bytes=56 * MIB),
+        carried = jnp.zeros((8, LANES), F32)
+    results = pl.pallas_call(
+        functools.partial(experts_kernel, started, last, stages),
+        grid_spec=pltpu.PrefetchScalarGridSpec(
+            num_scalar_prefetch=1,
+            grid=(count,),
+            in_specs=[whole(t.shape) for t in (b, bt, dy, dyt, gates)]
+            + [
+                pl.BlockSpec(
+                    (shards, kinds, 1, per_shard, hidden),
+                    lambda e, place: (0, 0, first + e, 0, 0),
+                ),
+                whole(carried.shape),
+            ],
+            out_specs=[
+                pl.BlockSpec(
+                    (size, kinds, 1, out_rows, hidden), lambda e, place: (0, 0, e, 0, 0)
+                )
+                for size in sizes
+            ]
+            + [
+                pl.BlockSpec((rows_all, hidden), lambda e, place: (0, e)),
+                whole((rows_all, width)),
+            ]
+            + [whole((local_rows, width))] * last,
+            scratch_shapes=[pltpu.VMEM((kinds, parts, out_rows, hidden), BF16)],
+        ),
+        out_shape=[
+            jax.ShapeDtypeStruct((size, kinds, count, out_rows, hidden), BF16) for size in sizes
+        ]
+        + [
+            jax.ShapeDtypeStruct((rows_all, count * hidden), BF16),
+            jax.ShapeDtypeStruct((rows_all, width), F32),
+        ]
+        + [jax.ShapeDtypeStruct((local_rows, width), BF16)] * last,
+        compiler_params=pltpu.CompilerParams(vmem_limit_bytes=48 * MIB),
         cost_estimate=pl.CostEstimate(
-            flops=flops, bytes_accessed=4 * weights.size + 24 * MIB, transcendentals=0
+            flops=8 * 2 * rows_all * width * hidden * count,
+            bytes_accessed=4 * kinds * count * width * hidden + 18 * MIB,
+            transcendentals=0,
         ),
         name="experts",
-    )(b, bt, dy, dyt, gates, weights, *carried)
+    )(place, b, bt, dy, dyt, gates, weights, carried)
+    pieces = len(sizes)
+    return results[:pieces], results[pieces], results[pieces + 1], results[pieces + 2 :]
+
+
+def run_output(hidden_parts, weight_parts, firsts, rows_all, width):
+    shards, _, _, per_shard, hidden = weight_parts[0].shape
+    counts = [h.shape[1] // hidden for h in hidden_parts]
+
+    def hidden_spec(count):
+        return pl.BlockSpec((rows_all, hidden), lambda e: (0, jnp.minimum(e, count - 1)))
+
+    def weight_spec(first, count):
+        return pl.BlockSpec(
+            (shards, 1, 1, per_shard, hidden),
+            lambda e: (0, 2, first + jnp.minimum(e, count - 1), 0, 0),
+        )
+
+    return pl.pallas_call(
+        functools.partial(output_kernel, counts),
+        grid=(max(counts),),
+        in_specs=[hidden_spec(count) for count in counts]
+        + [weight_spec(first, count) for first, count in zip(firsts, counts)],
+        out_specs=whole((rows_all, width)),
+        out_shape=jax.ShapeDtypeStruct((rows_all, width), BF16),
+        scratch_shapes=[pltpu.VMEM((rows_all, width), F32)],
+        compiler_params=pltpu.CompilerParams(vmem_limit_bytes=40 * MIB),
+        cost_estimate=pl.CostEstimate(
+            flops=2 * rows_all * width * hidden * sum(counts),
+            bytes_accessed=18 * MIB,
+            transcendentals=0,
+        ),
+        name="expert_output",
+    )(*hidden_parts, *weight_parts)
+
+
+class PieceSum:
+    def __init__(self, pieces, shards):
+        self.shards = shards
+        self.stages = len(pieces) - 1
+        self.own, self.rest = pieces[0], pieces[1:]
+        self.stage = 0
+        self.got = self.swap(self.rest[0])
+
+    def swap(self, values):
+        bit = 1 << self.stage
+        return lax.ppermute(values, "fsdp", [(s, s ^ bit) for s in range(self.shards)])
+
+    def ready(self):
+        if self.stage == self.stages - 1:
+            return [self.own.astype(F32) + self.got[:1].astype(F32)]
+        left = [self.own + self.got[:1]]
+        for n, piece in enumerate(self.rest[self.stage + 1 :]):
+            left.append(piece + self.got[1 << n :: 2 << n])
+        return left
+
+    def send(self, values):
+        if self.stage == self.stages - 1:
+            self.total = values[0][0]
+            self.stage += 1
+            return
+        self.stage += 1
+        self.own = values[0]
+        self.rest = [None] * self.stage + values[1:]
+        self.got = self.swap(self.rest[self.stage])
 
 
 def per_device(
@@ -331,10 +551,8 @@
         return lax.ppermute(values, "tp", [(0, 1), (1, 0)])
 
     def both(own, other):
-        return jnp.where(
-            place == 0,
-            jnp.concatenate([own, other], axis=0),
-            jnp.concatenate([other, own], axis=0),
+        return lax.dynamic_update_slice_in_dim(
+            jnp.concatenate([own, own], axis=0), other, other_at, axis=0
         )
 
     attn_local = jnp.concatenate(
@@ -343,24 +561,32 @@
             key_matrix,
             value_matrix,
             out_weight,
-            swap(out_weight),
             jnp.pad(norm_gains.T, ((0, 0), (0, LANES - 2))),
         ],
         axis=1,
     )
     attn_w = lax.all_gather(attn_local, "fsdp", axis=0, tiled=True)
-    gain_rows = attn_w[:, qkv_width + 2 * q_width :][:, :2].T.astype(F32)
-    expert_local = jnp.stack([gate_weight, up_weight, down_weight], axis=1)
-    per_chunk = EXPERTS // CHUNKS
-    small_shards = per_shard % 16 != 0
-    expert_w = []
-    for chunk in range(CHUNKS):
-        part = lax.all_gather(
-            expert_local[chunk * per_chunk : (chunk + 1) * per_chunk], "fsdp", axis=0, tiled=False
+    hidden_width = gate_weight.shape[-1]
+    expert_w, expert_at = [], []
+    start = 0
+    for count in GATHERED:
+        part = jnp.concatenate(
+            [
+                w[start : start + count].reshape(-1, hidden_width)
+                for w in (gate_weight, up_weight, down_weight)
+            ]
         )
-        if small_shards:
-            part = part.transpose(1, 2, 0, 3, 4).reshape((1,) + part.shape[1:3] + (width, -1))
+        part = lax.all_gather(part, "fsdp", axis=0, tiled=True)
+        part = part.reshape(shards, 3, count, per_shard, hidden_width)
+        if per_shard % 16 != 0:
+            part = part.transpose(1, 2, 0, 3, 4).reshape(1, 3, count, width, hidden_width)
         expert_w.append(part)
+        expert_at += [(len(expert_w) - 1, at) for at in range(count)]
+        start += count
+    stages = shards.bit_length() - 1
+    whole_tiles = per_shard % 16 == 0
+    direct = 2 <= shards <= DIRECT_MAX and 1 << stages == shards and whole_tiles
+    index = lax.axis_index("fsdp") if direct else 0
 
     x_full = both(tokens, swap(tokens))
     dy_full = both(cotangent, swap(cotangent))
@@ -376,34 +602,44 @@
         axis=1,
     )
 
+    out_own, x_full = lax.optimization_barrier(
+        (attn_w[:, qkv_width : qkv_width + q_width], x_full)
+    )
+    out_other = swap(out_own)
     heads = q_width // HEAD_DIM
     rows_of = lambda n, t: jax.ShapeDtypeStruct((rows_all, n), t)
-    normed_one, q_rows, k_rows, v_rows, o_own, lse = pl.pallas_call(
+    normed_one_t, q_rows, k_rows, v_rows, o_own, lse, gain_rows = pl.pallas_call(
         functools.partial(attend_kernel, q_width),
         grid=(1,),
         in_specs=[
             whole((rows_all, width)),
-            whole((1, width)),
+            pl.BlockSpec(
+                (width, LANES),
+                lambda i: (0, (qkv_width + q_width) // LANES),
+                pipeline_mode=pl.Buffered(1),
+            ),
             whole((width, qkv_width)),
             whole((rows_all, LANES)),
             whole((rows_all, LANES)),
             whole((rows_all, 1)),
         ],
         out_specs=[
-            whole((rows_all, width)),
+            whole((width, rows_all)),
             whole((rows_all, q_width)),
             whole((rows_all, kv_width)),
             whole((rows_all, kv_width)),
             whole((rows_all, q_width)),
             whole((heads, rows_all)),
+            whole((8, width)),
         ],
         out_shape=[
-            rows_of(width, BF16),
+            jax.ShapeDtypeStruct((width, rows_all), BF16),
             rows_of(q_width, BF16),
             rows_of(kv_width, BF16),
             rows_of(kv_width, BF16),
             rows_of(q_width, BF16),
             jax.ShapeDtypeStruct((heads, rows_all), F32),
+            jax.ShapeDtypeStruct((8, width), F32),
         ],
         scratch_shapes=[pltpu.VMEM((rows_all, LANES), F32)],
         compiler_params=pltpu.CompilerParams(vmem_limit_bytes=48 * MIB),
@@ -411,13 +647,13 @@
             flops=8 * rows_all * width * qkv_width, bytes_accessed=12 * MIB, transcendentals=0
         ),
         name="attend",
-    )(x_full, gain_rows[:1], attn_w, cos_table, sine_table, opening[:, None])
+    )(x_full, attn_w, attn_w, cos_table, sine_table, opening[:, None])
 
     o_other = swap(o_own)
     steps = rows_all // ROWS
     by_rows = lambda n: pl.BlockSpec((ROWS, n), lambda i: (i, 0))
     first_out = qkv_width // q_width
-    middle, normed_two = pl.pallas_call(
+    middle, normed_two, normed_two_t = pl.pallas_call(
         middle_kernel,
         grid=(steps,),
         in_specs=[
@@ -425,74 +661,134 @@
             by_rows(q_width),
             by_rows(q_width),
             pl.BlockSpec((width, q_width), lambda i: (0, first_out)),
-            pl.BlockSpec((width, q_width), lambda i: (0, first_out + 1)),
-            pl.BlockSpec((1, width), lambda i: (0, 0)),
-        ],
-        out_specs=[by_rows(width), by_rows(width)],
-        out_shape=[rows_of(width, F32), rows_of(width, BF16)],
+            pl.BlockSpec((width, q_width), lambda i: (0, 0)),
+            pl.BlockSpec((8, width), lambda i: (0, 0)),
+        ],
+        out_specs=[
+            by_rows(width),
+            by_rows(width),
+            pl.BlockSpec((width, ROWS), lambda i: (0, i)),
+        ],
+        out_shape=[
+            rows_of(width, F32),
+            rows_of(width, BF16),
+            jax.ShapeDtypeStruct((width, rows_all), BF16),
+        ],
         compiler_params=pltpu.CompilerParams(vmem_limit_bytes=32 * MIB),
         cost_estimate=pl.CostEstimate(
             flops=4 * rows_all * width * q_width, bytes_accessed=14 * MIB, transcendentals=0
         ),
         name="middle",
-    )(x_full, o_own, o_other, attn_w, attn_w, gain_rows[1:])
-
-    normed_two_t = normed_two.T
-    carried = None
-    expert_parts = []
-    for chunk in range(CHUNKS):
-        grads, moe, grad_two = run_experts(
-            chunk * per_chunk,
+    )(x_full, o_own, o_other, attn_w, out_other, gain_rows)
+
+    def advance(anchor, parts):
+        parts = [part for part in parts if isinstance(part, PieceSum)]
+        if not parts:
+            return anchor
+        parts = [part for part in parts if part.stage < part.stages]
+        if not parts:
+            return anchor
+        values = [part.ready() for part in parts]
+        anchor, values = lax.optimization_barrier((anchor, values))
+        for part, value in zip(parts, values):
+            part.send(value)
+        return anchor
+
+    grad_two = None
+    sums, hidden_parts, held_parts, firsts = [], [], [], []
+    start = 0
+    for count in SPLIT:
+        if len(sums) >= 2:
+            grad_two = advance(grad_two, sums[:-1])
+        permuted = direct and PERMUTED[len(sums)]
+        held, first = expert_at[start]
+        where = jnp.stack([index, start, other_at]).astype(jnp.int32)
+        grads, hidden, grad_two, sent = run_experts(
+            where,
             normed_two,
             normed_two_t,
             dy_full,
             dy_t,
             gates,
-            expert_w[chunk],
-            carried,
+            expert_w[held],
+            first,
+            count,
+            shards if whole_tiles else 1,
+            stages if permuted else 0,
+            grad_two,
+            start + count == EXPERTS,
         )
-        carried = (moe, grad_two)
-        if small_shards:
-            grads = grads.reshape(per_chunk, 3, shards, per_shard, -1).transpose(2, 0, 1, 3, 4)
-        expert_parts.append(
-            lax.psum_scatter(grads, "fsdp", scatter_dimension=0, tiled=False)
-        )
-    expert_grads = jnp.concatenate(expert_parts, axis=0).astype(F32)
-
-    def own_rows(values):
-        return lax.dynamic_slice_in_dim(values, mine_at, local_rows, axis=0)
-
-    def other_rows(values):
-        return lax.dynamic_slice_in_dim(values, other_at, local_rows, axis=0)
-
-    grad_two_own = own_rows(grad_two) + swap(other_rows(grad_two).astype(BF16)).astype(F32)
-    middle_own = own_rows(middle)
-    scale_two = lax.rsqrt(jnp.mean(middle_own * middle_own, axis=1, keepdims=True) + EPSILON)
-    unit_two = middle_own * scale_two
-    scaled_two = grad_two_own * gain_rows[1]
-    grad_middle = cotangent.astype(F32) + scale_two * (
-        scaled_two - unit_two * jnp.mean(scaled_two * unit_two, axis=1, keepdims=True)
-    )
-    gain_two = jnp.sum(grad_two_own * unit_two, axis=0, keepdims=True)
-    grad_attn = (BRANCH_SCALE * grad_middle).astype(BF16)
-    out_own = attn_w[:, qkv_width : qkv_width + q_width]
-    out_other = attn_w[:, qkv_width + q_width : qkv_width + 2 * q_width]
-    go_send = jnp.dot(grad_attn, out_other, preferred_element_type=F32).astype(BF16)
+        hidden_parts.append(hidden)
+        held_parts.append(expert_w[held])
+        firsts.append(first)
+        if permuted:
+            sums.append(PieceSum(grads, shards))
+        else:
+            grads = grads[0]
+            if not whole_tiles:
+                grads = grads.reshape(3, count, shards, per_shard, -1).transpose(2, 0, 1, 3, 4)
+            grads = lax.psum_scatter(
+                grads.reshape(-1, hidden_width), "fsdp", scatter_dimension=0, tiled=True
+            )
+            sums.append(grads.reshape(3, count, per_shard, hidden_width))
+        start += count
+
+    grad_two_other = swap(sent[0])
+    grad_two_other = advance(grad_two_other, sums)
+    here = place.astype(jnp.int32)[None]
+    steps = local_rows // ROWS
+    own_block = lambda i, here: (here[0] * steps + i, 0)
+    local_block = lambda i, here: (i, 0)
+    grad_middle, grad_attn, go_send, go_own, gain_two = pl.pallas_call(
+        middle_back_kernel,
+        grid_spec=pltpu.PrefetchScalarGridSpec(
+            num_scalar_prefetch=1,
+            grid=(steps,),
+            in_specs=[
+                pl.BlockSpec((ROWS, width), own_block),
+                pl.BlockSpec((ROWS, width), local_block),
+                pl.BlockSpec((ROWS, width), own_block),
+                pl.BlockSpec((ROWS, width), local_block),
+                whole((8, width)),
+                whole((width, q_width)),
+                whole((width, q_width)),
+            ],
+            out_specs=[
+                pl.BlockSpec((ROWS, width), local_block),
+                pl.BlockSpec((ROWS, width), local_block),
+                pl.BlockSpec((ROWS, q_width), local_block),
+                pl.BlockSpec((ROWS, q_width), local_block),
+                whole((1, width)),
+            ],
+        ),
+        out_shape=[
+            jax.ShapeDtypeStruct((local_rows, width), F32),
+            jax.ShapeDtypeStruct((local_rows, width), BF16),
+            jax.ShapeDtypeStruct((local_rows, q_width), BF16),
+            jax.ShapeDtypeStruct((local_rows, q_width), BF16),
+            jax.ShapeDtypeStruct((1, width), F32),
+        ],
+        compiler_params=pltpu.CompilerParams(vmem_limit_bytes=32 * MIB),
+        cost_estimate=pl.CostEstimate(
+            flops=4 * local_rows * width * q_width, bytes_accessed=12 * MIB, transcendentals=0
+        ),
+        name="middle_back",
+    )(here, grad_two, grad_two_other, middle, cotangent, gain_rows, out_own, out_other)
     go_other = swap(go_send)
-    go_own = jnp.dot(grad_attn, out_own, preferred_element_type=F32).astype(BF16)
-    go_full = both(go_own, go_other)
-    grad_attn_full = both(grad_attn, swap(grad_attn))
-    moe_own = own_rows(moe) + swap(other_rows(moe).astype(BF16)).astype(F32)
-    layer_out = (middle_own + BRANCH_SCALE * moe_own).astype(BF16)
-
-    d_qkv, grad_one, gain_one = pl.pallas_call(
+    go_other, attn_send = lax.optimization_barrier((go_other, grad_attn))
+    grad_attn_other = swap(attn_send)
+    go_other = advance(go_other, sums[:2])
+
+    d_qkv, grad_one, grad_one_send, gain_one = pl.pallas_call(
         attend_back_kernel,
         grid=(1,),
         in_specs=[
+            pl.BlockSpec(memory_space=pltpu.SMEM),
             whole((rows_all, q_width)),
             whole((rows_all, kv_width)),
             whole((rows_all, kv_width)),
-            whole((rows_all, q_width)),
+            whole((local_rows, q_width)),
+            whole((local_rows, q_width)),
             whole((heads, rows_all)),
             whole((rows_all, LANES)),
             whole((rows_all, LANES)),
@@ -500,16 +796,23 @@
             whole((rows_all, width)),
             whole((width, qkv_width)),
         ],
-        out_specs=[whole((rows_all, qkv_width)), whole((rows_all, width)), whole((1, width))],
+        out_specs=[
+            whole((rows_all, qkv_width)),
+            whole((local_rows, width)),
+            whole((local_rows, width)),
+            whole((1, width)),
+        ],
         out_shape=[
             rows_of(qkv_width, BF16),
-            rows_of(width, BF16),
+            jax.ShapeDtypeStruct((local_rows, width), BF16),
+            jax.ShapeDtypeStruct((local_rows, width), BF16),
             jax.ShapeDtypeStruct((1, width), F32),
         ],
         scratch_shapes=[
             pltpu.VMEM((rows_all, kv_width), F32),
             pltpu.VMEM((rows_all, kv_width), F32),
             pltpu.VMEM((rows_all, q_width), F32),
+            pltpu.VMEM((rows_all, q_width), BF16),
         ],
         compiler_params=pltpu.CompilerParams(vmem_limit_bytes=48 * MIB),
         cost_estimate=pl.CostEstimate(
@@ -517,10 +820,12 @@
         ),
         name="attend_back",
     )(
+        here,
         q_rows,
         k_rows,
         v_rows,
-        go_full,
+        go_own,
+        go_other,
         lse,
         cos_table,
         sine_table,
@@ -529,20 +834,57 @@
         attn_w,
     )
 
-    grad_one_own = own_rows(grad_one).astype(F32) + swap(other_rows(grad_one)).astype(F32)
+    grad_one_other = swap(grad_one_send)
+    d_qkv = advance(d_qkv, sums[1:3])
     gain_part = jnp.concatenate([gain_one, gain_two], axis=0)
-    gain_sum = gain_part + swap(gain_part)
-    grad_qkv_w = dot_tn(normed_one, d_qkv)
-    grad_out_w = dot_tn(grad_attn_full, o_own)
-    attn_parts = jnp.concatenate(
-        [grad_qkv_w, grad_out_w, jnp.pad(gain_sum.T, ((0, 0), (0, LANES - 2)))], axis=1
-    ).astype(BF16)
+    gain_cols = jnp.pad(gain_part.T, ((0, 0), (0, LANES - 2)))
+    parts_width = qkv_width + q_width + LANES
+    by_cols = pl.BlockSpec((local_rows, ROWS), lambda i: (0, i))
+    attn_parts = pl.pallas_call(
+        attn_grads_kernel,
+        grid=(width // ROWS,),
+        in_specs=[
+            pl.BlockSpec(memory_space=pltpu.SMEM),
+            pl.BlockSpec((ROWS, rows_all), lambda i: (i, 0)),
+            whole((rows_all, qkv_width)),
+            by_cols,
+            by_cols,
+            whole((rows_all, q_width)),
+            pl.BlockSpec((ROWS, LANES), lambda i: (i, 0)),
+        ],
+        out_specs=pl.BlockSpec((ROWS, parts_width), lambda i: (i, 0)),
+        out_shape=jax.ShapeDtypeStruct((width, parts_width), BF16),
+        compiler_params=pltpu.CompilerParams(vmem_limit_bytes=32 * MIB),
+        cost_estimate=pl.CostEstimate(
+            flops=2 * rows_all * width * parts_width, bytes_accessed=11 * MIB, transcendentals=0
+        ),
+        name="attn_grads",
+    )(here, normed_one_t, d_qkv, grad_attn, grad_attn_other, o_own, gain_cols)
     attn_grads = lax.psum_scatter(attn_parts, "fsdp", scatter_dimension=0, tiled=True).astype(F32)
+
+    gain_grads = attn_grads[:, qkv_width + q_width :][:, :2].T
+    gain_grads = gain_grads + swap(gain_grads)
+    grad_one_other = advance(grad_one_other, sums)
+    hidden_parts[-1], grad_one_other = lax.optimization_barrier((hidden_parts[-1], grad_one_other))
+    moe = run_output(hidden_parts, held_parts, firsts, rows_all, width)
+    totals = []
+    for part in sums:
+        if isinstance(part, PieceSum):
+            while part.stage < stages:
+                part.send(part.ready())
+            part = part.total
+        totals.append(part.astype(F32))
+    expert_grads = jnp.concatenate(totals, axis=1)
+    moe_own = lax.dynamic_slice_in_dim(moe, mine_at, local_rows).astype(F32)
+    moe_other = swap(lax.dynamic_slice_in_dim(moe, other_at, local_rows)).astype(F32)
+    middle_own = lax.dynamic_slice_in_dim(middle, mine_at, local_rows)
+    layer_out = (middle_own + BRANCH_SCALE * (moe_own + moe_other)).astype(BF16)
+    grad_one_own = grad_one.astype(F32) + grad_one_other.astype(F32)
 
     inputs = tokens.astype(F32)
     scale_one = lax.rsqrt(jnp.mean(inputs * inputs, axis=1, keepdims=True) + EPSILON)
     unit_one = inputs * scale_one
-    scaled_one = grad_one_own * gain_rows[0]
+    scaled_one = grad_one_own * gain_rows[0:1]
     grad_tokens = (
         grad_middle
         + scale_one
@@ -555,10 +897,10 @@
         attn_grads[:, q_width : q_width + kv_width],
         attn_grads[:, q_width + kv_width : qkv_width],
         attn_grads[:, qkv_width : qkv_width + q_width],
-        attn_grads[:, qkv_width + q_width :][:, :2].T,
-        expert_grads[:, 0],
-        expert_grads[:, 1],
-        expert_grads[:, 2],
+        gain_grads,
+        expert_grads[0],
+        expert_grads[1],
+        expert_grads[2],
     )
 
 

time: 812 us -> 558 us (0.69)
  waiting for transfers between devices: 503 us -> 191 us
  Pallas kernels: 160 us -> 211 us
  other arithmetic: 36.1 us -> 63.7 us
  local copies, waits for them, and re-layouts: 65.1 us -> 41.4 us
  starting transfers between devices: 13.1 us -> 29.9 us
  matrix products: 9.28 us -> 0 us
    reduce_scatter x2 -> x1, waiting for transfers between devices: 271 us -> 0.01 us  [per_device(): lax.psum_scatter(attn_parts, 'fsdp', scatter_dimension=0, tiled=True)]
    ppermute x0 -> x16, waiting for transfers between devices: none -> 106 us  [swap(): lax.ppermute(values, 'fsdp', [(s, s ^ bit) for s in range(self.shards)])]
    all_gather x2, waiting for transfers between devices: 76.1 us -> 14.4 us  [per_device(): part = lax.all_gather(part, 'fsdp', axis=0, tiled=True)]
    pallas_call x3 -> x8, Pallas kernels: 137 us -> 186 us  [the longest x4 134 us: run_experts(): pl.pallas_call(functools.partial(experts_kernel, started, last, stages),...]
    ppermute x10, waiting for transfers between devices: 98.2 us -> 51.2 us  [swap(): return lax.ppermute(values, 'tp', [(0, 1), (1, 0)])]
    unnamed x7 -> x4, waiting for transfers between devices: 39.9 us -> 0.07 us
    add x0 -> x27, other arithmetic: none -> 37.8 us  [the longest x24 34.6 us: ready(): left.append(piece + self.got[1 << n::2 << n])]
    all_gather x2 -> x0, local copies, waits for them, and re-layouts: 21.8 us -> none  [per_device(): lax.all_gather(expert_local[chunk * per_chunk:(chunk + 1) * per_chunk], '...]
  transfers between devices with their start and end apart: 16 -> 30, of which waited for: 12 -> 12; matrix products, arithmetic and copies ran while one was open for 9% -> 15% of each run, Pallas kernels for 13% -> 38%
where the time goes in v2:
time: 558 us; the launch traced here: 552 us
  Pallas kernels  211 us (38%)
  waiting for transfers between devices  191 us (34%)
  other arithmetic  63.7 us (11%)
  local copies, waits for them, and re-layouts  41.4 us (7%)
  starting transfers between devices  29.9 us (5%)
  between operations  14.7 us (3%)
    pallas_call x4, Pallas kernels, run_experts(): pl.pallas_call(functools.partial(experts_kernel, started, last, stages),...  134 us
    ppermute x16, waiting for transfers between devices, swap(): lax.ppermute(values, 'fsdp', [(s, s ^ bit) for s in range(self.shards)])  106 us
    ppermute x10, waiting for transfers between devices, swap(): return lax.ppermute(values, 'tp', [(0, 1), (1, 0)])  51.2 us
    add x24, other arithmetic, ready(): left.append(piece + self.got[1 << n::2 << n])  34.6 us
    pallas_call x1, Pallas kernels, per_device(): pl.pallas_call(attend_back_kernel, grid=(1,), in_specs=[pl.BlockSpec(memo...  29.3 us
    unnamed x135, local copies, waits for them, and re-layouts  22.3 us
    pallas_call x1, Pallas kernels, per_device(): pl.pallas_call(functools.partial(attend_kernel, q_width), grid=(1,), in_s...  20 us
    all_gather x1, waiting for transfers between devices, per_device(): attn_w = lax.all_gather(attn_local, 'fsdp', axis=0, tiled=True)  19.3 us
  transfers between devices with their start and end apart: 30, of which 12 were waited for; matrix products, arithmetic and copies ran while one was open for 15% of the time, Pallas kernels for 38%

profile of v2, /device:TPU:0, one launch (start us, length us, event | category | flops | bytes accessed | tf_op | source)
XLA Modules:
  0.0 552.2 jit_solution(10220611458952399038)
XLA Ops:
  13.3 3.0 collective-permute-start
  25.2 15.4 %collective-permute-done = bf16[512,1024]{1,0:T(8,128)(2,1)} collective-permute-done((bf16[512,1024]{1,0:T(8,128)(2,1)}, bf16[512,1024]{1,0:T(8,128)(2,1)}, u32[]{:S(2)}, u32[]{:S(2)}) %collective-permute-start) | collective-permute-done | bytes 1048608 | tf_op jit(solution)/shard_map/ppermute | solution.py:551
  42.1 19.3 %all-gather.4.cloned.1.call-done.gain_ref.w_ref.w_own_ref = bf16[1024,1664]{1,0:T(8,128)(2,1)} async-done(((bf16[64,1664]{1,0:T(8,128)(2,1)}), bf16[1024,1664]{1,0:T(8,128)(2,1)}) %all-gather.4.cloned.1.call-update) | async-done | bytes 3407888 | tf_op jit(solution)/shard_map/all_gather | solution.py:568
  61.4 2.3 slice.222.w_own_ref
  63.8 20.0 %attend.1 = (bf16[1024,1024]{1,0:T(8,128)(2,1)}, bf16[1024,512]{1,0:T(8,128)(2,1)S(1)}, bf16[1024,256]{1,0:T(8,128)(2,1)S(1)}, bf16[1024,256]{1,0:T(8,128)(2,1)S...) custom-call(bf16[1024,1024]{1,0:T(8,128)(2,1)} %copy-done.3, ...), custom_call_target="tpu_custom_call" | custom-call | flops 8589934592 | bytes 12582912 | tf_op jit(solution)/shard_map/attend/pallas_call | solution.py:611
  88.9 3.1 pad_maximum_fusion.2
  92.0 5.8 %select_reduce_fusion.gates_ref = f32[1024,128]{1,0:T(8,128)} fusion(f32[1024,8]{1,0:T(8,128)S(1)} %copy.83, s32[1024,8]{1,0:T(8,128)S(1)} %copy.82), kind=kLoop, calls=%fused_computation | loop fusion | flops 3014656 | bytes 589824 | tf_op jit(solution)/shard_map/reduce_sum | solution.py:596
  97.8 2.3 constant_dynamic-update-slice_fusion.4
  100.1 4.1 copy.84.dy_ref
  104.2 8.4 %collective-permute-done.1.other_ref = bf16[1024,512]{1,0:T(8,128)(2,1)} collective-permute-done((bf16[1024,512]{1,0:T(8,128)(2,1)}, bf16[1024,512]{1,0:T(8,128)(2,1)}, u32[]{:S(2)}, u32[]{:S(2)}) %collective-permute-start.1) | collective-permute-done | bytes 1048608 | tf_op jit(solution)/shard_map/ppermute | solution.py:551
  112.6 21.7 %collective-permute-done.2.w_other_ref = bf16[1024,512]{1,0:T(8,128)(2,1)S(1)} collective-permute-done((bf16[1024,512]{1,0:T(8,128)(2,1)}, bf16[1024,512]{1,0:T(8,128)(2,1)S(1)}, u32[]{:S(2)}, u32[]{:S(2)}) %collective-permute-start.2) | collective-permute-done | bytes 1048608 | tf_op jit(solution)/shard_map/ppermute | solution.py:551
  136.5 5.3 middle.1
  146.5 14.4 %all-gather.6.cloned.1.call-done = bf16[36864,256]{1,0:T(8,128)(2,1)} async-done(((bf16[2304,256]{1,0:T(8,128)(2,1)}), bf16[36864,256]{1,0:T(8,128)(2,1)}) %all-gather.6.cloned.1.call-update) | async-done | bytes 18874384 | tf_op jit(solution)/shard_map/all_gather | solution.py:579
  162.0 29.9 %experts.4 = (bf16[1,3,4,64,256]{4,3,2,1,0:T(8,128)(2,1)S(1)}, bf16[8,3,4,64,256]{4,3,2,1,0:T(8,128)(2,1)}, bf16[4,3,4,64,256]{4,3,2,1,0:T(8,128)(2,1)S(1)}, bf1...) custom-call(s32[3]{0:T(128)S(1)} %get-tuple-element.284.place_ref, ...), custom_call_target="tpu_custom_call" | custom-call | flops 17179869184 | bytes 31457280 | tf_op jit(solution)/shard_map/experts/pallas_call | solution.py:416
  192.2 41.0 %experts.5 = (bf16[1,3,4,64,256]{4,3,2,1,0:T(8,128)(2,1)S(1)}, bf16[8,3,4,64,256]{4,3,2,1,0:T(8,128)(2,1)}, bf16[4,3,4,64,256]{4,3,2,1,0:T(8,128)(2,1)S(1)}, bf1...) custom-call(s32[3]{0:T(128)S(1)} %get-tuple-element.285.place_ref, ...), custom_call_target="tpu_custom_call" | custom-call | flops 17179869184 | bytes 31457280 | tf_op jit(solution)/shard_map/experts/pallas_call | solution.py:416
  237.3 2.8 slice_add_fusion.3
  241.8 31.2 %experts.6 = (bf16[1,3,4,64,256]{4,3,2,1,0:T(8,128)(2,1)S(1)}, bf16[8,3,4,64,256]{4,3,2,1,0:T(8,128)(2,1)}, bf16[4,3,4,64,256]{4,3,2,1,0:T(8,128)(2,1)S(1)}, bf1...) custom-call(s32[3]{0:T(128)S(1)} %add_add_fusion.2.place_ref, ...), custom_call_target="tpu_custom_call" | custom-call | flops 17179869184 | bytes 31457280 | tf_op jit(solution)/shard_map/experts/pallas_call | solution.py:416
  283.0 31.6 %experts.7 = (bf16[1,3,4,64,256]{4,3,2,1,0:T(8,128)(2,1)S(1)}, bf16[8,3,4,64,256]{4,3,2,1,0:T(8,128)(2,1)}, bf16[4,3,4,64,256]{4,3,2,1,0:T(8,128)(2,1)S(1)}, bf1...) custom-call(s32[3]{0:T(128)S(1)} %add_add_fusion.3.place_ref, ...), custom_call_target="tpu_custom_call" | custom-call | flops 17179869184 | bytes 31457280 | tf_op jit(solution)/shard_map/experts/pallas_call | solution.py:416
  318.7 16.7 %collective-permute-done.8 = bf16[2,3,4,64,256]{4,3,2,1,0:T(8,128)(2,1)S(1)} collective-permute-done((bf16[2,3,4,64,256]{4,3,2,1,0:T(8,128)(2,1)S(1)}, bf16[2,3,4,64,256]{4,3,2,1,0:T(8,128)(2,1)S(1)}, u32[]{:S(2)}, u32[]{:S(2)}) %collective-permute-start.8) | collective-permute-done | bytes 786464 | tf_op jit(solution)/shard_map/ppermute | solution.py:503
  335.5 16.0 %collective-permute-done.9 = bf16[4,3,4,64,256]{4,3,2,1,0:T(8,128)(2,1)S(1)} collective-permute-done((bf16[4,3,4,64,256]{4,3,2,1,0:T(8,128)(2,1)S(1)}, bf16[4,3,4,64,256]{4,3,2,1,0:T(8,128)(2,1)S(1)}, u32[]{:S(2)}, u32[]{:S(2)}) %collective-permute-start.9) | collective-permute-done | bytes 1572896 | tf_op jit(solution)/shard_map/ppermute | solution.py:503
  354.0 2.8 slice_add_fusion.1
  365.4 4.9 middle_back.1
  374.0 14.2 %collective-permute-done.13 = bf16[1,3,4,64,256]{4,3,2,1,0:T(8,128)(2,1)S(1)} collective-permute-done((bf16[1,3,4,64,256]{4,3,2,1,0:T(8,128)(2,1)S(1)}, bf16[1,3,4,64,256]{4,3,2,1,0:T(8,128)(2,1)S(1)}, u32[]{:S(2)}, u32[]{:S(2)}) %collective-permute-start.13) | collective-permute-done | bytes 393248 | tf_op jit(solution)/shard_map/ppermute | solution.py:503
  391.7 3.4 collective-permute-start.16
  395.1 29.3 %attend_back.1 = (bf16[1024,1024]{1,0:T(8,128)(2,1)}, bf16[512,1024]{1,0:T(8,128)(2,1)S(1)}, bf16[512,1024]{1,0:T(8,128)(2,1)S(1)}, f32[1,1024]{1,0:T(1,128)S(1)}) custom-call(s32[1]{0:T(128)} %bitcast.17.here_ref, bf16[1024,512]{1,0:T(8,128)(2,1)} %copy-done.37, bf16[1024,256]{1,0:T(8,128)(2,1)S(1)} %copy-done.39, bf16[1024,256]{1,0:T(8,128)(2,1)S(1)} %copy-done.41, ...), custom_call_target="tpu_custom_call" | custom-call | flops 17179869184 | bytes 12582912 | tf_op jit(solution)/shard_map/attend_back/pallas_call | solution.py:782
  434.1 5.5 attn_grads.1
  447.3 11.7 %collective-permute-done.18 = bf16[2,3,4,64,256]{4,3,2,1,0:T(8,128)(2,1)} collective-permute-done((bf16[2,3,4,64,256]{4,3,2,1,0:T(8,128)(2,1)}, bf16[2,3,4,64,256]{4,3,2,1,0:T(8,128)(2,1)}, u32[]{:S(2)}, u32[]{:S(2)}) %collective-permute-start.18) | collective-permute-done | bytes 786464 | tf_op jit(solution)/shard_map/ppermute | solution.py:503
  460.5 5.7 %collective-permute-done.15 = bf16[512,1024]{1,0:T(8,128)(2,1)S(1)} collective-permute-done((bf16[512,1024]{1,0:T(8,128)(2,1)}, bf16[512,1024]{1,0:T(8,128)(2,1)S(1)}, u32[]{:S(2)}, u32[]{:S(2)}) %collective-permute-start.15) | collective-permute-done | bytes 1048608 | tf_op jit(solution)/shard_map/ppermute | solution.py:551
  466.2 12.6 %expert_output.1 = bf16[1024,1024]{1,0:T(8,128)(2,1)S(1)} custom-call(bf16[1024,1024]{1,0:T(8,128)(2,1)S(1)} %get-tuple-element.113.refs_0_, bf16[1024,1024]{1,0:T(8,128)(2,1)S(1)} %copy-done.11, bf16[1024,1024]{1,0:T(8,128)(2,1)S(1)} %copy-done.13, bf16[1024,1024]{1,0:T(8,128)(2,1)S(1)} %copy-done.14, bf16[16,3,12,64,256]{4,3,2,1,0:T(8,128)(2,1)} %bitcast.46, ...), custom_call_target="tpu_custom_call" | custom-call | flops 8589934592 | bytes 18874368 | tf_op jit(solution)/shard_map/expert_output/pallas_call | solution.py:475
  484.4 3.1 fusion.6
  487.5 28.7 %collective-permute-done.24 = bf16[2,3,4,64,256]{4,3,2,1,0:T(8,128)(2,1)S(1)} collective-permute-done((bf16[2,3,4,64,256]{4,3,2,1,0:T(8,128)(2,1)S(1)}, bf16[2,3,4,64,256]{4,3,2,1,0:T(8,128)(2,1)S(1)}, u32[]{:S(2)}, u32[]{:S(2)}) %collective-permute-start.24) | collective-permute-done | bytes 786464 | tf_op jit(solution)/shard_map/ppermute | solution.py:503
  518.0 19.0 %collective-permute-done.25 = bf16[1,3,4,64,256]{4,3,2,1,0:T(8,128)(2,1)S(1)} collective-permute-done((bf16[1,3,4,64,256]{4,3,2,1,0:T(8,128)(2,1)S(1)}, bf16[1,3,4,64,256]{4,3,2,1,0:T(8,128)(2,1)S(1)}, u32[]{:S(2)}, u32[]{:S(2)}) %collective-permute-start.25) | collective-permute-done | bytes 393248 | tf_op jit(solution)/shard_map/ppermute | solution.py:503
  (258 shorter events, 102.3 us)
Async XLA Ops:
  7.2 54.2 %all-gather.4.cloned.1.call-start = ((), (), s32[]{:S(2)}) async-start(), calls=%async_computation.1 | async-start | bytes 3620864 | tf_op jit(solution)/shard_map/all_gather | solution.py:568
  12.0 148.9 %all-gather.6.cloned.1.call-start = ((), (), s32[]{:S(2)}) async-start(), calls=%async_computation.2 | async-start | bytes 20054016 | tf_op jit(solution)/shard_map/all_gather | solution.py:579
  13.3 268.7 %all-gather.8.cloned.1.call-start = ((), (), s32[]{:S(2)}) async-start(), calls=%async_computation.3 | async-start | bytes 6684672 | tf_op jit(solution)/shard_map/all_gather | solution.py:579
  13.3 27.3 %collective-permute-start = (bf16[512,1024]{1,0:T(8,128)(2,1)}, bf16[512,1024]{1,0:T(8,128)(2,1)}, u32[]{:S(2)}, u32[]{:S(2)}) collective-permute-start(bf16[512,1024]{1,0:T(8,128)(2,1)} %param.13), channel_id=1, source_target_pairs={{0,1},{1,0},{2,3},{3,2},{4,5},{5,4},{6,7},{7,6},{8,9},{9,8},{10,11... | collective-permute-start | bytes 3145736 | tf_op jit(solution)/shard_map/ppermute | solution.py:551
  17.7 80.1 %collective-permute-start.3 = (bf16[512,1024]{0,1:T(8,128)(2,1)}, bf16[512,1024]{0,1:T(8,128)(2,1)}, u32[]{:S(2)}, u32[]{:S(2)}) collective-permute-start(bf16[512,1024]{0,1:T(8,128)(2,1)} %copy.79), channel_id=1, source_target_pairs={{0,1},{1,0},{2,3},{3,2},{4,5},{5,4},{6,7},{7,6},{8,9},{9,8},{10,11... | collective-permute-start | bytes 3145736 | tf_op jit(solution)/shard_map/ppermute | solution.py:551
  18.8 520.5 %reduce-scatter.2.cloned.1.call-start = ((), (), s32[]{:S(2)}) async-start(), calls=%async_computation.4 | async-start | bytes 3620864 | tf_op jit(solution)/shard_map/reduce_scatter | solution.py:863
  86.3 26.3 %collective-permute-start.1 = (bf16[1024,512]{1,0:T(8,128)(2,1)}, bf16[1024,512]{1,0:T(8,128)(2,1)}, u32[]{:S(2)}, u32[]{:S(2)}) collective-permute-start(bf16[1024,512]{1,0:T(8,128)(2,1)} %get-tuple-element.107.own_ref.o_ref), channel_id=1, source_target_pairs={{0,1},{1,0},{2,3},{3,2},{4,5},{5,4},{6,7},{7,6},{8,9},{9,8},{10,11... | collective-permute-start | bytes 3145736 | tf_op jit(solution)/shard_map/ppermute | solution.py:551
  87.8 46.5 %collective-permute-start.2 = (bf16[1024,512]{1,0:T(8,128)(2,1)}, bf16[1024,512]{1,0:T(8,128)(2,1)S(1)}, u32[]{:S(2)}, u32[]{:S(2)}) collective-permute-start(bf16[1024,512]{1,0:T(8,128)(2,1)} %slice.222.w_own_ref), channel_id=1, source_target_pairs={{0,1},{1,0},{2,3},{3,2},{4,5},{5,4},{6,7},{7,6},{8,9},{9,8},{10,11... | collective-permute-start | bytes 3145736 | tf_op jit(solution)/shard_map/ppermute | solution.py:551
  191.9 41.9 %collective-permute-start.4 = (bf16[8,3,4,64,256]{4,3,2,1,0:T(8,128)(2,1)}, bf16[8,3,4,64,256]{4,3,2,1,0:T(8,128)(2,1)}, u32[]{:S(2)}, u32[]{:S(2)}) collective-permute-start(bf16[8,3,4,64,256]{4,3,2,1,0:T(8,128)(2,1)} %get-tuple-element.118), channel_id=1, source_target_pairs={{0,2},{2,0},{4,6},{6,4},{8,10},{10,8},{12,14},{14,12},{16,18},{18,... | collective-permute-start | bytes 9437192 | tf_op jit(solution)/shard_map/ppermute | solution.py:503
  233.2 40.6 %collective-permute-start.6 = (bf16[8,3,4,64,256]{4,3,2,1,0:T(8,128)(2,1)}, bf16[8,3,4,64,256]{4,3,2,1,0:T(8,128)(2,1)S(1)}, u32[]{:S(2)}, u32[]{:S(2)}) collective-permute-start(bf16[8,3,4,64,256]{4,3,2,1,0:T(8,128)(2,1)} %get-tuple-element.130), channel_id=1, source_target_pairs={{0,2},{2,0},{4,6},{6,4},{8,10},{10,8},{12,14},{14,12},{16,18},{18,... | collective-permute-start | bytes 9437192 | tf_op jit(solution)/shard_map/ppermute | solution.py:503
  240.0 37.7 %collective-permute-start.5 = (bf16[4,3,4,64,256]{4,3,2,1,0:T(8,128)(2,1)}, bf16[4,3,4,64,256]{4,3,2,1,0:T(8,128)(2,1)}, u32[]{:S(2)}, u32[]{:S(2)}) collective-permute-start(bf16[4,3,4,64,256]{4,3,2,1,0:T(8,128)(2,1)} %slice_add_fusion.3), channel_id=1, source_target_pairs={{0,4},{2,6},{4,0},{6,2},{8,12},{10,14},{12,8},{14,10},{16,20},{18,... | collective-permute-start | bytes 4718600 | tf_op jit(solution)/shard_map/ppermute | solution.py:503
  273.8 78.0 %collective-permute-start.10 = (bf16[8,3,4,64,256]{4,3,2,1,0:T(8,128)(2,1)}, bf16[8,3,4,64,256]{4,3,2,1,0:T(8,128)(2,1)}, u32[]{:S(2)}, u32[]{:S(2)}) collective-permute-start(bf16[8,3,4,64,256]{4,3,2,1,0:T(8,128)(2,1)} %get-tuple-element.149), channel_id=1, source_target_pairs={{0,2},{2,0},{4,6},{6,4},{8,10},{10,8},{12,14},{14,12},{16,18},{18,... | collective-permute-start | bytes 9437192 | tf_op jit(solution)/shard_map/ppermute | solution.py:503
  283.0 52.4 %copy-start.53 = (bf16[1,3,4,64,256]{4,3,2,1,0:T(8,128)(2,1)S(1)}, bf16[1,3,4,64,256]{4,3,2,1,0:T(8,128)(2,1)}, u32[]{:S(2)}) copy-start(bf16[1,3,4,64,256]{4,3,2,1,0:T(8,128)(2,1)} %get-tuple-element.143) | copy-start | bytes 1179652
  283.0 52.4 %copy-start.54 = (bf16[1,3,4,64,256]{4,3,2,1,0:T(8,128)(2,1)S(1)}, bf16[1,3,4,64,256]{4,3,2,1,0:T(8,128)(2,1)}, u32[]{:S(2)}) copy-start(bf16[1,3,4,64,256]{4,3,2,1,0:T(8,128)(2,1)} %get-tuple-element.141) | copy-start | bytes 1179652
  314.7 44.3 %collective-permute-start.11 = (bf16[8,3,4,64,256]{4,3,2,1,0:T(8,128)(2,1)}, bf16[8,3,4,64,256]{4,3,2,1,0:T(8,128)(2,1)S(1)}, u32[]{:S(2)}, u32[]{:S(2)}) collective-permute-start(bf16[8,3,4,64,256]{4,3,2,1,0:T(8,128)(2,1)} %get-tuple-element.154), channel_id=1, source_target_pairs={{0,2},{2,0},{4,6},{6,4},{8,10},{10,8},{12,14},{14,12},{16,18},{18,... | collective-permute-start | bytes 9437192 | tf_op jit(solution)/shard_map/ppermute | solution.py:503
  315.1 36.4 %collective-permute-start.9 = (bf16[4,3,4,64,256]{4,3,2,1,0:T(8,128)(2,1)S(1)}, bf16[4,3,4,64,256]{4,3,2,1,0:T(8,128)(2,1)S(1)}, u32[]{:S(2)}, u32[]{:S(2)}) collective-permute-start(bf16[4,3,4,64,256]{4,3,2,1,0:T(8,128)(2,1)S(1)} %copy-done.57), channel_id=1, source_target_pairs={{0,4},{2,6},{4,0},{6,2},{8,12},{10,14},{12,8},{14,10},{16,20},{18,... | collective-permute-start | bytes 4718600 | tf_op jit(solution)/shard_map/ppermute | solution.py:503
  315.8 19.6 %collective-permute-start.8 = (bf16[2,3,4,64,256]{4,3,2,1,0:T(8,128)(2,1)S(1)}, bf16[2,3,4,64,256]{4,3,2,1,0:T(8,128)(2,1)S(1)}, u32[]{:S(2)}, u32[]{:S(2)}) collective-permute-start(bf16[2,3,4,64,256]{4,3,2,1,0:T(8,128)(2,1)S(1)} %copy-done.58), channel_id=1, source_target_pairs={{0,8},{2,10},{4,12},{6,14},{8,0},{10,2},{12,4},{14,6},{16,24},{18,... | collective-permute-start | bytes 2359304 | tf_op jit(solution)/shard_map/ppermute | solution.py:503
  317.3 44.7 %collective-permute-start.7 = (bf16[512,1024]{1,0:T(8,128)(2,1)S(1)}, bf16[512,1024]{1,0:T(8,128)(2,1)S(1)}, u32[]{:S(2)}, u32[]{:S(2)}) collective-permute-start(bf16[512,1024]{1,0:T(8,128)(2,1)S(1)} %get-tuple-element.140), channel_id=1, source_target_pairs={{0,1},{1,0},{2,3},{3,2},{4,5},{5,4},{6,7},{7,6},{8,9},{9,8},{10,11... | collective-permute-start | bytes 3145736 | tf_op jit(solution)/shard_map/ppermute | solution.py:551
  362.0 28.7 %collective-permute-start.14 = (bf16[2,3,4,64,256]{4,3,2,1,0:T(8,128)(2,1)S(1)}, bf16[2,3,4,64,256]{4,3,2,1,0:T(8,128)(2,1)S(1)}, u32[]{:S(2)}, u32[]{:S(2)}) collective-permute-start(bf16[2,3,4,64,256]{4,3,2,1,0:T(8,128)(2,1)S(1)} %slice_add_fusion.8), channel_id=1, source_target_pairs={{0,8},{2,10},{4,12},{6,14},{8,0},{10,2},{12,4},{14,6},{16,24},{18,... | collective-permute-start | bytes 2359304 | tf_op jit(solution)/shard_map/ppermute | solution.py:503
  363.5 24.7 %collective-permute-start.13 = (bf16[1,3,4,64,256]{4,3,2,1,0:T(8,128)(2,1)S(1)}, bf16[1,3,4,64,256]{4,3,2,1,0:T(8,128)(2,1)S(1)}, u32[]{:S(2)}, u32[]{:S(2)}) collective-permute-start(bf16[1,3,4,64,256]{4,3,2,1,0:T(8,128)(2,1)S(1)} %get-tuple-element.164), channel_id=1, source_target_pairs={{0,16},{2,18},{4,20},{6,22},{8,24},{10,26},{12,28},{14,30},{16,0},... | collective-permute-start | bytes 1179656 | tf_op jit(solution)/shard_map/ppermute | solution.py:503
  370.4 18.8 %collective-permute-start.12 = (bf16[512,512]{1,0:T(8,128)(2,1)S(1)}, bf16[512,512]{1,0:T(8,128)(2,1)S(1)}, u32[]{:S(2)}, u32[]{:S(2)}) collective-permute-start(bf16[512,512]{1,0:T(8,128)(2,1)S(1)} %get-tuple-element.160), channel_id=1, source_target_pairs={{0,1},{1,0},{2,3},{3,2},{4,5},{5,4},{6,7},{7,6},{8,9},{9,8},{10,11... | collective-permute-start | bytes 1572872 | tf_op jit(solution)/shard_map/ppermute | solution.py:551
  372.0 57.8 %collective-permute-start.17 = (bf16[4,3,4,64,256]{4,3,2,1,0:T(8,128)(2,1)}, bf16[4,3,4,64,256]{4,3,2,1,0:T(8,128)(2,1)}, u32[]{:S(2)}, u32[]{:S(2)}) collective-permute-start(bf16[4,3,4,64,256]{4,3,2,1,0:T(8,128)(2,1)} %slice_add_fusion.1), channel_id=1, source_target_pairs={{0,4},{2,6},{4,0},{6,2},{8,12},{10,14},{12,8},{14,10},{16,20},{18,... | collective-permute-start | bytes 4718600 | tf_op jit(solution)/shard_map/ppermute | solution.py:503
  373.1 71.4 %collective-permute-start.19 = (bf16[4,3,4,64,256]{4,3,2,1,0:T(8,128)(2,1)}, bf16[4,3,4,64,256]{4,3,2,1,0:T(8,128)(2,1)}, u32[]{:S(2)}, u32[]{:S(2)}) collective-permute-start(bf16[4,3,4,64,256]{4,3,2,1,0:T(8,128)(2,1)} %slice_add_fusion), channel_id=1, source_target_pairs={{0,4},{2,6},{4,0},{6,2},{8,12},{10,14},{12,8},{14,10},{16,20},{18,... | collective-permute-start | bytes 4718600 | tf_op jit(solution)/shard_map/ppermute | solution.py:503
  389.2 44.9 %collective-permute-start.21 = (bf16[512,1024]{1,0:T(8,128)(2,1)}, bf16[512,1024]{1,0:T(8,128)(2,1)}, u32[]{:S(2)}, u32[]{:S(2)}) collective-permute-start(bf16[512,1024]{1,0:T(8,128)(2,1)} %get-tuple-element.192.own_ref), channel_id=1, source_target_pairs={{0,1},{1,0},{2,3},{3,2},{4,5},{5,4},{6,7},{7,6},{8,9},{9,8},{10,11... | collective-permute-start | bytes 3145736 | tf_op jit(solution)/shard_map/ppermute | solution.py:551
  391.7 35.9 %collective-permute-start.16 = (bf16[1,3,4,64,256]{4,3,2,1,0:T(8,128)(2,1)}, bf16[1,3,4,64,256]{4,3,2,1,0:T(8,128)(2,1)}, u32[]{:S(2)}, u32[]{:S(2)}) collective-permute-start(bf16[1,3,4,64,256]{4,3,2,1,0:T(8,128)(2,1)} %get-tuple-element.173), channel_id=1, source_target_pairs={{0,16},{2,18},{4,20},{6,22},{8,24},{10,26},{12,28},{14,30},{16,0},... | collective-permute-start | bytes 1179656 | tf_op jit(solution)/shard_map/ppermute | solution.py:503
  441.4 17.6 %collective-permute-start.18 = (bf16[2,3,4,64,256]{4,3,2,1,0:T(8,128)(2,1)}, bf16[2,3,4,64,256]{4,3,2,1,0:T(8,128)(2,1)}, u32[]{:S(2)}, u32[]{:S(2)}) collective-permute-start(bf16[2,3,4,64,256]{4,3,2,1,0:T(8,128)(2,1)} %slice_add_fusion.5), channel_id=1, source_target_pairs={{0,8},{2,10},{4,12},{6,14},{8,0},{10,2},{12,4},{14,6},{16,24},{18,... | collective-permute-start | bytes 2359304 | tf_op jit(solution)/shard_map/ppermute | solution.py:503
  443.0 23.1 %collective-permute-start.15 = (bf16[512,1024]{1,0:T(8,128)(2,1)}, bf16[512,1024]{1,0:T(8,128)(2,1)S(1)}, u32[]{:S(2)}, u32[]{:S(2)}) collective-permute-start(bf16[512,1024]{1,0:T(8,128)(2,1)} %copy-done.34), channel_id=1, source_target_pairs={{0,1},{1,0},{2,3},{3,2},{4,5},{5,4},{6,7},{7,6},{8,9},{9,8},{10,11... | collective-permute-start | bytes 3145736 | tf_op jit(solution)/shard_map/ppermute | solution.py:551
  478.9 37.5 %collective-permute-start.20 = (bf16[512,1024]{1,0:T(8,128)(2,1)S(1)}, bf16[512,1024]{1,0:T(8,128)(2,1)S(1)}, u32[]{:S(2)}, u32[]{:S(2)}) collective-permute-start(bf16[512,1024]{1,0:T(8,128)(2,1)S(1)} %constant_dynamic-slice_fusion), channel_id=1, source_target_pairs={{0,1},{1,0},{2,3},{3,2},{4,5},{5,4},{6,7},{7,6},{8,9},{9,8},{10,11... | collective-permute-start | bytes 3145736 | tf_op jit(solution)/shard_map/ppermute | solution.py:551
  479.5 36.6 %collective-permute-start.24 = (bf16[2,3,4,64,256]{4,3,2,1,0:T(8,128)(2,1)S(1)}, bf16[2,3,4,64,256]{4,3,2,1,0:T(8,128)(2,1)S(1)}, u32[]{:S(2)}, u32[]{:S(2)}) collective-permute-start(bf16[2,3,4,64,256]{4,3,2,1,0:T(8,128)(2,1)S(1)} %slice_add_fusion.4), channel_id=1, source_target_pairs={{0,8},{2,10},{4,12},{6,14},{8,0},{10,2},{12,4},{14,6},{16,24},{18,... | collective-permute-start | bytes 2359304 | tf_op jit(solution)/shard_map/ppermute | solution.py:503
  481.2 35.1 %collective-permute-start.23 = (bf16[1,3,4,64,256]{4,3,2,1,0:T(8,128)(2,1)S(1)}, bf16[1,3,4,64,256]{4,3,2,1,0:T(8,128)(2,1)S(1)}, u32[]{:S(2)}, u32[]{:S(2)}) collective-permute-start(bf16[1,3,4,64,256]{4,3,2,1,0:T(8,128)(2,1)S(1)} %get-tuple-element.198), channel_id=1, source_target_pairs={{0,16},{2,18},{4,20},{6,22},{8,24},{10,26},{12,28},{14,30},{16,0},... | collective-permute-start | bytes 1179656 | tf_op jit(solution)/shard_map/ppermute | solution.py:503
  516.2 20.8 %collective-permute-start.25 = (bf16[1,3,4,64,256]{4,3,2,1,0:T(8,128)(2,1)S(1)}, bf16[1,3,4,64,256]{4,3,2,1,0:T(8,128)(2,1)S(1)}, u32[]{:S(2)}, u32[]{:S(2)}) collective-permute-start(bf16[1,3,4,64,256]{4,3,2,1,0:T(8,128)(2,1)S(1)} %slice_add_fusion.12), channel_id=1, source_target_pairs={{0,16},{2,18},{4,20},{6,22},{8,24},{10,26},{12,28},{14,30},{16,0},... | collective-permute-start | bytes 1179656 | tf_op jit(solution)/shard_map/ppermute | solution.py:503
  540.2 4.5 collective-permute-start.22
  (67 other events, 838.2 us)
Sparse Core Ops, SparseCore 0:
  12.2 49.1 all-gather.3
  63.0 97.9 all-gather.5
  163.2 61.8 all-gather.7
  441.5 88.9 reduce-scatter.1

commit v3 on v2

--- a/solution.py
+++ b/solution.py
@@ -734,7 +734,7 @@
         start += count
 
     grad_two_other = swap(sent[0])
-    grad_two_other = advance(grad_two_other, sums)
+    grad_two_other = advance(grad_two_other, sums[2:])
     here = place.astype(jnp.int32)[None]
     steps = local_rows // ROWS
     own_block = lambda i, here: (here[0] * steps + i, 0)
@@ -835,7 +835,7 @@
     )
 
     grad_one_other = swap(grad_one_send)
-    d_qkv = advance(d_qkv, sums[1:3])
+    d_qkv = advance(d_qkv, sums[:3])
     gain_part = jnp.concatenate([gain_one, gain_two], axis=0)
     gain_cols = jnp.pad(gain_part.T, ((0, 0), (0, LANES - 2)))
     parts_width = qkv_width + q_width + LANES
@@ -864,9 +864,10 @@
 
     gain_grads = attn_grads[:, qkv_width + q_width :][:, :2].T
     gain_grads = gain_grads + swap(gain_grads)
-    grad_one_other = advance(grad_one_other, sums)
-    hidden_parts[-1], grad_one_other = lax.optimization_barrier((hidden_parts[-1], grad_one_other))
+    hidden_parts[-1], attn_parts = lax.optimization_barrier((hidden_parts[-1], attn_parts))
     moe = run_output(hidden_parts, held_parts, firsts, rows_all, width)
+    grad_one_other, moe = lax.optimization_barrier((grad_one_other, moe))
+    grad_one_other = advance(grad_one_other, sums[1:])
     totals = []
     for part in sums:
         if isinstance(part, PieceSum):

time: 558 us -> 553 us (level)
  waiting for transfers between devices: 191 us -> 174 us
  local copies, waits for them, and re-layouts: 41.4 us -> 48.2 us
    ppermute x16, waiting for transfers between devices: 106 us -> 86.9 us  [swap(): lax.ppermute(values, 'fsdp', [(s, s ^ bit) for s in range(self.shards)])]
    unnamed x135 -> x149, local copies, waits for them, and re-layouts: 22.3 us -> 29.1 us
  transfers between devices with their start and end apart: 30 -> 30, of which waited for: 12 -> 12; matrix products, arithmetic and copies ran while one was open for 15% -> 16% of each run, Pallas kernels for 38% -> 38%
where the time goes in v3:
time: 553 us; the launch traced here: 547 us
  Pallas kernels  211 us (38%)
  waiting for transfers between devices  174 us (31%)
  other arithmetic  65.9 us (12%)
  local copies, waits for them, and re-layouts  48.2 us (9%)
  starting transfers between devices  33.8 us (6%)
  between operations  14.7 us (3%)
    pallas_call x4, Pallas kernels, run_experts(): pl.pallas_call(functools.partial(experts_kernel, started, last, stages),...  134 us
    ppermute x16, waiting for transfers between devices, swap(): lax.ppermute(values, 'fsdp', [(s, s ^ bit) for s in range(self.shards)])  86.9 us
    ppermute x10, waiting for transfers between devices, swap(): return lax.ppermute(values, 'tp', [(0, 1), (1, 0)])  53 us
    add x24, other arithmetic, ready(): left.append(piece + self.got[1 << n::2 << n])  37.1 us
    pallas_call x1, Pallas kernels, per_device(): pl.pallas_call(attend_back_kernel, grid=(1,), in_specs=[pl.BlockSpec(memo...  29.3 us
    unnamed x149, local copies, waits for them, and re-layouts  29.1 us
    pallas_call x1, Pallas kernels, per_device(): pl.pallas_call(functools.partial(attend_kernel, q_width), grid=(1,), in_s...  20 us
    ppermute x16, starting transfers between devices, swap(): lax.ppermute(values, 'fsdp', [(s, s ^ bit) for s in range(self.shards)])  19.8 us
  transfers between devices with their start and end apart: 30, of which 12 were waited for; matrix products, arithmetic and copies ran while one was open for 16% of the time, Pallas kernels for 38%

profile of v3, /device:TPU:0, one launch (start us, length us, event | category | flops | bytes accessed | tf_op | source)
XLA Modules:
  0.0 546.8 jit_solution(13345485535771173010)
XLA Ops:
  13.3 3.0 collective-permute-start
  25.2 15.5 %collective-permute-done = bf16[512,1024]{1,0:T(8,128)(2,1)} collective-permute-done((bf16[512,1024]{1,0:T(8,128)(2,1)}, bf16[512,1024]{1,0:T(8,128)(2,1)}, u32[]{:S(2)}, u32[]{:S(2)}) %collective-permute-start) | collective-permute-done | bytes 1048608 | tf_op jit(solution)/shard_map/ppermute | solution.py:551
  42.1 19.3 %all-gather.4.cloned.1.call-done.gain_ref.w_ref.w_own_ref = bf16[1024,1664]{1,0:T(8,128)(2,1)} async-done(((bf16[64,1664]{1,0:T(8,128)(2,1)}), bf16[1024,1664]{1,0:T(8,128)(2,1)}) %all-gather.4.cloned.1.call-update) | async-done | bytes 3407888 | tf_op jit(solution)/shard_map/all_gather | solution.py:568
  61.4 2.3 slice.222.w_own_ref
  63.8 20.0 %attend.1 = (bf16[1024,1024]{1,0:T(8,128)(2,1)}, bf16[1024,512]{1,0:T(8,128)(2,1)S(1)}, bf16[1024,256]{1,0:T(8,128)(2,1)S(1)}, bf16[1024,256]{1,0:T(8,128)(2,1)S...) custom-call(bf16[1024,1024]{1,0:T(8,128)(2,1)} %copy-done.3, ...), custom_call_target="tpu_custom_call" | custom-call | flops 8589934592 | bytes 12582912 | tf_op jit(solution)/shard_map/attend/pallas_call | solution.py:611
  88.9 3.2 pad_maximum_fusion.2
  92.1 5.8 %select_reduce_fusion.gates_ref = f32[1024,128]{1,0:T(8,128)} fusion(f32[1024,8]{1,0:T(8,128)S(1)} %copy.83, s32[1024,8]{1,0:T(8,128)S(1)} %copy.82), kind=kLoop, calls=%fused_computation | loop fusion | flops 3014656 | bytes 589824 | tf_op jit(solution)/shard_map/reduce_sum | solution.py:596
  97.9 2.3 constant_dynamic-update-slice_fusion.4
  100.2 4.1 copy.87.dy_ref
  104.3 8.3 %collective-permute-done.1.other_ref = bf16[1024,512]{1,0:T(8,128)(2,1)} collective-permute-done((bf16[1024,512]{1,0:T(8,128)(2,1)}, bf16[1024,512]{1,0:T(8,128)(2,1)}, u32[]{:S(2)}, u32[]{:S(2)}) %collective-permute-start.1) | collective-permute-done | bytes 1048608 | tf_op jit(solution)/shard_map/ppermute | solution.py:551
  112.7 21.7 %collective-permute-done.2.w_other_ref = bf16[1024,512]{1,0:T(8,128)(2,1)S(1)} collective-permute-done((bf16[1024,512]{1,0:T(8,128)(2,1)}, bf16[1024,512]{1,0:T(8,128)(2,1)S(1)}, u32[]{:S(2)}, u32[]{:S(2)}) %collective-permute-start.2) | collective-permute-done | bytes 1048608 | tf_op jit(solution)/shard_map/ppermute | solution.py:551
  136.5 5.3 middle.1
  146.5 14.4 %all-gather.8.cloned.1.call-done = bf16[36864,256]{1,0:T(8,128)(2,1)} async-done(((bf16[2304,256]{1,0:T(8,128)(2,1)}), bf16[36864,256]{1,0:T(8,128)(2,1)}) %all-gather.8.cloned.1.call-update) | async-done | bytes 18874384 | tf_op jit(solution)/shard_map/all_gather | solution.py:579
  162.0 30.0 %experts.4 = (bf16[1,3,4,64,256]{4,3,2,1,0:T(8,128)(2,1)S(1)}, bf16[8,3,4,64,256]{4,3,2,1,0:T(8,128)(2,1)}, bf16[4,3,4,64,256]{4,3,2,1,0:T(8,128)(2,1)S(1)}, bf1...) custom-call(s32[3]{0:T(128)S(1)} %add_add_fusion.3.place_ref, ...), custom_call_target="tpu_custom_call" | custom-call | flops 17179869184 | bytes 31457280 | tf_op jit(solution)/shard_map/experts/pallas_call | solution.py:416
  192.3 40.7 %experts.5 = (bf16[1,3,4,64,256]{4,3,2,1,0:T(8,128)(2,1)S(1)}, bf16[8,3,4,64,256]{4,3,2,1,0:T(8,128)(2,1)}, bf16[4,3,4,64,256]{4,3,2,1,0:T(8,128)(2,1)S(1)}, bf1...) custom-call(s32[3]{0:T(128)S(1)} %get-tuple-element.287.place_ref, ...), custom_call_target="tpu_custom_call" | custom-call | flops 17179869184 | bytes 31457280 | tf_op jit(solution)/shard_map/experts/pallas_call | solution.py:416
  233.5 2.4 slice_add_fusion.34
  237.1 2.8 slice_add_fusion.3
  241.6 31.2 %experts.6 = (bf16[1,3,4,64,256]{4,3,2,1,0:T(8,128)(2,1)S(1)}, bf16[8,3,4,64,256]{4,3,2,1,0:T(8,128)(2,1)}, bf16[4,3,4,64,256]{4,3,2,1,0:T(8,128)(2,1)S(1)}, bf1...) custom-call(s32[3]{0:T(128)S(1)} %get-tuple-element.286.place_ref, ...), custom_call_target="tpu_custom_call" | custom-call | flops 17179869184 | bytes 31457280 | tf_op jit(solution)/shard_map/experts/pallas_call | solution.py:416
  282.8 31.7 %experts.7 = (bf16[1,3,4,64,256]{4,3,2,1,0:T(8,128)(2,1)S(1)}, bf16[8,3,4,64,256]{4,3,2,1,0:T(8,128)(2,1)}, bf16[4,3,4,64,256]{4,3,2,1,0:T(8,128)(2,1)S(1)}, bf1...) custom-call(s32[3]{0:T(128)S(1)} %add_add_fusion.place_ref, ...), custom_call_target="tpu_custom_call" | custom-call | flops 17179869184 | bytes 31457280 | tf_op jit(solution)/shard_map/experts/pallas_call | solution.py:416
  318.5 16.0 %collective-permute-done.11 = bf16[2,3,4,64,256]{4,3,2,1,0:T(8,128)(2,1)S(1)} collective-permute-done((bf16[2,3,4,64,256]{4,3,2,1,0:T(8,128)(2,1)S(1)}, bf16[2,3,4,64,256]{4,3,2,1,0:T(8,128)(2,1)S(1)}, u32[]{:S(2)}, u32[]{:S(2)}) %collective-permute-start.11) | collective-permute-done | bytes 786464 | tf_op jit(solution)/shard_map/ppermute | solution.py:503
  335.5 2.9 slice_add_fusion.1
  347.7 4.2 middle_back.1
  357.7 7.5 %collective-permute-done.10.go_other_ref = bf16[512,512]{1,0:T(8,128)(2,1)S(1)} collective-permute-done((bf16[512,512]{1,0:T(8,128)(2,1)S(1)}, bf16[512,512]{1,0:T(8,128)(2,1)S(1)}, u32[]{:S(2)}, u32[]{:S(2)}) %collective-permute-start.10) | collective-permute-done | bytes 524320 | tf_op jit(solution)/shard_map/ppermute | solution.py:551
  368.7 29.3 %attend_back.1 = (bf16[1024,1024]{1,0:T(8,128)(2,1)}, bf16[512,1024]{1,0:T(8,128)(2,1)S(1)}, bf16[512,1024]{1,0:T(8,128)(2,1)S(1)}, f32[1,1024]{1,0:T(1,128)S(1)}) custom-call(s32[1]{0:T(128)} %bitcast.6.here_ref, bf16[1024,512]{1,0:T(8,128)(2,1)} %copy-done.39, bf16[1024,256]{1,0:T(8,128)(2,1)S(1)} %copy-done.41, bf16[1024,256]{1,0:T(8,128)(2,1)S(1)} %copy-done.43, ...), custom_call_target="tpu_custom_call" | custom-call | flops 17179869184 | bytes 12582912 | tf_op jit(solution)/shard_map/attend_back/pallas_call | solution.py:782
  407.2 17.7 %collective-permute-done.16 = bf16[4,3,4,64,256]{4,3,2,1,0:T(8,128)(2,1)} collective-permute-done((bf16[4,3,4,64,256]{4,3,2,1,0:T(8,128)(2,1)}, bf16[4,3,4,64,256]{4,3,2,1,0:T(8,128)(2,1)}, u32[]{:S(2)}, u32[]{:S(2)}) %collective-permute-start.16) | collective-permute-done | bytes 1572896 | tf_op jit(solution)/shard_map/ppermute | solution.py:503
  429.1 5.5 %attn_grads.1 = bf16[1024,1664]{1,0:T(8,128)(2,1)S(1)} custom-call(s32[1]{0:T(128)} %bitcast.6.here_ref, bf16[1024,1024]{1,0:T(8,128)(2,1)S(1)} %copy-done.37, bf16[1024,1024]{1,0:T(8,128)(2,1)S(1)} %copy-done.38, bf16[512,1024]{1,0:T(8,128)(2,1)S(1)} %copy-done.36, bf16[512,1024]{1,0:T(8,128)(2,1)S(1)} %collective-permute-done.17.other_ref, ...), custom_call_target="tpu_custom_call" | custom-call | flops 3489660928 | bytes 11534336 | tf_op jit(solution)/shard_map/attn_grads/pallas_call | solution.py:843
  448.1 12.7 %expert_output.1 = bf16[1024,1024]{1,0:T(8,128)(2,1)S(1)} custom-call(bf16[1024,1024]{1,0:T(8,128)(2,1)S(1)} %get-tuple-element.163.refs_0_, bf16[1024,1024]{1,0:T(8,128)(2,1)S(1)} %copy-done.11, bf16[1024,1024]{1,0:T(8,128)(2,1)S(1)} %copy-done.13, bf16[1024,1024]{1,0:T(8,128)(2,1)S(1)} %copy-done.14, bf16[16,3,12,64,256]{4,3,2,1,0:T(8,128)(2,1)} %bitcast.46, ...), custom_call_target="tpu_custom_call" | custom-call | flops 8589934592 | bytes 18874368 | tf_op jit(solution)/shard_map/expert_output/pallas_call | solution.py:475
  466.1 3.3 collective-permute-start.23
  471.7 3.4 fusion.6
  475.2 30.2 %collective-permute-done.24 = bf16[2,3,4,64,256]{4,3,2,1,0:T(8,128)(2,1)S(1)} collective-permute-done((bf16[2,3,4,64,256]{4,3,2,1,0:T(8,128)(2,1)S(1)}, bf16[2,3,4,64,256]{4,3,2,1,0:T(8,128)(2,1)S(1)}, u32[]{:S(2)}, u32[]{:S(2)}) %collective-permute-start.24) | collective-permute-done | bytes 786464 | tf_op jit(solution)/shard_map/ppermute | solution.py:503
  505.5 2.5 collective-permute-start.25
  509.6 21.7 %collective-permute-done.25 = bf16[1,3,4,64,256]{4,3,2,1,0:T(8,128)(2,1)S(1)} collective-permute-done((bf16[1,3,4,64,256]{4,3,2,1,0:T(8,128)(2,1)S(1)}, bf16[1,3,4,64,256]{4,3,2,1,0:T(8,128)(2,1)S(1)}, u32[]{:S(2)}, u32[]{:S(2)}) %collective-permute-start.25) | collective-permute-done | bytes 393248 | tf_op jit(solution)/shard_map/ppermute | solution.py:503
  (272 shorter events, 111.2 us)
Async XLA Ops:
  7.2 54.2 %all-gather.4.cloned.1.call-start = ((), (), s32[]{:S(2)}) async-start(), calls=%async_computation.1 | async-start | bytes 3620864 | tf_op jit(solution)/shard_map/all_gather | solution.py:568
  12.0 148.9 %all-gather.8.cloned.1.call-start = ((), (), s32[]{:S(2)}) async-start(), calls=%async_computation.3 | async-start | bytes 20054016 | tf_op jit(solution)/shard_map/all_gather | solution.py:579
  13.3 268.4 %all-gather.6.cloned.1.call-start = ((), (), s32[]{:S(2)}) async-start(), calls=%async_computation.2 | async-start | bytes 6684672 | tf_op jit(solution)/shard_map/all_gather | solution.py:579
  13.3 27.3 %collective-permute-start = (bf16[512,1024]{1,0:T(8,128)(2,1)}, bf16[512,1024]{1,0:T(8,128)(2,1)}, u32[]{:S(2)}, u32[]{:S(2)}) collective-permute-start(bf16[512,1024]{1,0:T(8,128)(2,1)} %param.13), channel_id=1, source_target_pairs={{0,1},{1,0},{2,3},{3,2},{4,5},{5,4},{6,7},{7,6},{8,9},{9,8},{10,11... | collective-permute-start | bytes 3145736 | tf_op jit(solution)/shard_map/ppermute | solution.py:551
  17.7 80.2 %collective-permute-start.3 = (bf16[512,1024]{0,1:T(8,128)(2,1)}, bf16[512,1024]{0,1:T(8,128)(2,1)}, u32[]{:S(2)}, u32[]{:S(2)}) collective-permute-start(bf16[512,1024]{0,1:T(8,128)(2,1)} %copy.79), channel_id=1, source_target_pairs={{0,1},{1,0},{2,3},{3,2},{4,5},{5,4},{6,7},{7,6},{8,9},{9,8},{10,11... | collective-permute-start | bytes 3145736 | tf_op jit(solution)/shard_map/ppermute | solution.py:551
  18.8 514.8 %reduce-scatter.2.cloned.1.call-start = ((), (), s32[]{:S(2)}) async-start(), calls=%async_computation.4 | async-start | bytes 3620864 | tf_op jit(solution)/shard_map/reduce_scatter | solution.py:863
  86.3 26.3 %collective-permute-start.1 = (bf16[1024,512]{1,0:T(8,128)(2,1)}, bf16[1024,512]{1,0:T(8,128)(2,1)}, u32[]{:S(2)}, u32[]{:S(2)}) collective-permute-start(bf16[1024,512]{1,0:T(8,128)(2,1)} %get-tuple-element.108.own_ref.o_ref), channel_id=1, source_target_pairs={{0,1},{1,0},{2,3},{3,2},{4,5},{5,4},{6,7},{7,6},{8,9},{9,8},{10,11... | collective-permute-start | bytes 3145736 | tf_op jit(solution)/shard_map/ppermute | solution.py:551
  87.8 46.5 %collective-permute-start.2 = (bf16[1024,512]{1,0:T(8,128)(2,1)}, bf16[1024,512]{1,0:T(8,128)(2,1)S(1)}, u32[]{:S(2)}, u32[]{:S(2)}) collective-permute-start(bf16[1024,512]{1,0:T(8,128)(2,1)} %slice.222.w_own_ref), channel_id=1, source_target_pairs={{0,1},{1,0},{2,3},{3,2},{4,5},{5,4},{6,7},{7,6},{8,9},{9,8},{10,11... | collective-permute-start | bytes 3145736 | tf_op jit(solution)/shard_map/ppermute | solution.py:551
  192.0 41.5 %collective-permute-start.4 = (bf16[8,3,4,64,256]{4,3,2,1,0:T(8,128)(2,1)}, bf16[8,3,4,64,256]{4,3,2,1,0:T(8,128)(2,1)}, u32[]{:S(2)}, u32[]{:S(2)}) collective-permute-start(bf16[8,3,4,64,256]{4,3,2,1,0:T(8,128)(2,1)} %get-tuple-element.120), channel_id=1, source_target_pairs={{0,2},{2,0},{4,6},{6,4},{8,10},{10,8},{12,14},{14,12},{16,18},{18,... | collective-permute-start | bytes 9437192 | tf_op jit(solution)/shard_map/ppermute | solution.py:503
  233.0 40.6 %collective-permute-start.6 = (bf16[8,3,4,64,256]{4,3,2,1,0:T(8,128)(2,1)}, bf16[8,3,4,64,256]{4,3,2,1,0:T(8,128)(2,1)S(1)}, u32[]{:S(2)}, u32[]{:S(2)}) collective-permute-start(bf16[8,3,4,64,256]{4,3,2,1,0:T(8,128)(2,1)} %get-tuple-element.131), channel_id=1, source_target_pairs={{0,2},{2,0},{4,6},{6,4},{8,10},{10,8},{12,14},{14,12},{16,18},{18,... | collective-permute-start | bytes 9437192 | tf_op jit(solution)/shard_map/ppermute | solution.py:503
  239.9 37.6 %collective-permute-start.5 = (bf16[4,3,4,64,256]{4,3,2,1,0:T(8,128)(2,1)}, bf16[4,3,4,64,256]{4,3,2,1,0:T(8,128)(2,1)}, u32[]{:S(2)}, u32[]{:S(2)}) collective-permute-start(bf16[4,3,4,64,256]{4,3,2,1,0:T(8,128)(2,1)} %slice_add_fusion.3), channel_id=1, source_target_pairs={{0,4},{2,6},{4,0},{6,2},{8,12},{10,14},{12,8},{14,10},{16,20},{18,... | collective-permute-start | bytes 4718600 | tf_op jit(solution)/shard_map/ppermute | solution.py:503
  273.6 62.0 %collective-permute-start.8 = (bf16[8,3,4,64,256]{4,3,2,1,0:T(8,128)(2,1)}, bf16[8,3,4,64,256]{4,3,2,1,0:T(8,128)(2,1)}, u32[]{:S(2)}, u32[]{:S(2)}) collective-permute-start(bf16[8,3,4,64,256]{4,3,2,1,0:T(8,128)(2,1)} %get-tuple-element.139), channel_id=1, source_target_pairs={{0,2},{2,0},{4,6},{6,4},{8,10},{10,8},{12,14},{14,12},{16,18},{18,... | collective-permute-start | bytes 9437192 | tf_op jit(solution)/shard_map/ppermute | solution.py:503
  282.8 51.7 %copy-start.59 = (bf16[1,3,4,64,256]{4,3,2,1,0:T(8,128)(2,1)S(1)}, bf16[1,3,4,64,256]{4,3,2,1,0:T(8,128)(2,1)}, u32[]{:S(2)}) copy-start(bf16[1,3,4,64,256]{4,3,2,1,0:T(8,128)(2,1)} %get-tuple-element.155) | copy-start | bytes 1179652
  282.8 51.7 %copy-start.60 = (bf16[1,3,4,64,256]{4,3,2,1,0:T(8,128)(2,1)S(1)}, bf16[1,3,4,64,256]{4,3,2,1,0:T(8,128)(2,1)}, u32[]{:S(2)}) copy-start(bf16[1,3,4,64,256]{4,3,2,1,0:T(8,128)(2,1)} %get-tuple-element.153) | copy-start | bytes 1179652
  314.5 28.2 %collective-permute-start.9 = (bf16[8,3,4,64,256]{4,3,2,1,0:T(8,128)(2,1)}, bf16[8,3,4,64,256]{4,3,2,1,0:T(8,128)(2,1)S(1)}, u32[]{:S(2)}, u32[]{:S(2)}) collective-permute-start(bf16[8,3,4,64,256]{4,3,2,1,0:T(8,128)(2,1)} %get-tuple-element.144), channel_id=1, source_target_pairs={{0,2},{2,0},{4,6},{6,4},{8,10},{10,8},{12,14},{14,12},{16,18},{18,... | collective-permute-start | bytes 9437192 | tf_op jit(solution)/shard_map/ppermute | solution.py:503
  314.9 19.6 %collective-permute-start.11 = (bf16[2,3,4,64,256]{4,3,2,1,0:T(8,128)(2,1)S(1)}, bf16[2,3,4,64,256]{4,3,2,1,0:T(8,128)(2,1)S(1)}, u32[]{:S(2)}, u32[]{:S(2)}) collective-permute-start(bf16[2,3,4,64,256]{4,3,2,1,0:T(8,128)(2,1)S(1)} %copy-done.65), channel_id=1, source_target_pairs={{0,8},{2,10},{4,12},{6,14},{8,0},{10,2},{12,4},{14,6},{16,24},{18,... | collective-permute-start | bytes 2359304 | tf_op jit(solution)/shard_map/ppermute | solution.py:503
  316.4 29.5 %collective-permute-start.7 = (bf16[512,1024]{1,0:T(8,128)(2,1)S(1)}, bf16[512,1024]{1,0:T(8,128)(2,1)S(1)}, u32[]{:S(2)}, u32[]{:S(2)}) collective-permute-start(bf16[512,1024]{1,0:T(8,128)(2,1)S(1)} %get-tuple-element.137), channel_id=1, source_target_pairs={{0,1},{1,0},{2,3},{3,2},{4,5},{5,4},{6,7},{7,6},{8,9},{9,8},{10,11... | collective-permute-start | bytes 3145736 | tf_op jit(solution)/shard_map/ppermute | solution.py:551
  317.8 35.9 %collective-permute-start.12 = (bf16[4,3,4,64,256]{4,3,2,1,0:T(8,128)(2,1)S(1)}, bf16[4,3,4,64,256]{4,3,2,1,0:T(8,128)(2,1)S(1)}, u32[]{:S(2)}, u32[]{:S(2)}) collective-permute-start(bf16[4,3,4,64,256]{4,3,2,1,0:T(8,128)(2,1)S(1)} %copy-done.64), channel_id=1, source_target_pairs={{0,4},{2,6},{4,0},{6,2},{8,12},{10,14},{12,8},{14,10},{16,20},{18,... | collective-permute-start | bytes 4718600 | tf_op jit(solution)/shard_map/ppermute | solution.py:503
  352.0 13.2 %collective-permute-start.10 = (bf16[512,512]{1,0:T(8,128)(2,1)S(1)}, bf16[512,512]{1,0:T(8,128)(2,1)S(1)}, u32[]{:S(2)}, u32[]{:S(2)}) collective-permute-start(bf16[512,512]{1,0:T(8,128)(2,1)S(1)} %get-tuple-element.150), channel_id=1, source_target_pairs={{0,1},{1,0},{2,3},{3,2},{4,5},{5,4},{6,7},{7,6},{8,9},{9,8},{10,11... | collective-permute-start | bytes 1572872 | tf_op jit(solution)/shard_map/ppermute | solution.py:551
  355.7 106.5 %collective-permute-start.21 = (bf16[4,3,4,64,256]{4,3,2,1,0:T(8,128)(2,1)}, bf16[4,3,4,64,256]{4,3,2,1,0:T(8,128)(2,1)}, u32[]{:S(2)}, u32[]{:S(2)}) collective-permute-start(bf16[4,3,4,64,256]{4,3,2,1,0:T(8,128)(2,1)} %slice_add_fusion), channel_id=1, source_target_pairs={{0,4},{2,6},{4,0},{6,2},{8,12},{10,14},{12,8},{14,10},{16,20},{18,... | collective-permute-start | bytes 4718600 | tf_op jit(solution)/shard_map/ppermute | solution.py:503
  356.6 68.2 %collective-permute-start.16 = (bf16[4,3,4,64,256]{4,3,2,1,0:T(8,128)(2,1)}, bf16[4,3,4,64,256]{4,3,2,1,0:T(8,128)(2,1)}, u32[]{:S(2)}, u32[]{:S(2)}) collective-permute-start(bf16[4,3,4,64,256]{4,3,2,1,0:T(8,128)(2,1)} %slice_add_fusion.1), channel_id=1, source_target_pairs={{0,4},{2,6},{4,0},{6,2},{8,12},{10,14},{12,8},{14,10},{16,20},{18,... | collective-permute-start | bytes 4718600 | tf_op jit(solution)/shard_map/ppermute | solution.py:503
  365.2 39.7 %collective-permute-start.15 = (bf16[2,3,4,64,256]{4,3,2,1,0:T(8,128)(2,1)}, bf16[2,3,4,64,256]{4,3,2,1,0:T(8,128)(2,1)}, u32[]{:S(2)}, u32[]{:S(2)}) collective-permute-start(bf16[2,3,4,64,256]{4,3,2,1,0:T(8,128)(2,1)} %slice_add_fusion.6), channel_id=1, source_target_pairs={{0,8},{2,10},{4,12},{6,14},{8,0},{10,2},{12,4},{14,6},{16,24},{18,... | collective-permute-start | bytes 2359304 | tf_op jit(solution)/shard_map/ppermute | solution.py:503
  366.7 36.1 %collective-permute-start.14 = (bf16[1,3,4,64,256]{4,3,2,1,0:T(8,128)(2,1)}, bf16[1,3,4,64,256]{4,3,2,1,0:T(8,128)(2,1)}, u32[]{:S(2)}, u32[]{:S(2)}) collective-permute-start(bf16[1,3,4,64,256]{4,3,2,1,0:T(8,128)(2,1)} %get-tuple-element.170), channel_id=1, source_target_pairs={{0,16},{2,18},{4,20},{6,22},{8,24},{10,26},{12,28},{14,30},{16,0},... | collective-permute-start | bytes 1179656 | tf_op jit(solution)/shard_map/ppermute | solution.py:503
  401.2 27.8 %collective-permute-start.17 = (bf16[512,1024]{1,0:T(8,128)(2,1)}, bf16[512,1024]{1,0:T(8,128)(2,1)S(1)}, u32[]{:S(2)}, u32[]{:S(2)}) collective-permute-start(bf16[512,1024]{1,0:T(8,128)(2,1)} %copy-done.35), channel_id=1, source_target_pairs={{0,1},{1,0},{2,3},{3,2},{4,5},{5,4},{6,7},{7,6},{8,9},{9,8},{10,11... | collective-permute-start | bytes 3145736 | tf_op jit(solution)/shard_map/ppermute | solution.py:551
  436.4 24.5 %collective-permute-start.13 = (bf16[512,1024]{1,0:T(8,128)(2,1)}, bf16[512,1024]{1,0:T(8,128)(2,1)}, u32[]{:S(2)}, u32[]{:S(2)}) collective-permute-start(bf16[512,1024]{1,0:T(8,128)(2,1)} %copy-done.34), channel_id=1, source_target_pairs={{0,1},{1,0},{2,3},{3,2},{4,5},{5,4},{6,7},{7,6},{8,9},{9,8},{10,11... | collective-permute-start | bytes 3145736 | tf_op jit(solution)/shard_map/ppermute | solution.py:551
  439.6 26.4 %collective-permute-start.20 = (bf16[2,3,4,64,256]{4,3,2,1,0:T(8,128)(2,1)}, bf16[2,3,4,64,256]{4,3,2,1,0:T(8,128)(2,1)S(1)}, u32[]{:S(2)}, u32[]{:S(2)}) collective-permute-start(bf16[2,3,4,64,256]{4,3,2,1,0:T(8,128)(2,1)} %slice_add_fusion.5), channel_id=1, source_target_pairs={{0,8},{2,10},{4,12},{6,14},{8,0},{10,2},{12,4},{14,6},{16,24},{18,... | collective-permute-start | bytes 2359304 | tf_op jit(solution)/shard_map/ppermute | solution.py:503
  441.1 24.8 %collective-permute-start.19 = (bf16[1,3,4,64,256]{4,3,2,1,0:T(8,128)(2,1)}, bf16[1,3,4,64,256]{4,3,2,1,0:T(8,128)(2,1)S(1)}, u32[]{:S(2)}, u32[]{:S(2)}) collective-permute-start(bf16[1,3,4,64,256]{4,3,2,1,0:T(8,128)(2,1)} %get-tuple-element.188), channel_id=1, source_target_pairs={{0,16},{2,18},{4,20},{6,22},{8,24},{10,26},{12,28},{14,30},{16,0},... | collective-permute-start | bytes 1179656 | tf_op jit(solution)/shard_map/ppermute | solution.py:503
  461.0 47.0 %collective-permute-start.18 = (bf16[512,1024]{1,0:T(8,128)(2,1)S(1)}, bf16[512,1024]{1,0:T(8,128)(2,1)S(1)}, u32[]{:S(2)}, u32[]{:S(2)}) collective-permute-start(bf16[512,1024]{1,0:T(8,128)(2,1)S(1)} %constant_dynamic-slice_fusion), channel_id=1, source_target_pairs={{0,1},{1,0},{2,3},{3,2},{4,5},{5,4},{6,7},{7,6},{8,9},{9,8},{10,11... | collective-permute-start | bytes 3145736 | tf_op jit(solution)/shard_map/ppermute | solution.py:551
  466.1 43.3 %collective-permute-start.23 = (bf16[1,3,4,64,256]{4,3,2,1,0:T(8,128)(2,1)S(1)}, bf16[1,3,4,64,256]{4,3,2,1,0:T(8,128)(2,1)S(1)}, u32[]{:S(2)}, u32[]{:S(2)}) collective-permute-start(bf16[1,3,4,64,256]{4,3,2,1,0:T(8,128)(2,1)S(1)} %get-tuple-element.200), channel_id=1, source_target_pairs={{0,16},{2,18},{4,20},{6,22},{8,24},{10,26},{12,28},{14,30},{16,0},... | collective-permute-start | bytes 1179656 | tf_op jit(solution)/shard_map/ppermute | solution.py:503
  469.5 35.9 %collective-permute-start.24 = (bf16[2,3,4,64,256]{4,3,2,1,0:T(8,128)(2,1)S(1)}, bf16[2,3,4,64,256]{4,3,2,1,0:T(8,128)(2,1)S(1)}, u32[]{:S(2)}, u32[]{:S(2)}) collective-permute-start(bf16[2,3,4,64,256]{4,3,2,1,0:T(8,128)(2,1)S(1)} %slice_add_fusion.4), channel_id=1, source_target_pairs={{0,8},{2,10},{4,12},{6,14},{8,0},{10,2},{12,4},{14,6},{16,24},{18,... | collective-permute-start | bytes 2359304 | tf_op jit(solution)/shard_map/ppermute | solution.py:503
  505.5 25.9 %collective-permute-start.25 = (bf16[1,3,4,64,256]{4,3,2,1,0:T(8,128)(2,1)S(1)}, bf16[1,3,4,64,256]{4,3,2,1,0:T(8,128)(2,1)S(1)}, u32[]{:S(2)}, u32[]{:S(2)}) collective-permute-start(bf16[1,3,4,64,256]{4,3,2,1,0:T(8,128)(2,1)S(1)} %slice_add_fusion.12), channel_id=1, source_target_pairs={{0,16},{2,18},{4,20},{6,22},{8,24},{10,26},{12,28},{14,30},{16,0},... | collective-permute-start | bytes 1179656 | tf_op jit(solution)/shard_map/ppermute | solution.py:503
  534.6 4.8 collective-permute-start.22
  (74 other events, 765.6 us)
Sparse Core Ops, SparseCore 0:
  12.2 49.1 all-gather.3
  63.0 97.8 all-gather.7
  163.2 61.7 all-gather.5
  436.5 95.7 reduce-scatter.1
